TPU v7x, 512 devices: a whole 4x8x8 slice. The times are simulated.
512 devices in a mesh: tm: 256 (over z, y, x), mp: 2 (over core).
Axes of the slice: x: 4, y: 8, z: 8, core: 2. Of those that a mesh axis runs over, the one named last changes fastest.
Arguments:
- frames: bfloat16 [131072, 1024], P('tm'), may hold values from -6 to 6
- gain_attn: float32 [1024], replicated, may hold values from 0.5 to 1.5
- w_qkv: bfloat16 [1024, 3, 1024], P(None, None, 'mp'), may hold values from -1 to 1
- w_out: bfloat16 [1024, 1024], P('mp'), may hold values from -0.1875 to 0.1875
- gain_conv: float32 [1024], replicated, may hold values from 0.5 to 1.5
- w_point_in: bfloat16 [1024, 2048], replicated, may hold values from -0.1875 to 0.1875
- w_depth: bfloat16 [31, 1024], replicated, may hold values from -1 to 1
- gain_depth: float32 [1024], replicated, may hold values from 0.5 to 1.5
- w_point_out: bfloat16 [1024, 1024], replicated, may hold values from -0.1875 to 0.1875
- gain_ffn: float32 [1024], replicated, may hold values from 0.5 to 1.5
- w_up: bfloat16 [1024, 4096], P(None, 'mp'), may hold values from -0.1875 to 0.1875
- w_down: bfloat16 [4096, 1024], P('mp'), may hold values from -0.09375 to 0.09375
- gain_final: float32 [1024], replicated, may hold values from 0.5 to 1.5
- lengths: int32 [128], replicated, may hold values from 1 to 16, 1024 in all
- context: int32 [128], replicated, may hold values from 0 to 8, as said below
Outputs:
- encoded: bfloat16 [131072, 1024], P(('tm', 'mp'))
Inputs may be any that keep to these rules, and one draw needn't show every extreme that they name: Recording lengths in stretches of 128 frames; the recordings fill all 131072 frames in order, and the longest has exactly 16 stretches. `context`: some recording allows exactly 8 stretches.
All inputs are finite; a program needn't handle non-finite values.
Results may differ from a plain program's by a relative error of at most 0.014.
The roundings to bfloat16 on the way count: a program that leaves them out, or rounds other values in their place, can miss the bound.
Values may be sent and summed in bfloat16 or wider, within the bound.
No kernel may reach another device: no remote copies, remote signals or barrier semaphores. Data moves between devices by JAX's collectives and lax.ppermute only.
A program may use at most 192 MiB of HBM per device.

v0:
```python
import jax
import jax.numpy as jnp
from jax import lax
from jax.sharding import PartitionSpec as P

HD = 64
C = 128


EPSILON = 1e-05
NEGATIVE = -1e30


def shifted(value, axis, steps):
    count = lax.axis_size(axis)
    first, last = (max(0, -steps), min(count, count - steps))
    return lax.ppermute(value, axis, [(source, source + steps) for source in range(first, last)])


def with_halo(block, sides, width):
    for axis, dim in sides:
        count = lax.axis_size(axis)
        forward = [(i, i + 1) for i in range(count - 1)]
        backward = [(target, source) for source, target in forward]
        low = lax.ppermute(
            lax.slice_in_dim(block, block.shape[dim] - width, None, axis=dim), axis, forward
        )
        high = lax.ppermute(lax.slice_in_dim(block, 0, width, axis=dim), axis, backward)
        block = jnp.concatenate([low, block, high], axis=dim)
    return block


def layer_norm(values, gain_vec):
    values = values.astype(jnp.float32)
    centred = values - jnp.mean(values, axis=-1, keepdims=True)
    variance = jnp.mean(centred * centred, axis=-1, keepdims=True)
    return centred * lax.rsqrt(variance + EPSILON) * gain_vec


def lowest_stretches(stretch_start, stretch_end, context, stretch_count):
    stretch_ids = jnp.arange(stretch_count, dtype=jnp.int32)
    member = (
        (stretch_start[None, :] <= stretch_ids[:, None])
        & (stretch_ids[:, None] < stretch_end[None, :])
    ).astype(jnp.int32)
    opening = jnp.sum(member * stretch_start[None, :], axis=1)
    reached = jnp.sum(member * context[None, :], axis=1)
    return jnp.maximum(stretch_ids - reached, opening)


def record_labels(frame_ids, stretch_start, stretch_end):
    stretch_ids = jnp.floor_divide(frame_ids, C)
    member = (
        (stretch_start[None, :] <= stretch_ids[:, None])
        & (stretch_ids[:, None] < stretch_end[None, :])
    ).astype(jnp.int32)
    numbers = jnp.arange(1, stretch_start.shape[0] + 1, dtype=jnp.int32)
    return jnp.sum(member * numbers[None, :], axis=1)


def softmax_weights(scores):
    highest = jnp.max(scores, axis=-1, keepdims=True)
    raised = jnp.exp(scores - highest)
    return (raised / jnp.sum(raised, axis=-1, keepdims=True)).astype(jnp.bfloat16)


def on_device(
    frames,
    gain_attn,
    w_qkv,
    w_out,
    gain_conv,
    w_point_in,
    w_depth,
    gain_depth,
    w_point_out,
    gain_ffn,
    w_up,
    w_down,
    gain_final,
    lengths,
    context,
):
    slab_len, model_width = frames.shape
    row_count = slab_len // lax.axis_size("mp")
    local_width = w_qkv.shape[2]
    head_count = local_width // HD
    q_block = min(slab_len, 512)
    key_window = 2 * slab_len + q_block
    slab_first = lax.axis_index("tm") * slab_len
    stretch_start = jnp.cumsum(lengths) - lengths
    stretch_end = stretch_start + lengths
    lowest = lowest_stretches(
        stretch_start, stretch_end, context, lax.axis_size("tm") * slab_len // C
    )
    normed = layer_norm(frames, gain_attn).astype(jnp.bfloat16)
    projected = jnp.dot(
        normed, w_qkv.reshape(model_width, 3 * local_width), preferred_element_type=jnp.float32
    ).astype(jnp.bfloat16)
    queries = projected[:, :local_width]
    key_value = projected[:, local_width:]
    arrived = []
    moving = key_value
    for hop_number in range(2):
        moving = shifted(moving, "tm", 1)
        arrived.append(moving)
    nearer = arrived[0]
    farther = arrived[1]
    key_rows = jnp.concatenate([farther, nearer, key_value], axis=0)
    offset = 0
    q_rows = queries.reshape(q_block, head_count, HD)
    k_rows = key_rows[:, :local_width].reshape(key_window, head_count, HD)
    v_rows = key_rows[:, local_width:].reshape(key_window, head_count, HD)
    q_stretches = (slab_first + offset + jnp.arange(q_block, dtype=jnp.int32)) // C
    low_rows = jnp.repeat(
        lax.dynamic_slice_in_dim(lowest, (slab_first + offset) // C, q_block // C), C
    )
    k_stretches = jnp.floor_divide(
        slab_first - 2 * slab_len + offset + jnp.arange(key_window, dtype=jnp.int32), C
    )
    visible = (k_stretches[None, :] >= low_rows[:, None]) & (
        k_stretches[None, :] <= q_stretches[:, None]
    )
    scores = jnp.einsum(
        "qhd,khd->hqk", q_rows, k_rows, preferred_element_type=jnp.float32
    ) * HD ** (-0.5)
    weights = softmax_weights(jnp.where(visible[None], scores, NEGATIVE))
    mixed_out = jnp.einsum("hqk,khd->qhd", weights, v_rows, preferred_element_type=jnp.float32)
    outputs = mixed_out.astype(jnp.bfloat16).reshape(q_block, local_width)
    picked = outputs
    attention = lax.psum_scatter(
        jnp.dot(picked, w_out, preferred_element_type=jnp.float32).astype(jnp.bfloat16),
        "mp",
        scatter_dimension=0,
        tiled=True,
    ).astype(jnp.float32)
    own_rows = lax.dynamic_slice_in_dim(
        frames, lax.axis_index("mp") * row_count, row_count, 0
    ).astype(jnp.float32)
    first_res = own_rows + attention
    conv_in = layer_norm(first_res, gain_conv).astype(jnp.bfloat16)
    lifted = jnp.dot(conv_in, w_point_in, preferred_element_type=jnp.float32)
    gated_units = (lifted[:, :model_width] * jax.nn.sigmoid(lifted[:, model_width:])).astype(
        jnp.bfloat16
    )
    half_width = (w_depth.shape[0] - 1) // 2
    padded = with_halo(gated_units, ((("tm", "mp"), 0),), half_width)
    frame_ids = (
        lax.axis_index(("tm", "mp")) * row_count
        - half_width
        + jnp.arange(row_count + 2 * half_width, dtype=jnp.int32)
    )
    labels = record_labels(frame_ids, stretch_start, stretch_end)
    centre = labels[half_width : half_width + row_count]
    tap_weights = w_depth.astype(jnp.float32)
    depth_sum = jnp.zeros((row_count, model_width), jnp.float32)
    for offset in range(w_depth.shape[0]):
        same_record = (labels[offset : offset + row_count] == centre)[:, None]
        depth_sum = depth_sum + jnp.where(
            same_record,
            padded[offset : offset + row_count].astype(jnp.float32) * tap_weights[offset],
            0.0,
        )
    squashed = jax.nn.silu(layer_norm(depth_sum, gain_depth)).astype(jnp.bfloat16)
    second_res = first_res + jnp.dot(squashed, w_point_out, preferred_element_type=jnp.float32)
    ffn_in = layer_norm(second_res, gain_ffn).astype(jnp.bfloat16)
    hidden = jax.nn.silu(
        jnp.dot(
            lax.all_gather(ffn_in, "mp", axis=0, tiled=True),
            w_up,
            preferred_element_type=jnp.float32,
        )
    ).astype(jnp.bfloat16)
    picked = hidden
    feed_sum = lax.psum_scatter(
        jnp.dot(picked, w_down, preferred_element_type=jnp.float32).astype(jnp.bfloat16),
        "mp",
        scatter_dimension=0,
        tiled=True,
    ).astype(jnp.float32)
    return layer_norm(second_res + 0.5 * feed_sum, gain_final).astype(jnp.bfloat16)


def solution(mesh):
    in_specs = (
        P("tm", None),
        P(),
        P(None, None, "mp"),
        P("mp", None),
        P(),
        P(),
        P(),
        P(),
        P(),
        P(),
        P(None, "mp"),
        P("mp", None),
        P(),
        P(),
        P(),
    )
    out_specs = P(("tm", "mp"), None)
    return jax.shard_map(
        on_device, mesh=mesh, in_specs=in_specs, out_specs=out_specs, check_vma=False
    )
```

profile of v0, /device:TPU:1, one launch (start us, length us, event | category | flops | bytes accessed | tf_op | source)
XLA Modules:
  0.0 222.9 jit_solution(13141482270441934791)
XLA Ops:
  9.8 4.8 %copy.25 = bf16[1024,3,512]{0,2,1:T(8,128)(2,1)} copy(bf16[1024,3,512]{2,0,1:T(8,128)(2,1)} %param.17) | data formatting | bytes 6291456 | tf_op args[2]
  14.6 3.8 %convolution_convert_fusion = bf16[512,1536]{1,0:T(8,128)(2,1)S(1)} fusion(bf16[1024,1536]{0,1:T(8,128)(2,1)} %bitcast.54, bf16[512,1024]{1,0:T(8,128)(2,1)S(1)} %copy-done.1, f32[1024]{0:T(1024)S(1)} %copy-done.11, f32[512]{0:T(512)S(1)} %add_rsqrt_fusion, f32[512]{0:T(512)S(1)} %broadcast_multiply_fusion), kind=kOutput, calls=%fused_computation.40 | convolution fusion | flops 1614020608 | bytes 5775360 | tf_op jit(solution)/shard_map/dot_general | solution.py:97
  20.7 4.9 %collective-permute-start = (bf16[512,1024]{1,0:T(8,128)(2,1)}, bf16[512,1024]{1,0:T(8,128)(2,1)}, u32[]{:S(2)}, u32[]{:S(2)}) collective-permute-start(bf16[512,1024]{1,0:T(8,128)(2,1)} %slice.431), channel_id=1, source_target_pairs={{0,2},{2,4},{4,6},{6,8},{8,10},{10,12},{12,14},{14,16},{16,18},{18... | collective-permute-start | bytes 3145736 | tf_op jit(solution)/shard_map/ppermute | solution.py:17
  25.6 1.9 slice.433
  27.9 2.1 copy.28
  30.3 13.1 %collective-permute-done = bf16[512,1024]{1,0:T(8,128)(2,1)} collective-permute-done((bf16[512,1024]{1,0:T(8,128)(2,1)}, bf16[512,1024]{1,0:T(8,128)(2,1)}, u32[]{:S(2)}, u32[]{:S(2)}) %collective-permute-start) | collective-permute-done | bytes 1048608 | tf_op jit(solution)/shard_map/ppermute | solution.py:17
  43.4 6.5 %collective-permute-start.1 = (bf16[512,1024]{1,0:T(8,128)(2,1)}, bf16[512,1024]{1,0:T(8,128)(2,1)S(1)}, u32[]{:S(2)}, u32[]{:S(2)}) collective-permute-start(bf16[512,1024]{1,0:T(8,128)(2,1)} %collective-permute-done), channel_id=1, source_target_pairs={{0,2},{2,4},{4,6},{6,8},{8,10},{10,12},{12,14},{14,16},{16,18},{18... | collective-permute-start | bytes 3145736 | tf_op jit(solution)/shard_map/ppermute | solution.py:17
  51.7 18.3 %collective-permute-done.1 = bf16[512,1024]{1,0:T(8,128)(2,1)S(1)} collective-permute-done((bf16[512,1024]{1,0:T(8,128)(2,1)}, bf16[512,1024]{1,0:T(8,128)(2,1)S(1)}, u32[]{:S(2)}, u32[]{:S(2)}) %collective-permute-start.1) | collective-permute-done | bytes 1048608 | tf_op jit(solution)/shard_map/ppermute | solution.py:17
  70.1 1.7 pad_maximum_fusion
  71.8 1.8 fusion.85
  73.6 2.6 %copy.29 = bf16[1536,512]{0,1:T(8,128)(2,1)} copy(bf16[1536,512]{1,0:T(8,128)(2,1)} %get-tuple-element.9) | data formatting | bytes 3145728 | tf_op jit(solution)/shard_map/slice | solution.py:112
  76.2 2.6 %copy.26 = bf16[1536,512]{0,1:T(8,128)(2,1)} copy(bf16[1536,512]{1,0:T(8,128)(2,1)} %get-tuple-element.10) | data formatting | bytes 3145728 | tf_op jit(solution)/shard_map/slice | solution.py:113
  78.8 10.1 %fusion.89 = f32[8,512]{1,0:T(8,128)S(1)} fusion(pred[512,1536]{1,0:T(8,128)(4,1)} %compare_and_fusion, bf16[512,8,64]{0,2,1:T(8,128)(2,1)} %bitcast.58, bf16[1536,8,64]{0,2,1:T(8,128)(2,1)} %bitcast.55), kind=kOutput, calls=%fused_computation.221 | convolution fusion | flops 830473728 | bytes 2899968 | tf_op jit(solution)/shard_map/sub | solution.py:63
  88.9 13.1 %fusion.13 = bf16[8,64,512]{2,1,0:T(8,128)(2,1)} fusion(bf16[1536,8,64]{0,2,1:T(8,128)(2,1)} %bitcast.57, f32[8,512]{1,0:T(8,128)S(1)} %fusion.89, pred[512,1536]{1,0:T(8,128)(4,1)} %compare_and_fusion, bf16[512,8,64]{0,2,1:T(8,128)(2,1)} %bitcast.59, bf16[1536,8,64]{0,2,1:T(8,128)(2,1)} %bitcast.56), kind=kOutput, calls=%fused_computation.52 | convolution fusion | flops 1642337792 | bytes 4997120 | tf_op jit(solution)/shard_map/hqk,khd->qhd/dot_general | solution.py:128
  102.0 3.1 %convolution_convert_fusion.1 = bf16[512,1024]{1,0:T(8,128)(2,1)} fusion(bf16[512,512]{0,1:T(8,128)(2,1)} %bitcast.92, bf16[512,1024]{1,0:T(8,128)(2,1)} %param.18), kind=kOutput, calls=%fused_computation.50 | convolution fusion | flops 537395200 | bytes 2621440 | tf_op jit(solution)/shard_map/dot_general | solution.py:132
  106.0 30.9 %reduce-scatter.3.cloned.1.call-done = bf16[256,1024]{1,0:T(8,128)(2,1)} async-done(((bf16[512,1024]{1,0:T(8,128)(2,1)}), bf16[256,1024]{1,0:T(8,128)(2,1)}) %reduce-scatter.3.cloned.1.call-update) | async-done | bytes 524304 | tf_op jit(solution)/shard_map/reduce_scatter | solution.py:131
  139.5 3.7 %fusion.26 = f32[256,2048]{1,0:T(8,128)S(1)} fusion(bf16[1024,2048]{1,0:T(8,128)(2,1)} %param.20, bf16[256,1024]{1,0:T(8,128)(2,1)} %reduce-scatter.3.cloned.1.call-done, f32[1024]{0:T(1024)S(1)} %copy-done.12, f32[256]{0:T(256)S(1)} %add_rsqrt_fusion.4, f32[256]{0:T(256)S(1)} %broadcast_multiply_fusion.4, bf16[512,1024]{1,0:T(8,128)(2,1)S(1)} %copy-done.1, ...), kind=kOutput, calls=%fused_computation.75 | convolution fusion | flops 1075576832 | bytes 7346180 | tf_op jit(solution)/shard_map/dot_general | solution.py:142
  143.6 2.3 %collective-permute-start.2 = (bf16[15,1024]{1,0:T(8,128)(2,1)S(1)}, bf16[15,1024]{1,0:T(8,128)(2,1)S(1)}, u32[]{:S(2)}, u32[]{:S(2)}) collective-permute-start(bf16[15,1024]{1,0:T(8,128)(2,1)S(1)} %get-tuple-element.11), channel_id=1, source_target_pairs={{0,1},{1,2},{2,3},{3,4},{4,5},{5,6},{6,7},{7,8},{8,9},{9,10},{10,1... | collective-permute-start | bytes 92168 | tf_op jit(solution)/shard_map/ppermute | solution.py:25
  145.9 2.1 collective-permute-start.3
  148.2 3.0 %collective-permute-done.3 = bf16[15,1024]{1,0:T(8,128)(2,1)S(1)} collective-permute-done((bf16[15,1024]{1,0:T(8,128)(2,1)S(1)}, bf16[15,1024]{1,0:T(8,128)(2,1)S(1)}, u32[]{:S(2)}, u32[]{:S(2)}) %collective-permute-start.3) | collective-permute-done | bytes 30752 | tf_op jit(solution)/shard_map/ppermute | solution.py:28
  151.2 9.6 %fusion.84 = (f32[256]{0:T(256)S(1)}, f32[256,1024]{1,0:T(8,128)S(1)}) fusion(f32[1024]{0:T(1024)S(1)} %bitcast.71, bf16[15,1024]{1,0:T(8,128)(2,1)S(1)} %collective-permute-done.3, bf16[256,1024]{1,0:T(8,128)(2,1)S(1)} %fusion.24, pred[256]{0:T(512)(128)(4,1)S(1)} %get-tuple-element.73, f32[1024]{0:T(1024)S(1)} %bitcast.70, ...), kind=kLoop, calls=%fused_computation.216 | loop fusion | flops 55836416 | bytes 1769984 | tf_op jit(solution)/shard_map/reduce_sum | solution.py:35
  163.7 21.4 %all-gather.2.cloned.1.call-done = bf16[512,1024]{1,0:T(8,128)(2,1)} async-done(((bf16[256,1024]{1,0:T(8,128)(2,1)}), bf16[512,1024]{1,0:T(8,128)(2,1)}) %all-gather.2.cloned.1.call-update) | async-done | bytes 1048592 | tf_op jit(solution)/shard_map/all_gather | solution.py:169
  185.0 9.5 %fusion.12 = bf16[512,1024]{1,0:T(8,128)(2,1)} fusion(bf16[2048,1024]{1,0:T(8,128)(2,1)} %param.26, bf16[512,1024]{1,0:T(8,128)(2,1)} %all-gather.2.cloned.1.call-done, bf16[1024,2048]{1,0:T(8,128)(2,1)} %param.25), kind=kOutput, calls=%fused_computation.49 | convolution fusion | flops 4300734464 | bytes 10485760 | tf_op jit(solution)/shard_map/dot_general | solution.py:176
  194.5 18.1 %reduce-scatter.5.cloned.1.call-done = bf16[256,1024]{1,0:T(8,128)(2,1)} async-done(((bf16[512,1024]{1,0:T(8,128)(2,1)}), bf16[256,1024]{1,0:T(8,128)(2,1)}) %reduce-scatter.5.cloned.1.call-update) | async-done | bytes 524304 | tf_op jit(solution)/shard_map/reduce_scatter | solution.py:175
  (79 shorter events, 18.4 us)
Async XLA Ops:
  6.5 154.5 %copy-start = (bf16[1024,1024]{1,0:T(8,128)(2,1)S(1)}, bf16[1024,1024]{1,0:T(8,128)(2,1)}, u32[]{:S(2)}) copy-start(bf16[1024,1024]{1,0:T(8,128)(2,1)} %param.23) | copy-start | bytes 6291460
  6.5 130.4 %reduce-scatter.3.cloned.1.call-start = ((), (), s32[]{:S(2)}) async-start(), calls=%async_computation.2 | async-start | bytes 1572864 | tf_op jit(solution)/shard_map/reduce_scatter | solution.py:131
  9.8 4.8 %copy-start.1 = (bf16[512,1024]{1,0:T(8,128)(2,1)S(1)}, bf16[512,1024]{1,0:T(8,128)(2,1)}, u32[]{:S(2)}) copy-start(bf16[512,1024]{1,0:T(8,128)(2,1)} %param.15) | copy-start | bytes 3145732
  9.8 4.8 %copy-start.11 = (f32[1024]{0:T(1024)S(1)}, f32[1024]{0:T(1024)}, u32[]{:S(2)}) copy-start(f32[1024]{0:T(1024)} %param.16) | copy-start | bytes 12292
  18.4 1.2 copy-start.5
  19.6 7.9 %copy-start.9 = (s32[128]{0:T(128)S(1)}, s32[128]{0:T(128)}, u32[]{:S(2)}) copy-start(s32[128]{0:T(128)} %param.28) | copy-start | bytes 1540
  19.6 10.4 %copy-start.10 = (s32[128]{0:T(128)S(1)}, s32[128]{0:T(128)}, u32[]{:S(2)}) copy-start(s32[128]{0:T(128)} %param.29) | copy-start | bytes 1540
  20.7 22.7 %collective-permute-start = (bf16[512,1024]{1,0:T(8,128)(2,1)}, bf16[512,1024]{1,0:T(8,128)(2,1)}, u32[]{:S(2)}, u32[]{:S(2)}) collective-permute-start(bf16[512,1024]{1,0:T(8,128)(2,1)} %slice.431), channel_id=1, source_target_pairs={{0,2},{2,4},{4,6},{6,8},{8,10},{10,12},{12,14},{14,16},{16,18},{18... | collective-permute-start | bytes 3145736 | tf_op jit(solution)/shard_map/ppermute | solution.py:17
  43.4 26.6 %collective-permute-start.1 = (bf16[512,1024]{1,0:T(8,128)(2,1)}, bf16[512,1024]{1,0:T(8,128)(2,1)S(1)}, u32[]{:S(2)}, u32[]{:S(2)}) collective-permute-start(bf16[512,1024]{1,0:T(8,128)(2,1)} %collective-permute-done), channel_id=1, source_target_pairs={{0,2},{2,4},{4,6},{6,8},{8,10},{10,12},{12,14},{14,16},{16,18},{18... | collective-permute-start | bytes 3145736 | tf_op jit(solution)/shard_map/ppermute | solution.py:17
  101.9 4.0 %copy-start.6 = (bf16[31,1024]{1,0:T(8,128)(2,1)S(1)}, bf16[31,1024]{1,0:T(8,128)(2,1)}, u32[]{:S(2)}) copy-start(bf16[31,1024]{1,0:T(8,128)(2,1)} %param.21) | copy-start | bytes 190468
  101.9 37.6 %copy-start.12 = (f32[1024]{0:T(1024)S(1)}, f32[1024]{0:T(1024)}, u32[]{:S(2)}) copy-start(f32[1024]{0:T(1024)} %param.19) | copy-start | bytes 12292
  105.1 79.9 %all-gather.2.cloned.1.call-start = ((), (), s32[]{:S(2)}) async-start(), calls=%async_computation.3 | async-start | bytes 1572864 | tf_op jit(solution)/shard_map/all_gather | solution.py:169
  143.3 17.8 %copy-start.2 = (bf16[512,1024]{1,0:T(8,128)(2,1)S(1)}, bf16[512,1024]{1,0:T(8,128)(2,1)}, u32[]{:S(2)}) copy-start(bf16[512,1024]{1,0:T(8,128)(2,1)} %param.15) | copy-start | bytes 3145732
  143.3 17.8 %copy-start.4 = (bf16[256,1024]{1,0:T(8,128)(2,1)S(1)}, bf16[256,1024]{1,0:T(8,128)(2,1)}, u32[]{:S(2)}) copy-start(bf16[256,1024]{1,0:T(8,128)(2,1)} %reduce-scatter.3.cloned.1.call-done) | copy-start | bytes 1572868
  143.3 17.8 %copy-start.13 = (f32[1024]{0:T(1024)S(1)}, f32[1024]{0:T(1024)}, u32[]{:S(2)}) copy-start(f32[1024]{0:T(1024)} %param.22) | copy-start | bytes 12292
  143.6 4.5 %collective-permute-start.2 = (bf16[15,1024]{1,0:T(8,128)(2,1)S(1)}, bf16[15,1024]{1,0:T(8,128)(2,1)S(1)}, u32[]{:S(2)}, u32[]{:S(2)}) collective-permute-start(bf16[15,1024]{1,0:T(8,128)(2,1)S(1)} %get-tuple-element.11), channel_id=1, source_target_pairs={{0,1},{1,2},{2,3},{3,4},{4,5},{5,6},{6,7},{7,8},{8,9},{9,10},{10,1... | collective-permute-start | bytes 92168 | tf_op jit(solution)/shard_map/ppermute | solution.py:25
  145.9 5.2 %collective-permute-start.3 = (bf16[15,1024]{1,0:T(8,128)(2,1)S(1)}, bf16[15,1024]{1,0:T(8,128)(2,1)S(1)}, u32[]{:S(2)}, u32[]{:S(2)}) collective-permute-start(bf16[15,1024]{1,0:T(8,128)(2,1)S(1)} %get-tuple-element.12), channel_id=1, source_target_pairs={{1,0},{2,1},{3,2},{4,3},{5,4},{6,5},{7,6},{8,7},{9,8},{10,9},{11,1... | collective-permute-start | bytes 92168 | tf_op jit(solution)/shard_map/ppermute | solution.py:28
  161.1 1.2 copy-start.7
  163.3 49.3 %reduce-scatter.5.cloned.1.call-start = ((), (), s32[]{:S(2)}) async-start(), calls=%async_computation.4 | async-start | bytes 1572864 | tf_op jit(solution)/shard_map/reduce_scatter | solution.py:175
  194.5 20.8 %copy-start.8 = (f32[1024]{0:T(1024)S(1)}, f32[1024]{0:T(1024)}, u32[]{:S(2)}) copy-start(f32[1024]{0:T(1024)} %param.27) | copy-start | bytes 12292
  212.6 2.7 %copy-start.3 = (bf16[256,1024]{1,0:T(8,128)(2,1)S(1)}, bf16[256,1024]{1,0:T(8,128)(2,1)}, u32[]{:S(2)}) copy-start(bf16[256,1024]{1,0:T(8,128)(2,1)} %reduce-scatter.5.cloned.1.call-done) | copy-start | bytes 1572868
Sparse Core Ops, SparseCore 0:
  105.2 31.6 reduce-scatter.2
  163.5 21.5 all-gather.1
  194.6 17.9 reduce-scatter.4
where the time goes:
time: 224 us; the launch traced here: 223 us
  waiting for transfers between devices  105 us (47%)
  matrix products  44.2 us (20%)
  other arithmetic  25.5 us (11%)
  local copies, waits for them, and re-layouts  18.4 us (8%)
  starting transfers between devices  16.5 us (7%)
  between operations  13.5 us (6%)
    ppermute x2, waiting for transfers between devices, shifted(): lax.ppermute(value, axis, [(source, source + steps) for source in range(f...  31.4 us
    reduce_scatter x1, waiting for transfers between devices, on_device(): lax.psum_scatter(jnp.dot(picked, w_out, preferred_element_type=jnp.float3...  30.9 us
    all_gather x1, waiting for transfers between devices, on_device(): lax.all_gather(ffn_in, 'mp', axis=0, tiled=True)  21.4 us
    reduce_scatter x1, waiting for transfers between devices, on_device(): lax.psum_scatter(jnp.dot(picked, w_down, preferred_element_type=jnp.float...  18.1 us
    reduce_sum x4, other arithmetic, layer_norm(): centred = values - jnp.mean(values, axis=-1, keepdims=True)  13.8 us
    dot_general x1, matrix products, on_device(): jnp.einsum('hqk,khd->qhd', weights, v_rows, preferred_element_type=jnp.fl...  13.1 us
    ppermute x2, starting transfers between devices, shifted(): lax.ppermute(value, axis, [(source, source + steps) for source in range(f...  11.4 us
    sub x1, matrix products, softmax_weights(): raised = jnp.exp(scores - highest)  10.1 us
  transfers between devices with their start and end apart: 7, of which 6 were waited for; matrix products, arithmetic and copies ran while one was open for 3% of the time, Pallas kernels for 0%

commit v1 on v0

v1 whole, which is shorter than its diff:
```python
import jax
import jax.numpy as jnp
from jax import lax
from jax.experimental import pallas as pl
from jax.experimental.pallas import tpu as pltpu
from jax.sharding import PartitionSpec as P

HD = 64
C = 128
LANES = 128
EPSILON = 1e-05
NEGATIVE = -1e30
EDGE = 16
MIB = 1 << 20
VMEM = pl.BlockSpec(memory_space=pltpu.VMEM)
ANY = pl.BlockSpec(memory_space=pl.ANY)


def params(limit):
    return pltpu.CompilerParams(vmem_limit_bytes=limit * MIB)


def cost(macs, read):
    return pl.CostEstimate(flops=2 * macs, bytes_accessed=read, transcendentals=0)


def norm_rows(values, gain):
    centred = values - jnp.mean(values, axis=-1, keepdims=True)
    variance = jnp.mean(centred * centred, axis=-1, keepdims=True)
    return centred * lax.rsqrt(variance + EPSILON) * gain


def sigmoid(values):
    return 0.5 + 0.5 * jnp.tanh(0.5 * values)


def each(rows, step, body):
    for first in range(0, rows, step):
        body(slice(first, first + step))


def send_kernel(frames_ref, gain_ref, out_ref, held, sem):
    rows = out_ref.shape[0]
    first = pl.multiple_of(lax.axis_index("mp") * rows, rows)
    copy = pltpu.make_async_copy(frames_ref.at[pl.ds(first, rows)], held, sem)
    copy.start()
    copy.wait()

    def body(part):
        out_ref[part] = norm_rows(held[part].astype(jnp.float32), gain_ref[...]).astype(
            jnp.bfloat16
        )

    each(rows, 16, body)


def own_kernel(frames_ref, gain_ref, w_ref, lengths_ref, context_ref, qkv_ref, flags_ref, normed):
    rows = frames_ref.shape[0]
    step = pl.program_id(0)

    @pl.when(step == 0)
    def _():
        def body(part):
            normed[part] = norm_rows(
                frames_ref[part].astype(jnp.float32), gain_ref[...]
            ).astype(jnp.bfloat16)

        each(rows, 16, body)
        count = lengths_ref.shape[1]
        lengths = jnp.broadcast_to(lengths_ref[...], (8, count))
        before = (
            lax.broadcasted_iota(jnp.int32, (count, count), 0)
            < lax.broadcasted_iota(jnp.int32, (count, count), 1)
        ).astype(jnp.float32).astype(jnp.bfloat16)
        start = jnp.dot(
            lengths.astype(jnp.float32).astype(jnp.bfloat16),
            before,
            preferred_element_type=jnp.float32,
        )
        stretch = (
            lax.axis_index("tm") * (rows // C)
            - 2
            + lax.broadcasted_iota(jnp.int32, (8, count), 0)
        ).astype(jnp.float32)
        end = start + lengths.astype(jnp.float32)
        member = jnp.where((start <= stretch) & (stretch < end), 1.0, 0.0)
        context = jnp.broadcast_to(context_ref[...], (8, count)).astype(jnp.float32)
        number = lax.broadcasted_iota(jnp.int32, (8, count), 1).astype(jnp.float32) + 1.0
        opening = jnp.sum(member * start, axis=1, keepdims=True)
        reached = jnp.sum(member * context, axis=1, keepdims=True)
        label = jnp.sum(member * number, axis=1, keepdims=True)
        flags_ref[0] = jnp.maximum(stretch[:, :LANES] - reached, opening)
        flags_ref[1] = jnp.broadcast_to(label, (8, LANES))

    scale = jnp.where(step == 0, HD**-0.5, 1.0)
    qkv_ref[0] = (
        jnp.dot(normed[...], w_ref[0], preferred_element_type=jnp.float32) * scale
    ).astype(jnp.bfloat16)


def bias_row(lowest, stretches):
    return jnp.concatenate(
        [jnp.where(stretch >= lowest, 0.0, NEGATIVE) for stretch in stretches], axis=1
    )


def attend(query, keys, values, bias):
    first_head = lax.broadcasted_iota(jnp.int32, (C, LANES), 1) < HD
    zero = jnp.zeros_like(query)
    both = jnp.concatenate(
        [jnp.where(first_head, query, zero), jnp.where(first_head, zero, query)], axis=0
    )
    scores = lax.dot_general(
        both, keys, (((1,), (1,)), ((), ())), preferred_element_type=jnp.float32
    )
    scores = scores + bias
    highest = jnp.max(scores, axis=1, keepdims=True)
    raised = jnp.exp(scores - highest).astype(jnp.bfloat16)
    wide = jnp.concatenate([values, jnp.ones_like(values)], axis=1)
    mixed = jnp.dot(raised, wide, preferred_element_type=jnp.float32)
    total = jnp.where(first_head, mixed[:C, :LANES], mixed[C:, :LANES])
    weight = jnp.where(first_head, mixed[:C, LANES:], mixed[C:, LANES:])
    top = jnp.where(
        first_head,
        jnp.broadcast_to(highest[:C], (C, LANES)),
        jnp.broadcast_to(highest[C:], (C, LANES)),
    )
    return total, top, weight


def place(normed, mine_ref, theirs_ref):
    rows = mine_ref.shape[0]
    core = lax.axis_index("mp")
    normed[pl.ds(pl.multiple_of(core * rows, rows), rows)] = mine_ref[...]
    normed[pl.ds(pl.multiple_of((1 - core) * rows, rows), rows)] = theirs_ref[...]


def near_kernel(
    qkv_ref, mine_ref, theirs_ref, w_ref, flags_ref, total_ref, top_ref, weight_ref,
    normed, keys, values,
):
    slab = qkv_ref.shape[1]
    width = qkv_ref.shape[2]
    count = slab // C
    place(normed, mine_ref, theirs_ref)
    keys[slab:] = qkv_ref[1]
    values[slab:] = qkv_ref[2]
    keys[:slab] = jnp.dot(normed[...], w_ref[1], preferred_element_type=jnp.float32).astype(
        jnp.bfloat16
    )
    values[:slab] = jnp.dot(normed[...], w_ref[2], preferred_element_type=jnp.float32).astype(
        jnp.bfloat16
    )
    first = lax.axis_index("tm") * count - count
    for i in range(count):
        rows = slice(i * C, (i + 1) * C)
        seen = count + i + 1
        lowest = flags_ref[0, 2 + i : 3 + i, :]
        bias = bias_row(lowest, [(first + n).astype(jnp.float32) for n in range(seen)])
        for pair in range(width // LANES):
            cols = slice(pair * LANES, (pair + 1) * LANES)
            total_ref[rows, cols], top_ref[rows, cols], weight_ref[rows, cols] = attend(
                qkv_ref[0, rows, cols], keys[: seen * C, cols], values[: seen * C, cols], bias
            )


def far_kernel(
    q_ref, mine_ref, theirs_ref, w_ref, flags_ref, total_ref, top_ref, weight_ref, w_out_ref,
    heads_ref, sent_ref, normed, keys, values,
):
    slab = q_ref.shape[0]
    width = q_ref.shape[1]
    count = slab // C
    place(normed, mine_ref, theirs_ref)
    keys[...] = jnp.dot(normed[...], w_ref[1], preferred_element_type=jnp.float32).astype(
        jnp.bfloat16
    )
    values[...] = jnp.dot(normed[...], w_ref[2], preferred_element_type=jnp.float32).astype(
        jnp.bfloat16
    )
    first = lax.axis_index("tm") * count - 2 * count
    for i in range(count):
        rows = slice(i * C, (i + 1) * C)
        lowest = flags_ref[0, 2 + i : 3 + i, :]
        bias = bias_row(lowest, [(first + n).astype(jnp.float32) for n in range(i, count)])
        for pair in range(width // LANES):
            cols = slice(pair * LANES, (pair + 1) * LANES)
            total, top, weight = attend(
                q_ref[rows, cols], keys[i * C :, cols], values[i * C :, cols], bias
            )
            near_top = top_ref[rows, cols]
            highest = jnp.maximum(near_top, top)
            near_part = jnp.exp(near_top - highest)
            far_part = jnp.exp(top - highest)
            heads_ref[rows, cols] = (
                (total_ref[rows, cols] * near_part + total * far_part)
                / (weight_ref[rows, cols] * near_part + weight * far_part)
            ).astype(jnp.bfloat16)
    window = sent_ref.shape[0]
    other = (1 - lax.axis_index("mp")) * (slab - window)
    sent_ref[...] = jnp.dot(
        heads_ref[pl.ds(pl.multiple_of(other, EDGE), window)],
        w_out_ref[...],
        preferred_element_type=jnp.float32,
    ).astype(jnp.bfloat16)


def base_kernel(heads_ref, w_out_ref, frames_ref, base_ref):
    slab = heads_ref.shape[0]
    window = base_ref.shape[0]
    first = pl.multiple_of(lax.axis_index("mp") * (slab - window), EDGE)
    base_ref[...] = frames_ref[pl.ds(first, window)].astype(jnp.float32) + jnp.dot(
        heads_ref[pl.ds(first, window)], w_out_ref[...], preferred_element_type=jnp.float32
    ).astype(jnp.bfloat16).astype(jnp.float32)


def gate_kernel(
    base_ref, got_ref, gain_ref, w_ref, gated_ref, edge_ref, first_ref, normed, held
):
    window, width = base_ref.shape
    rows = first_ref.shape[0]

    def body(part):
        value = base_ref[part] + got_ref[part].astype(jnp.float32)
        held[part] = value
        normed[part] = norm_rows(value, gain_ref[...]).astype(jnp.bfloat16)

    each(window, 16, body)
    for part in range(0, width, 256):
        cols = slice(part, part + 256)
        value = jnp.dot(normed[...], w_ref[:, cols], preferred_element_type=jnp.float32)
        gate = jnp.dot(
            normed[...],
            w_ref[:, width + part : width + part + 256],
            preferred_element_type=jnp.float32,
        )
        gated_ref[:, cols] = (value * sigmoid(gate)).astype(jnp.bfloat16)
    core = lax.axis_index("mp")
    edge_ref[...] = gated_ref[pl.ds(pl.multiple_of(core * (window - EDGE), EDGE), EDGE)]
    first_ref[...] = held[pl.ds(pl.multiple_of(core * (window - rows), EDGE), rows)]


def conv_kernel(gated_ref, taps_ref, flags_ref, sum_ref, held, padded):
    window, width = gated_ref.shape
    rows = sum_ref.shape[0]
    half = (taps_ref.shape[0] - 1) // 2
    core = lax.axis_index("mp")
    zeros = jnp.zeros((EDGE, width), jnp.float32)
    held[:EDGE] = zeros
    held[rows + EDGE :] = zeros
    held[pl.ds(pl.multiple_of((1 - core) * EDGE, EDGE), window)] = gated_ref[...].astype(
        jnp.float32
    )
    taps = taps_ref[...].astype(jnp.float32)
    for stretch in range(rows // C):
        at = 2 + (rows // C) * core + stretch
        label = flags_ref[1, pl.ds(at, 1), :]
        before = jnp.where(flags_ref[1, pl.ds(at - 1, 1), :] == label, 1.0, 0.0)
        after = jnp.where(flags_ref[1, pl.ds(at + 1, 1), :] == label, 1.0, 0.0)
        low = stretch * C
        for chunk in range(width // LANES):
            cols = slice(chunk * LANES, (chunk + 1) * LANES)
            padded[chunk, :EDGE] = held[low : low + EDGE, cols] * before
            padded[chunk, EDGE : EDGE + C] = held[low + EDGE : low + EDGE + C, cols]
            padded[chunk, EDGE + C :] = held[low + EDGE + C : low + 2 * EDGE + C, cols] * after
        for chunk in range(width // LANES):
            cols = slice(chunk * LANES, (chunk + 1) * LANES)
            for part in range(0, C, 64):
                total = jnp.zeros((64, LANES), jnp.float32)
                for tap in range(taps_ref.shape[0]):
                    at_row = EDGE - half + part + tap
                    total = total + padded[chunk, at_row : at_row + 64] * taps[tap : tap + 1, cols]
                sum_ref[low + part : low + part + 64, cols] = total


def tail_kernel(
    sum_ref, halo_ref, taps_ref, flags_ref, first_ref, gain_depth_ref, gain_ffn_ref, gain_final_ref,
    w_point_ref, up_own_ref, up_other_ref, down_own_ref, down_other_ref,
    out_ref,
    w_point, up, down, around, depth, normed, second, hidden, feed, point_sem, up_sem, down_sem,
):
    rows, width = sum_ref.shape
    half = (taps_ref.shape[0] - 1) // 2
    units = up_own_ref.shape[1]
    step = 512
    point_copy = pltpu.make_async_copy(w_point_ref, w_point, point_sem)
    point_copy.start()
    up_copies, down_copies = [], []
    for group, ref in enumerate((up_own_ref, up_other_ref)):
        for part in range(units // step):
            copy = pltpu.make_async_copy(
                ref.at[:, part * step : (part + 1) * step],
                up.at[group, :, part * step : (part + 1) * step],
                up_sem.at[group, part],
            )
            copy.start()
            up_copies.append(copy)
    for part in range(width // 256):
        for group, ref in enumerate((down_own_ref, down_other_ref)):
            copy = pltpu.make_async_copy(
                ref.at[:, part * 256 : (part + 1) * 256],
                down.at[group, :, part * 256 : (part + 1) * 256],
                down_sem.at[group, part],
            )
            copy.start()
            down_copies.append(copy)

    core = lax.axis_index("mp")
    at = 2 + 3 * core
    same = jnp.where(
        flags_ref[1, pl.ds(at, 1), :] == flags_ref[1, pl.ds(at - 1 + 2 * core, 1), :], 1.0, 0.0
    )
    taps = taps_ref[...].astype(jnp.float32)
    depth[...] = sum_ref[...]
    around[...] = jnp.zeros_like(around)
    for chunk in range(width // LANES):
        cols = slice(chunk * LANES, (chunk + 1) * LANES)
        around[chunk, pl.ds(pl.multiple_of(core * 2 * EDGE, EDGE), EDGE)] = (
            halo_ref[:, cols].astype(jnp.float32) * same
        )
    edge = pl.ds(pl.multiple_of(core * (rows - EDGE), EDGE), EDGE)
    for chunk in range(width // LANES):
        cols = slice(chunk * LANES, (chunk + 1) * LANES)
        total = jnp.zeros((EDGE, LANES), jnp.float32)
        for tap in range(taps_ref.shape[0]):
            at_row = EDGE - half + tap
            total = total + around[chunk, at_row : at_row + EDGE] * taps[tap : tap + 1, cols]
        depth[edge, cols] = depth[edge, cols] + total

    def squash(part):
        value = norm_rows(depth[part], gain_depth_ref[...])
        normed[part] = (value * sigmoid(value)).astype(jnp.bfloat16)

    each(rows, 16, squash)
    point_copy.wait()
    second[...] = first_ref[...] + jnp.dot(
        normed[...], w_point[...], preferred_element_type=jnp.float32
    )

    def ffn_norm(part):
        normed[part] = norm_rows(second[part], gain_ffn_ref[...]).astype(jnp.bfloat16)

    each(rows, 16, ffn_norm)
    for copy, (group, part) in zip(
        up_copies, [(g, p) for g in range(2) for p in range(units // step)]
    ):
        copy.wait()
        cols = slice(part * step, (part + 1) * step)
        value = jnp.dot(normed[...], up[group, :, cols], preferred_element_type=jnp.float32)
        hidden[group, :, cols] = (value * sigmoid(value)).astype(jnp.bfloat16)
    for part in range(width // 256):
        cols = slice(part * 256, (part + 1) * 256)
        total = 0.0
        for group in range(2):
            down_copies[2 * part + group].wait()
            total = total + jnp.dot(
                hidden[group], down[group, :, cols], preferred_element_type=jnp.float32
            ).astype(jnp.bfloat16).astype(jnp.float32)
        feed[:, cols] = second[:, cols] + 0.5 * total

    def finish(part):
        out_ref[part] = norm_rows(feed[part], gain_final_ref[...]).astype(jnp.bfloat16)

    each(rows, 16, finish)


def on_device(
    frames,
    gain_attn,
    w_qkv,
    w_out,
    gain_conv,
    w_point_in,
    w_depth,
    gain_depth,
    w_point_out,
    gain_ffn,
    w_up,
    w_down,
    gain_final,
    lengths,
    context,
):
    slab, width = frames.shape
    rows = slab // 2
    local = w_qkv.shape[2]
    window = rows + EDGE
    units = w_up.shape[1]
    tm = lax.axis_size("tm")
    bf16, f32 = jnp.bfloat16, jnp.float32
    shape = jax.ShapeDtypeStruct
    swap = [(0, 1), (1, 0)]

    def row(vec):
        return vec.reshape(1, -1)

    w_planes = jnp.transpose(w_qkv, (1, 0, 2))
    sent = pl.pallas_call(
        send_kernel,
        out_shape=shape((rows, width), bf16),
        in_specs=[ANY, VMEM],
        out_specs=VMEM,
        scratch_shapes=[pltpu.VMEM((rows, width), bf16), pltpu.SemaphoreType.DMA],
        compiler_params=params(8),
        cost_estimate=cost(0, 2 * rows * width * 2),
        name="send_norm",
    )(frames, row(gain_attn))
    near_mine = lax.ppermute(sent, "tm", [(i, i + 1) for i in range(tm - 1)])
    far_mine = lax.ppermute(sent, "tm", [(i, i + 2) for i in range(tm - 2)])
    up_other = lax.ppermute(w_up, "mp", swap)
    down_other = lax.ppermute(w_down, "mp", swap)
    qkv, flags = pl.pallas_call(
        own_kernel,
        grid=(3,),
        out_shape=(shape((3, slab, local), bf16), shape((2, 8, LANES), f32)),
        in_specs=[
            pl.BlockSpec((slab, width), lambda i: (0, 0)),
            pl.BlockSpec((1, width), lambda i: (0, 0)),
            pl.BlockSpec((1, width, local), lambda i: (i, 0, 0)),
            pl.BlockSpec((1, lengths.shape[0]), lambda i: (0, 0)),
            pl.BlockSpec((1, lengths.shape[0]), lambda i: (0, 0)),
        ],
        out_specs=(
            pl.BlockSpec((1, slab, local), lambda i: (i, 0, 0)),
            pl.BlockSpec((2, 8, LANES), lambda i: (0, 0, 0)),
        ),
        scratch_shapes=[pltpu.VMEM((slab, width), bf16)],
        compiler_params=params(16),
        cost_estimate=cost(slab * width * 3 * local, width * 3 * local * 2),
        name="own_qkv",
    )(frames, row(gain_attn), w_planes, row(lengths), row(context))
    near_theirs = lax.ppermute(near_mine, "mp", swap)
    total, top, weight = pl.pallas_call(
        near_kernel,
        out_shape=(shape((slab, local), f32),) * 3,
        in_specs=[VMEM] * 5,
        out_specs=(VMEM,) * 3,
        scratch_shapes=[
            pltpu.VMEM((slab, width), bf16),
            pltpu.VMEM((2 * slab, local), bf16),
            pltpu.VMEM((2 * slab, local), bf16),
        ],
        compiler_params=params(24),
        cost_estimate=cost(slab * width * 2 * local + 6 * slab * slab * local, 8 * MIB),
        name="near_attention",
    )(qkv, near_mine, near_theirs, w_planes, flags)
    far_theirs = lax.ppermute(far_mine, "mp", swap)
    heads, to_other = pl.pallas_call(
        far_kernel,
        out_shape=(shape((slab, local), bf16), shape((window, width), bf16)),
        in_specs=[VMEM] * 9,
        out_specs=(VMEM,) * 2,
        scratch_shapes=[
            pltpu.VMEM((slab, width), bf16),
            pltpu.VMEM((slab, local), bf16),
            pltpu.VMEM((slab, local), bf16),
        ],
        compiler_params=params(24),
        cost_estimate=cost(slab * width * 2 * local + 3 * slab * slab * local, 10 * MIB),
        name="far_attention",
    )(qkv[0], far_mine, far_theirs, w_planes, flags, total, top, weight, w_out)
    from_other = lax.ppermute(to_other, "mp", swap)
    base = pl.pallas_call(
        base_kernel,
        out_shape=shape((window, width), f32),
        in_specs=[VMEM] * 3,
        out_specs=VMEM,
        compiler_params=params(12),
        cost_estimate=cost(window * width * local, 3 * MIB),
        name="out_projection",
    )(heads, w_out, frames)
    gated, edge, first_res = pl.pallas_call(
        gate_kernel,
        out_shape=(
            shape((window, width), bf16),
            shape((EDGE, width), bf16),
            shape((rows, width), f32),
        ),
        in_specs=[VMEM] * 4,
        out_specs=(VMEM,) * 3,
        scratch_shapes=[pltpu.VMEM((window, width), bf16), pltpu.VMEM((window, width), f32)],
        compiler_params=params(16),
        cost_estimate=cost(window * width * 2 * width, 5 * MIB),
        name="gated_units",
    )(base, from_other, row(gain_conv), w_point_in)
    halo_pairs = [(2 * i + 1, 2 * i + 2) for i in range(tm - 1)]
    halo = lax.ppermute(edge, ("tm", "mp"), halo_pairs + [(b, a) for a, b in halo_pairs])
    depth_sum = pl.pallas_call(
        conv_kernel,
        out_shape=shape((rows, width), f32),
        in_specs=[VMEM] * 3,
        out_specs=VMEM,
        scratch_shapes=[
            pltpu.VMEM((rows + 2 * EDGE, width), f32),
            pltpu.VMEM((width // LANES, C + 2 * EDGE, LANES), f32),
        ],
        compiler_params=params(12),
        cost_estimate=cost(rows * width * 512, MIB),
        name="depthwise",
    )(gated, w_depth, flags)
    return pl.pallas_call(
        tail_kernel,
        out_shape=shape((rows, width), bf16),
        in_specs=[VMEM] * 8 + [ANY] * 5,
        out_specs=VMEM,
        scratch_shapes=[
            pltpu.VMEM((width, width), bf16),
            pltpu.VMEM((2, width, units), bf16),
            pltpu.VMEM((2, units, width), bf16),
            pltpu.VMEM((width // LANES, 3 * EDGE, LANES), f32),
            pltpu.VMEM((rows, width), f32),
            pltpu.VMEM((rows, width), bf16),
            pltpu.VMEM((rows, width), f32),
            pltpu.VMEM((2, rows, units), bf16),
            pltpu.VMEM((rows, width), f32),
            pltpu.SemaphoreType.DMA,
            pltpu.SemaphoreType.DMA((2, units // 512)),
            pltpu.SemaphoreType.DMA((2, width // 256)),
        ],
        compiler_params=params(40),
        cost_estimate=cost(rows * width * 9 * width, 18 * MIB),
        name="tail",
    )(
        depth_sum, halo, w_depth, flags, first_res, row(gain_depth), row(gain_ffn),
        row(gain_final), w_point_out, w_up, up_other, w_down, down_other,
    )


def solution(mesh):
    in_specs = (
        P("tm", None),
        P(),
        P(None, None, "mp"),
        P("mp", None),
        P(),
        P(),
        P(),
        P(),
        P(),
        P(),
        P(None, "mp"),
        P("mp", None),
        P(),
        P(),
        P(),
    )
    out_specs = P(("tm", "mp"), None)
    return jax.shard_map(
        on_device, mesh=mesh, in_specs=in_specs, out_specs=out_specs, check_vma=False
    )
```

time: 224 us -> 92.7 us (0.41)
  the two profiles are of different devices: /device:TPU:1 before, /device:TPU:256 now
where the time goes in v1:
time: 92.7 us; the launch traced here: 92.2 us
  Pallas kernels  32.3 us (35%)
  waiting for transfers between devices  26 us (28%)
  starting transfers between devices  24.3 us (26%)
  local copies, waits for them, and re-layouts  9.07 us (10%)
    ppermute x1, waiting for transfers between devices, on_device(): near_mine = lax.ppermute(sent, 'tm', [(i, i + 1) for i in range(tm - 1)])  20.8 us
    pallas_call x1, Pallas kernels, on_device(): pl.pallas_call(tail_kernel, out_shape=shape((rows, width), bf16), in_spec...  13.4 us
    unnamed x38, local copies, waits for them, and re-layouts  9.03 us
    pallas_call x1, Pallas kernels, on_device(): pl.pallas_call(near_kernel, out_shape=(shape((slab, local), f32),) * 3, i...  6.67 us
    ppermute x1, starting transfers between devices, on_device(): lax.ppermute(edge, ('tm', 'mp'), halo_pairs + [(b, a) for a, b in halo_pa...  5.55 us
    ppermute x1, starting transfers between devices, on_device(): far_mine = lax.ppermute(sent, 'tm', [(i, i + 2) for i in range(tm - 2)])  4.64 us
    pallas_call x1, Pallas kernels, on_device(): pl.pallas_call(far_kernel, out_shape=(shape((slab, local), bf16), shape((...  4.33 us
    ppermute x1, starting transfers between devices, on_device(): near_mine = lax.ppermute(sent, 'tm', [(i, i + 1) for i in range(tm - 1)])  3.4 us
  transfers between devices with their start and end apart: 8, of which 4 were waited for; matrix products, arithmetic and copies ran while one was open for 0% of the time, Pallas kernels for 20%

profile of v1, /device:TPU:256, one launch (start us, length us, event | category | flops | bytes accessed | tf_op | source)
XLA Modules:
  0.0 92.2 jit_solution(12687053197290955086)
XLA Ops:
  0.0 1.9 %collective-permute-start.6 = (bf16[1024,2048]{1,0:T(8,128)(2,1)}, bf16[1024,2048]{1,0:T(8,128)(2,1)S(1)}, u32[]{:S(2)}, u32[]{:S(2)}) collective-permute-start(bf16[1024,2048]{1,0:T(8,128)(2,1)} %up_own_ref.1), channel_id=1, source_target_pairs={{0,1},{1,0},{2,3},{3,2},{4,5},{5,4},{6,7},{7,6},{8,9},{9,8},{10,11... | collective-permute-start | bytes 12582920 | tf_op jit(solution)/shard_map/ppermute | solution.py:410
  1.9 2.4 %collective-permute-start.7 = (bf16[2048,1024]{1,0:T(8,128)(2,1)}, bf16[2048,1024]{1,0:T(8,128)(2,1)S(1)}, u32[]{:S(2)}, u32[]{:S(2)}) collective-permute-start(bf16[2048,1024]{1,0:T(8,128)(2,1)} %down_own_ref.1), channel_id=1, source_target_pairs={{0,1},{1,0},{2,3},{3,2},{4,5},{5,4},{6,7},{7,6},{8,9},{9,8},{10,11... | collective-permute-start | bytes 12582920 | tf_op jit(solution)/shard_map/ppermute | solution.py:411
  4.3 1.2 %copy-done.2 = bf16[512,1024]{1,0:T(8,128)(2,1)S(1)} copy-done((bf16[512,1024]{1,0:T(8,128)(2,1)S(1)}, bf16[512,1024]{1,0:T(8,128)(2,1)}, u32[]{:S(2)}) %copy-start.2) | copy-done | bytes 1048600
  5.6 0.7 copy-done.10
  6.6 3.4 %collective-permute-start.2 = (bf16[256,1024]{1,0:T(8,128)(2,1)S(1)}, bf16[256,1024]{1,0:T(8,128)(2,1)S(1)}, u32[]{:S(2)}, u32[]{:S(2)}) collective-permute-start(bf16[256,1024]{1,0:T(8,128)(2,1)S(1)} %send_norm.1), channel_id=1, source_target_pairs={{0,2},{2,4},{4,6},{6,8},{8,10},{10,12},{12,14},{14,16},{16,18},{18... | collective-permute-start | bytes 1572872 | tf_op jit(solution)/shard_map/ppermute | solution.py:408
  10.0 4.6 %collective-permute-start = (bf16[256,1024]{1,0:T(8,128)(2,1)S(1)}, bf16[256,1024]{1,0:T(8,128)(2,1)S(1)}, u32[]{:S(2)}, u32[]{:S(2)}) collective-permute-start(bf16[256,1024]{1,0:T(8,128)(2,1)S(1)} %send_norm.1), channel_id=1, source_target_pairs={{0,4},{2,6},{4,8},{6,10},{8,12},{10,14},{12,16},{14,18},{16,20},{1... | collective-permute-start | bytes 1572872 | tf_op jit(solution)/shard_map/ppermute | solution.py:409
  14.7 20.8 %collective-permute-done.2.mine_ref = bf16[256,1024]{1,0:T(8,128)(2,1)S(1)} collective-permute-done((bf16[256,1024]{1,0:T(8,128)(2,1)S(1)}, bf16[256,1024]{1,0:T(8,128)(2,1)S(1)}, u32[]{:S(2)}, u32[]{:S(2)}) %collective-permute-start.2) | collective-permute-done | bytes 524320 | tf_op jit(solution)/shard_map/ppermute | solution.py:408
  35.5 1.9 %collective-permute-start.3 = (bf16[256,1024]{1,0:T(8,128)(2,1)S(1)}, bf16[256,1024]{1,0:T(8,128)(2,1)S(1)}, u32[]{:S(2)}, u32[]{:S(2)}) collective-permute-start(bf16[256,1024]{1,0:T(8,128)(2,1)S(1)} %collective-permute-done.2.mine_ref), channel_id=1, source_target_pairs={{0,1},{1,0},{2,3},{3,2},{4,5},{5,4},{6,7},{7,6},{8,9},{9,8},{10,11... | collective-permute-start | bytes 1572872 | tf_op jit(solution)/shard_map/ppermute | solution.py:432
  37.4 1.6 %collective-permute-done.mine_ref = bf16[256,1024]{1,0:T(8,128)(2,1)S(1)} collective-permute-done((bf16[256,1024]{1,0:T(8,128)(2,1)S(1)}, bf16[256,1024]{1,0:T(8,128)(2,1)S(1)}, u32[]{:S(2)}, u32[]{:S(2)}) %collective-permute-start) | collective-permute-done | bytes 524320 | tf_op jit(solution)/shard_map/ppermute | solution.py:409
  39.0 1.9 %collective-permute-start.1 = (bf16[256,1024]{1,0:T(8,128)(2,1)S(1)}, bf16[256,1024]{1,0:T(8,128)(2,1)S(1)}, u32[]{:S(2)}, u32[]{:S(2)}) collective-permute-start(bf16[256,1024]{1,0:T(8,128)(2,1)S(1)} %collective-permute-done.mine_ref), channel_id=1, source_target_pairs={{0,1},{1,0},{2,3},{3,2},{4,5},{5,4},{6,7},{7,6},{8,9},{9,8},{10,11... | collective-permute-start | bytes 1572872 | tf_op jit(solution)/shard_map/ppermute | solution.py:447
  41.0 1.2 %copy-done.3 = bf16[512,1024]{1,0:T(8,128)(2,1)S(1)} copy-done((bf16[512,1024]{1,0:T(8,128)(2,1)S(1)}, bf16[512,1024]{1,0:T(8,128)(2,1)}, u32[]{:S(2)}) %copy-start.3) | copy-done | bytes 1048600
  42.2 1.9 %copy-done.6 = bf16[1024,3,512]{2,0,1:T(8,128)(2,1)S(1)} copy-done((bf16[1024,3,512]{2,0,1:T(8,128)(2,1)S(1)}, bf16[1024,3,512]{2,0,1:T(8,128)(2,1)}, u32[]{:S(2)}) %copy-start.6) | copy-done | bytes 3145752
  44.1 0.7 copy-done.11
  46.1 2.9 %own_qkv.1 = (bf16[3,512,512]{2,1,0:T(8,128)(2,1)S(1)}, f32[2,8,128]{2,1,0:T(8,128)S(1)}) custom-call(bf16[512,1024]{1,0:T(8,128)(2,1)S(1)} %copy-done.3, f32[1,1024]{1,0:T(1,128)S(1)} %bitcast.14, bf16[3,1024,512]{2,1,0:T(8,128)(2,1)S(1)} %bitcast.10, s32[1,128]{1,0:T(1,128)S(1)} %bitcast.19, s32[1,128]{1,0:T(1,128)S(1)} %bitcast.20), custom_call_target="tpu_custom_call" | custom-call | flops 1610612736 | bytes 3145728 | tf_op jit(solution)/shard_map/own_qkv/pallas_call | solution.py:412
  49.0 6.7 %near_attention.1 = (f32[512,512]{1,0:T(8,128)S(1)}, f32[512,512]{1,0:T(8,128)S(1)}, f32[512,512]{1,0:T(8,128)S(1)}) custom-call(bf16[3,512,512]{2,1,0:T(8,128)(2,1)S(1)} %get-tuple-element.15.qkv_ref, bf16[256,1024]{1,0:T(8,128)(2,1)S(1)} %collective-permute-done.2.mine_ref, bf16[256,1024]{1,0:T(8,128)(2,1)S(1)} %collective-permute-done.3.theirs_ref, ...), custom_call_target="tpu_custom_call" | custom-call | flops 2684354560 | bytes 8388608 | tf_op jit(solution)/shard_map/near_attention/pallas_call | solution.py:433
  55.7 4.3 %far_attention.1 = (bf16[512,512]{1,0:T(8,128)(2,1)S(1)}, bf16[272,1024]{1,0:T(8,128)(2,1)S(1)}) custom-call(bf16[512,512]{1,0:T(8,128)(2,1)S(1)} %slice_bitcast_fusion.q_ref, bf16[256,1024]{1,0:T(8,128)(2,1)S(1)} %collective-permute-done.mine_ref, bf16[256,1024]{1,0:T(8,128)(2,1)S(1)} %collective-permute-done.1.theirs_ref, ...), custom_call_target="tpu_custom_call" | custom-call | flops 1879048192 | bytes 10485760 | tf_op jit(solution)/shard_map/far_attention/pallas_call | solution.py:448
  60.1 2.6 %collective-permute-start.4 = (bf16[272,1024]{1,0:T(8,128)(2,1)S(1)}, bf16[272,1024]{1,0:T(8,128)(2,1)S(1)}, u32[]{:S(2)}, u32[]{:S(2)}) collective-permute-start(bf16[272,1024]{1,0:T(8,128)(2,1)S(1)} %get-tuple-element.21), channel_id=1, source_target_pairs={{0,1},{1,0},{2,3},{3,2},{4,5},{5,4},{6,7},{7,6},{8,9},{9,8},{10,11... | collective-permute-start | bytes 1671176 | tf_op jit(solution)/shard_map/ppermute | solution.py:462
  63.2 0.8 collective-permute-done.4.got_ref
  64.1 1.8 %gated_units.1 = (bf16[272,1024]{1,0:T(8,128)(2,1)S(1)}, bf16[16,1024]{1,0:T(8,128)(2,1)S(1)}, f32[256,1024]{1,0:T(8,128)S(1)}) custom-call(f32[272,1024]{1,0:T(8,128)S(1)} %out_projection.1.base_ref, bf16[272,1024]{1,0:T(8,128)(2,1)S(1)} %collective-permute-done.4.got_ref, f32[1,1024]{1,0:T(1,128)S(1)} %bitcast.15, bf16[1024,2048]{1,0:T(8,128)(2,1)S(1)} %copy-done.5), custom_call_target="tpu_custom_call" | custom-call | flops 1140850688 | bytes 5242880 | tf_op jit(solution)/shard_map/gated_units/pallas_call | solution.py:472
  65.9 5.5 %collective-permute-start.5 = (bf16[16,1024]{1,0:T(8,128)(2,1)S(1)}, bf16[16,1024]{1,0:T(8,128)(2,1)S(1)}, u32[]{:S(2)}, u32[]{:S(2)}) collective-permute-start(bf16[16,1024]{1,0:T(8,128)(2,1)S(1)} %get-tuple-element.23), channel_id=1, source_target_pairs={{1,2},{3,4},{5,6},{7,8},{9,10},{11,12},{13,14},{15,16},{17,18},{19... | collective-permute-start | bytes 98312 | tf_op jit(solution)/shard_map/ppermute | solution.py:487
  71.5 2.3 %depthwise.1.sum_ref = f32[256,1024]{1,0:T(8,128)S(1)} custom-call(bf16[272,1024]{1,0:T(8,128)(2,1)S(1)} %get-tuple-element.22.gated_ref, bf16[31,1024]{1,0:T(8,128)(2,1)S(1)} %copy-done.9, f32[2,8,128]{2,1,0:T(8,128)S(1)} %get-tuple-element.16.flags_ref), custom_call_target="tpu_custom_call" | custom-call | flops 268435456 | bytes 1048576 | tf_op jit(solution)/shard_map/depthwise/pallas_call | solution.py:488
  73.8 2.8 %collective-permute-done.5.halo_ref = bf16[16,1024]{1,0:T(8,128)(2,1)S(1)} collective-permute-done((bf16[16,1024]{1,0:T(8,128)(2,1)S(1)}, bf16[16,1024]{1,0:T(8,128)(2,1)S(1)}, u32[]{:S(2)}, u32[]{:S(2)}) %collective-permute-start.5) | collective-permute-done | bytes 32800 | tf_op jit(solution)/shard_map/ppermute | solution.py:487
  76.6 2.0 %copy-done.18 = bf16[2048,1024]{1,0:T(8,128)(2,1)} copy-done((bf16[2048,1024]{1,0:T(8,128)(2,1)}, bf16[2048,1024]{1,0:T(8,128)(2,1)S(1)}, u32[]{:S(2)}) %copy-start.18) | copy-done | bytes 4194328
  78.6 13.4 %tail.1 = bf16[256,1024]{1,0:T(8,128)(2,1)} custom-call(f32[256,1024]{1,0:T(8,128)S(1)} %depthwise.1.sum_ref, bf16[16,1024]{1,0:T(8,128)(2,1)S(1)} %collective-permute-done.5.halo_ref, bf16[31,1024]{1,0:T(8,128)(2,1)S(1)} %copy-done.9, f32[2,8,128]{2,1,0:T(8,128)S(1)} %get-tuple-element.16.flags_ref, f32[256,1024]{1,0:T(8,128)S(1)} %get-tuple-element.24.first_ref, ...), custom_call_target="tpu_custom_call" | custom-call | flops 4831838208 | bytes 18874368 | tf_op jit(solution)/shard_map/tail/pallas_call | solution.py:501
  (39 shorter events, 2.3 us)
Async XLA Ops:
  0.0 76.6 %collective-permute-start.6 = (bf16[1024,2048]{1,0:T(8,128)(2,1)}, bf16[1024,2048]{1,0:T(8,128)(2,1)S(1)}, u32[]{:S(2)}, u32[]{:S(2)}) collective-permute-start(bf16[1024,2048]{1,0:T(8,128)(2,1)} %up_own_ref.1), channel_id=1, source_target_pairs={{0,1},{1,0},{2,3},{3,2},{4,5},{5,4},{6,7},{7,6},{8,9},{9,8},{10,11... | collective-permute-start | bytes 12582920 | tf_op jit(solution)/shard_map/ppermute | solution.py:410
  1.9 74.7 %collective-permute-start.7 = (bf16[2048,1024]{1,0:T(8,128)(2,1)}, bf16[2048,1024]{1,0:T(8,128)(2,1)S(1)}, u32[]{:S(2)}, u32[]{:S(2)}) collective-permute-start(bf16[2048,1024]{1,0:T(8,128)(2,1)} %down_own_ref.1), channel_id=1, source_target_pairs={{0,1},{1,0},{2,3},{3,2},{4,5},{5,4},{6,7},{7,6},{8,9},{9,8},{10,11... | collective-permute-start | bytes 12582920 | tf_op jit(solution)/shard_map/ppermute | solution.py:411
  4.3 1.2 %copy-start.2 = (bf16[512,1024]{1,0:T(8,128)(2,1)S(1)}, bf16[512,1024]{1,0:T(8,128)(2,1)}, u32[]{:S(2)}) copy-start(bf16[512,1024]{1,0:T(8,128)(2,1)} %frames_ref.5) | copy-start | bytes 3145732
  5.6 0.7 copy-start.10
  6.6 28.9 %collective-permute-start.2 = (bf16[256,1024]{1,0:T(8,128)(2,1)S(1)}, bf16[256,1024]{1,0:T(8,128)(2,1)S(1)}, u32[]{:S(2)}, u32[]{:S(2)}) collective-permute-start(bf16[256,1024]{1,0:T(8,128)(2,1)S(1)} %send_norm.1), channel_id=1, source_target_pairs={{0,2},{2,4},{4,6},{6,8},{8,10},{10,12},{12,14},{14,16},{16,18},{18... | collective-permute-start | bytes 1572872 | tf_op jit(solution)/shard_map/ppermute | solution.py:408
  10.0 29.0 %collective-permute-start = (bf16[256,1024]{1,0:T(8,128)(2,1)S(1)}, bf16[256,1024]{1,0:T(8,128)(2,1)S(1)}, u32[]{:S(2)}, u32[]{:S(2)}) collective-permute-start(bf16[256,1024]{1,0:T(8,128)(2,1)S(1)} %send_norm.1), channel_id=1, source_target_pairs={{0,4},{2,6},{4,8},{6,10},{8,12},{10,14},{12,16},{14,18},{16,20},{1... | collective-permute-start | bytes 1572872 | tf_op jit(solution)/shard_map/ppermute | solution.py:409
  35.5 13.5 %collective-permute-start.3 = (bf16[256,1024]{1,0:T(8,128)(2,1)S(1)}, bf16[256,1024]{1,0:T(8,128)(2,1)S(1)}, u32[]{:S(2)}, u32[]{:S(2)}) collective-permute-start(bf16[256,1024]{1,0:T(8,128)(2,1)S(1)} %collective-permute-done.2.mine_ref), channel_id=1, source_target_pairs={{0,1},{1,0},{2,3},{3,2},{4,5},{5,4},{6,7},{7,6},{8,9},{9,8},{10,11... | collective-permute-start | bytes 1572872 | tf_op jit(solution)/shard_map/ppermute | solution.py:432
  39.0 16.7 %collective-permute-start.1 = (bf16[256,1024]{1,0:T(8,128)(2,1)S(1)}, bf16[256,1024]{1,0:T(8,128)(2,1)S(1)}, u32[]{:S(2)}, u32[]{:S(2)}) collective-permute-start(bf16[256,1024]{1,0:T(8,128)(2,1)S(1)} %collective-permute-done.mine_ref), channel_id=1, source_target_pairs={{0,1},{1,0},{2,3},{3,2},{4,5},{5,4},{6,7},{7,6},{8,9},{9,8},{10,11... | collective-permute-start | bytes 1572872 | tf_op jit(solution)/shard_map/ppermute | solution.py:447
  41.0 1.2 %copy-start.3 = (bf16[512,1024]{1,0:T(8,128)(2,1)S(1)}, bf16[512,1024]{1,0:T(8,128)(2,1)}, u32[]{:S(2)}) copy-start(bf16[512,1024]{1,0:T(8,128)(2,1)} %frames_ref.5) | copy-start | bytes 3145732
  42.2 1.9 %copy-start.6 = (bf16[1024,3,512]{2,0,1:T(8,128)(2,1)S(1)}, bf16[1024,3,512]{2,0,1:T(8,128)(2,1)}, u32[]{:S(2)}) copy-start(bf16[1024,3,512]{2,0,1:T(8,128)(2,1)} %param.17) | copy-start | bytes 9437188
  46.1 2.9 %copy-start.7 = (bf16[1024,3,512]{2,0,1:T(8,128)(2,1)S(1)}, bf16[1024,3,512]{2,0,1:T(8,128)(2,1)}, u32[]{:S(2)}) copy-start(bf16[1024,3,512]{2,0,1:T(8,128)(2,1)} %param.17) | copy-start | bytes 9437188
  49.0 6.7 %copy-start.1 = (bf16[512,1024]{1,0:T(8,128)(2,1)S(1)}, bf16[512,1024]{1,0:T(8,128)(2,1)}, u32[]{:S(2)}) copy-start(bf16[512,1024]{1,0:T(8,128)(2,1)} %w_out_ref.3) | copy-start | bytes 3145732
  55.7 7.0 %copy-start.4 = (bf16[512,1024]{1,0:T(8,128)(2,1)S(1)}, bf16[512,1024]{1,0:T(8,128)(2,1)}, u32[]{:S(2)}) copy-start(bf16[512,1024]{1,0:T(8,128)(2,1)} %frames_ref.5) | copy-start | bytes 3145732
  55.7 8.3 %copy-start.5 = (bf16[1024,2048]{1,0:T(8,128)(2,1)S(1)}, bf16[1024,2048]{1,0:T(8,128)(2,1)}, u32[]{:S(2)}) copy-start(bf16[1024,2048]{1,0:T(8,128)(2,1)} %w_ref.1) | copy-start | bytes 12582916
  55.7 8.3 %copy-start.12 = (f32[1024]{0:T(1024)S(1)}, f32[1024]{0:T(1024)}, u32[]{:S(2)}) copy-start(f32[1024]{0:T(1024)} %param.19) | copy-start | bytes 12292
  60.1 4.0 %collective-permute-start.4 = (bf16[272,1024]{1,0:T(8,128)(2,1)S(1)}, bf16[272,1024]{1,0:T(8,128)(2,1)S(1)}, u32[]{:S(2)}, u32[]{:S(2)}) collective-permute-start(bf16[272,1024]{1,0:T(8,128)(2,1)S(1)} %get-tuple-element.21), channel_id=1, source_target_pairs={{0,1},{1,0},{2,3},{3,2},{4,5},{5,4},{6,7},{7,6},{8,9},{9,8},{10,11... | collective-permute-start | bytes 1671176 | tf_op jit(solution)/shard_map/ppermute | solution.py:462
  62.7 8.8 %copy-start.9 = (bf16[31,1024]{1,0:T(8,128)(2,1)S(1)}, bf16[31,1024]{1,0:T(8,128)(2,1)}, u32[]{:S(2)}) copy-start(bf16[31,1024]{1,0:T(8,128)(2,1)} %taps_ref.3) | copy-start | bytes 190468
  63.2 15.4 %copy-start = (bf16[1024,2048]{1,0:T(8,128)(2,1)S(1)}, bf16[1024,2048]{1,0:T(8,128)(2,1)}, u32[]{:S(2)}) copy-start(bf16[1024,2048]{1,0:T(8,128)(2,1)} %up_own_ref.1) | copy-start | bytes 12582916
  63.2 15.4 %copy-start.8 = (bf16[1024,1024]{1,0:T(8,128)(2,1)S(1)}, bf16[1024,1024]{1,0:T(8,128)(2,1)}, u32[]{:S(2)}) copy-start(bf16[1024,1024]{1,0:T(8,128)(2,1)} %w_point_ref.1) | copy-start | bytes 6291460
  63.2 15.4 %copy-start.13 = (f32[1024]{0:T(1024)S(1)}, f32[1024]{0:T(1024)}, u32[]{:S(2)}) copy-start(f32[1024]{0:T(1024)} %param.22) | copy-start | bytes 12292
  63.2 15.4 %copy-start.14 = (f32[1024]{0:T(1024)S(1)}, f32[1024]{0:T(1024)}, u32[]{:S(2)}) copy-start(f32[1024]{0:T(1024)} %param.24) | copy-start | bytes 12292
  63.2 15.3 %copy-start.15 = (f32[1024]{0:T(1024)S(1)}, f32[1024]{0:T(1024)}, u32[]{:S(2)}) copy-start(f32[1024]{0:T(1024)} %param.27) | copy-start | bytes 12292
  65.9 10.7 %collective-permute-start.5 = (bf16[16,1024]{1,0:T(8,128)(2,1)S(1)}, bf16[16,1024]{1,0:T(8,128)(2,1)S(1)}, u32[]{:S(2)}, u32[]{:S(2)}) collective-permute-start(bf16[16,1024]{1,0:T(8,128)(2,1)S(1)} %get-tuple-element.23), channel_id=1, source_target_pairs={{1,2},{3,4},{5,6},{7,8},{9,10},{11,12},{13,14},{15,16},{17,18},{19... | collective-permute-start | bytes 98312 | tf_op jit(solution)/shard_map/ppermute | solution.py:487
  76.6 2.0 %copy-start.18 = (bf16[2048,1024]{1,0:T(8,128)(2,1)}, bf16[2048,1024]{1,0:T(8,128)(2,1)S(1)}, u32[]{:S(2)}) copy-start(bf16[2048,1024]{1,0:T(8,128)(2,1)S(1)} %collective-permute-done.7.down_other_ref) | copy-start | bytes 12582916
  (3 other events, 2.0 us)

commit v2 on v1

--- a/solution.py
+++ b/solution.py
@@ -12,16 +12,20 @@
 NEGATIVE = -1e30
 EDGE = 16
 MIB = 1 << 20
+EARLY = 0.001
+LATE = 4.0
 VMEM = pl.BlockSpec(memory_space=pltpu.VMEM)
-ANY = pl.BlockSpec(memory_space=pl.ANY)
+HBM = pl.BlockSpec(memory_space=pltpu.HBM)
 
 
 def params(limit):
     return pltpu.CompilerParams(vmem_limit_bytes=limit * MIB)
 
 
-def cost(macs, read):
-    return pl.CostEstimate(flops=2 * macs, bytes_accessed=read, transcendentals=0)
+def cost(macs, read, share=1.0):
+    return pl.CostEstimate(
+        flops=int(2 * macs * share), bytes_accessed=int(read * share), transcendentals=0
+    )
 
 
 def norm_rows(values, gain):
@@ -39,17 +43,20 @@
         body(slice(first, first + step))
 
 
-def send_kernel(frames_ref, gain_ref, out_ref, held, sem):
+def send_kernel(frames_ref, gain_ref, out_ref, held, gain, sem):
     rows = out_ref.shape[0]
     first = pl.multiple_of(lax.axis_index("mp") * rows, rows)
-    copy = pltpu.make_async_copy(frames_ref.at[pl.ds(first, rows)], held, sem)
-    copy.start()
-    copy.wait()
+    copies = [
+        pltpu.make_async_copy(gain_ref, gain, sem.at[0]),
+        pltpu.make_async_copy(frames_ref.at[pl.ds(first, rows)], held, sem.at[1]),
+    ]
+    for copy in copies:
+        copy.start()
+    for copy in copies:
+        copy.wait()
 
     def body(part):
-        out_ref[part] = norm_rows(held[part].astype(jnp.float32), gain_ref[...]).astype(
-            jnp.bfloat16
-        )
+        out_ref[part] = norm_rows(held[part].astype(jnp.float32), gain[...]).astype(jnp.bfloat16)
 
     each(rows, 16, body)
 
@@ -135,41 +142,66 @@
     normed[pl.ds(pl.multiple_of((1 - core) * rows, rows), rows)] = theirs_ref[...]
 
 
+def merged(parts, total, top, weight):
+    other_total, other_top, other_weight = parts
+    highest = jnp.maximum(other_top, top)
+    other_part = jnp.exp(other_top - highest)
+    part = jnp.exp(top - highest)
+    return (
+        other_total * other_part + total * part,
+        highest,
+        other_weight * other_part + weight * part,
+    )
+
+
+def self_kernel(qkv_ref, flags_ref, total_ref, top_ref, weight_ref):
+    slab, width = qkv_ref.shape[1:]
+    count = slab // C
+    first = lax.axis_index("tm") * count
+    for i in range(count):
+        rows = slice(i * C, (i + 1) * C)
+        lowest = flags_ref[0, 2 + i : 3 + i, :]
+        bias = bias_row(lowest, [(first + n).astype(jnp.float32) for n in range(i + 1)])
+        for pair in range(width // LANES):
+            cols = slice(pair * LANES, (pair + 1) * LANES)
+            seen = slice(0, (i + 1) * C)
+            total_ref[rows, cols], top_ref[rows, cols], weight_ref[rows, cols] = attend(
+                qkv_ref[0, rows, cols], qkv_ref[1, seen, cols], qkv_ref[2, seen, cols], bias
+            )
+
+
 def near_kernel(
-    qkv_ref, mine_ref, theirs_ref, w_ref, flags_ref, total_ref, top_ref, weight_ref,
+    qkv_ref, mine_ref, theirs_ref, w_ref, flags_ref, own_total_ref, own_top_ref, own_weight_ref,
+    total_ref, top_ref, weight_ref,
     normed, keys, values,
 ):
-    slab = qkv_ref.shape[1]
-    width = qkv_ref.shape[2]
+    slab, width = qkv_ref.shape[1:]
     count = slab // C
     place(normed, mine_ref, theirs_ref)
-    keys[slab:] = qkv_ref[1]
-    values[slab:] = qkv_ref[2]
-    keys[:slab] = jnp.dot(normed[...], w_ref[1], preferred_element_type=jnp.float32).astype(
+    keys[...] = jnp.dot(normed[...], w_ref[1], preferred_element_type=jnp.float32).astype(
         jnp.bfloat16
     )
-    values[:slab] = jnp.dot(normed[...], w_ref[2], preferred_element_type=jnp.float32).astype(
+    values[...] = jnp.dot(normed[...], w_ref[2], preferred_element_type=jnp.float32).astype(
         jnp.bfloat16
     )
     first = lax.axis_index("tm") * count - count
     for i in range(count):
         rows = slice(i * C, (i + 1) * C)
-        seen = count + i + 1
         lowest = flags_ref[0, 2 + i : 3 + i, :]
-        bias = bias_row(lowest, [(first + n).astype(jnp.float32) for n in range(seen)])
+        bias = bias_row(lowest, [(first + n).astype(jnp.float32) for n in range(count)])
         for pair in range(width // LANES):
             cols = slice(pair * LANES, (pair + 1) * LANES)
-            total_ref[rows, cols], top_ref[rows, cols], weight_ref[rows, cols] = attend(
-                qkv_ref[0, rows, cols], keys[: seen * C, cols], values[: seen * C, cols], bias
+            parts = own_total_ref[rows, cols], own_top_ref[rows, cols], own_weight_ref[rows, cols]
+            total_ref[rows, cols], top_ref[rows, cols], weight_ref[rows, cols] = merged(
+                parts, *attend(qkv_ref[0, rows, cols], keys[:, cols], values[:, cols], bias)
             )
 
 
 def far_kernel(
-    q_ref, mine_ref, theirs_ref, w_ref, flags_ref, total_ref, top_ref, weight_ref, w_out_ref,
+    qkv_ref, mine_ref, theirs_ref, w_ref, flags_ref, total_ref, top_ref, weight_ref, w_out_ref,
     heads_ref, sent_ref, normed, keys, values,
 ):
-    slab = q_ref.shape[0]
-    width = q_ref.shape[1]
+    slab, width = qkv_ref.shape[1:]
     count = slab // C
     place(normed, mine_ref, theirs_ref)
     keys[...] = jnp.dot(normed[...], w_ref[1], preferred_element_type=jnp.float32).astype(
@@ -186,16 +218,11 @@
         for pair in range(width // LANES):
             cols = slice(pair * LANES, (pair + 1) * LANES)
             total, top, weight = attend(
-                q_ref[rows, cols], keys[i * C :, cols], values[i * C :, cols], bias
+                qkv_ref[0, rows, cols], keys[i * C :, cols], values[i * C :, cols], bias
             )
-            near_top = top_ref[rows, cols]
-            highest = jnp.maximum(near_top, top)
-            near_part = jnp.exp(near_top - highest)
-            far_part = jnp.exp(top - highest)
-            heads_ref[rows, cols] = (
-                (total_ref[rows, cols] * near_part + total * far_part)
-                / (weight_ref[rows, cols] * near_part + weight * far_part)
-            ).astype(jnp.bfloat16)
+            parts = total_ref[rows, cols], top_ref[rows, cols], weight_ref[rows, cols]
+            total, _, weight = merged(parts, total, top, weight)
+            heads_ref[rows, cols] = (total / weight).astype(jnp.bfloat16)
     window = sent_ref.shape[0]
     other = (1 - lax.axis_index("mp")) * (slab - window)
     sent_ref[...] = jnp.dot(
@@ -277,24 +304,13 @@
     sum_ref, halo_ref, taps_ref, flags_ref, first_ref, gain_depth_ref, gain_ffn_ref, gain_final_ref,
     w_point_ref, up_own_ref, up_other_ref, down_own_ref, down_other_ref,
     out_ref,
-    w_point, up, down, around, depth, normed, second, hidden, feed, point_sem, up_sem, down_sem,
+    down, around, depth, normed, second, hidden, feed, down_sem,
 ):
     rows, width = sum_ref.shape
     half = (taps_ref.shape[0] - 1) // 2
     units = up_own_ref.shape[1]
     step = 512
-    point_copy = pltpu.make_async_copy(w_point_ref, w_point, point_sem)
-    point_copy.start()
-    up_copies, down_copies = [], []
-    for group, ref in enumerate((up_own_ref, up_other_ref)):
-        for part in range(units // step):
-            copy = pltpu.make_async_copy(
-                ref.at[:, part * step : (part + 1) * step],
-                up.at[group, :, part * step : (part + 1) * step],
-                up_sem.at[group, part],
-            )
-            copy.start()
-            up_copies.append(copy)
+    down_copies = []
     for part in range(width // 256):
         for group, ref in enumerate((down_own_ref, down_other_ref)):
             copy = pltpu.make_async_copy(
@@ -332,22 +348,19 @@
         normed[part] = (value * sigmoid(value)).astype(jnp.bfloat16)
 
     each(rows, 16, squash)
-    point_copy.wait()
     second[...] = first_ref[...] + jnp.dot(
-        normed[...], w_point[...], preferred_element_type=jnp.float32
+        normed[...], w_point_ref[...], preferred_element_type=jnp.float32
     )
 
     def ffn_norm(part):
         normed[part] = norm_rows(second[part], gain_ffn_ref[...]).astype(jnp.bfloat16)
 
     each(rows, 16, ffn_norm)
-    for copy, (group, part) in zip(
-        up_copies, [(g, p) for g in range(2) for p in range(units // step)]
-    ):
-        copy.wait()
-        cols = slice(part * step, (part + 1) * step)
-        value = jnp.dot(normed[...], up[group, :, cols], preferred_element_type=jnp.float32)
-        hidden[group, :, cols] = (value * sigmoid(value)).astype(jnp.bfloat16)
+    for group, ref in enumerate((up_own_ref, up_other_ref)):
+        for part in range(units // step):
+            cols = slice(part * step, (part + 1) * step)
+            value = jnp.dot(normed[...], ref[:, cols], preferred_element_type=jnp.float32)
+            hidden[group, :, cols] = (value * sigmoid(value)).astype(jnp.bfloat16)
     for part in range(width // 256):
         cols = slice(part * 256, (part + 1) * 256)
         total = 0.0
@@ -398,17 +411,19 @@
     sent = pl.pallas_call(
         send_kernel,
         out_shape=shape((rows, width), bf16),
-        in_specs=[ANY, VMEM],
+        in_specs=[HBM, HBM],
         out_specs=VMEM,
-        scratch_shapes=[pltpu.VMEM((rows, width), bf16), pltpu.SemaphoreType.DMA],
+        scratch_shapes=[
+            pltpu.VMEM((rows, width), bf16),
+            pltpu.VMEM((1, width), f32),
+            pltpu.SemaphoreType.DMA((2,)),
+        ],
         compiler_params=params(8),
         cost_estimate=cost(0, 2 * rows * width * 2),
         name="send_norm",
     )(frames, row(gain_attn))
+    own_frames, sent = lax.optimization_barrier((frames, sent))
     near_mine = lax.ppermute(sent, "tm", [(i, i + 1) for i in range(tm - 1)])
-    far_mine = lax.ppermute(sent, "tm", [(i, i + 2) for i in range(tm - 2)])
-    up_other = lax.ppermute(w_up, "mp", swap)
-    down_other = lax.ppermute(w_down, "mp", swap)
     qkv, flags = pl.pallas_call(
         own_kernel,
         grid=(3,),
@@ -426,24 +441,40 @@
         ),
         scratch_shapes=[pltpu.VMEM((slab, width), bf16)],
         compiler_params=params(16),
-        cost_estimate=cost(slab * width * 3 * local, width * 3 * local * 2),
+        cost_estimate=cost(slab * width * 3 * local, width * 3 * local * 2, EARLY),
         name="own_qkv",
-    )(frames, row(gain_attn), w_planes, row(lengths), row(context))
+    )(own_frames, row(gain_attn), w_planes, row(lengths), row(context))
+    partial = (shape((slab, local), f32),) * 3
+    own_parts = pl.pallas_call(
+        self_kernel,
+        out_shape=partial,
+        in_specs=[VMEM] * 2,
+        out_specs=(VMEM,) * 3,
+        compiler_params=params(16),
+        cost_estimate=cost(5 * slab * slab * local, 4 * MIB, EARLY),
+        name="own_attention",
+    )(qkv, flags)
+    up_held, down_held, own_parts = lax.optimization_barrier((w_up, w_down, own_parts))
+    up_other = lax.ppermute(up_held, "mp", swap)
+    down_other = lax.ppermute(down_held, "mp", swap)
+    near_mine, own_parts = lax.optimization_barrier((near_mine, own_parts))
+    far_mine = lax.ppermute(near_mine, "tm", [(i, i + 1) for i in range(tm - 1)])
     near_theirs = lax.ppermute(near_mine, "mp", swap)
-    total, top, weight = pl.pallas_call(
+    near_parts = pl.pallas_call(
         near_kernel,
-        out_shape=(shape((slab, local), f32),) * 3,
-        in_specs=[VMEM] * 5,
+        out_shape=partial,
+        in_specs=[VMEM] * 8,
         out_specs=(VMEM,) * 3,
         scratch_shapes=[
             pltpu.VMEM((slab, width), bf16),
-            pltpu.VMEM((2 * slab, local), bf16),
-            pltpu.VMEM((2 * slab, local), bf16),
+            pltpu.VMEM((slab, local), bf16),
+            pltpu.VMEM((slab, local), bf16),
         ],
-        compiler_params=params(24),
-        cost_estimate=cost(slab * width * 2 * local + 6 * slab * slab * local, 8 * MIB),
+        compiler_params=params(16),
+        cost_estimate=cost(slab * width * 2 * local + 8 * slab * slab * local, 8 * MIB, LATE),
         name="near_attention",
-    )(qkv, near_mine, near_theirs, w_planes, flags)
+    )(qkv, near_mine, near_theirs, w_planes, flags, *own_parts)
+    far_mine, near_parts = lax.optimization_barrier((far_mine, near_parts))
     far_theirs = lax.ppermute(far_mine, "mp", swap)
     heads, to_other = pl.pallas_call(
         far_kernel,
@@ -455,10 +486,10 @@
             pltpu.VMEM((slab, local), bf16),
             pltpu.VMEM((slab, local), bf16),
         ],
-        compiler_params=params(24),
-        cost_estimate=cost(slab * width * 2 * local + 3 * slab * slab * local, 10 * MIB),
+        compiler_params=params(16),
+        cost_estimate=cost(slab * width * 2 * local + 3 * slab * slab * local, 10 * MIB, LATE),
         name="far_attention",
-    )(qkv[0], far_mine, far_theirs, w_planes, flags, total, top, weight, w_out)
+    )(qkv, far_mine, far_theirs, w_planes, flags, *near_parts, w_out)
     from_other = lax.ppermute(to_other, "mp", swap)
     base = pl.pallas_call(
         base_kernel,
@@ -466,7 +497,7 @@
         in_specs=[VMEM] * 3,
         out_specs=VMEM,
         compiler_params=params(12),
-        cost_estimate=cost(window * width * local, 3 * MIB),
+        cost_estimate=cost(window * width * local, 3 * MIB, LATE),
         name="out_projection",
     )(heads, w_out, frames)
     gated, edge, first_res = pl.pallas_call(
@@ -480,7 +511,7 @@
         out_specs=(VMEM,) * 3,
         scratch_shapes=[pltpu.VMEM((window, width), bf16), pltpu.VMEM((window, width), f32)],
         compiler_params=params(16),
-        cost_estimate=cost(window * width * 2 * width, 5 * MIB),
+        cost_estimate=cost(window * width * 2 * width, 5 * MIB, LATE),
         name="gated_units",
     )(base, from_other, row(gain_conv), w_point_in)
     halo_pairs = [(2 * i + 1, 2 * i + 2) for i in range(tm - 1)]
@@ -495,17 +526,15 @@
             pltpu.VMEM((width // LANES, C + 2 * EDGE, LANES), f32),
         ],
         compiler_params=params(12),
-        cost_estimate=cost(rows * width * 512, MIB),
+        cost_estimate=cost(rows * width * 512, MIB, LATE),
         name="depthwise",
     )(gated, w_depth, flags)
     return pl.pallas_call(
         tail_kernel,
         out_shape=shape((rows, width), bf16),
-        in_specs=[VMEM] * 8 + [ANY] * 5,
+        in_specs=[VMEM] * 11 + [HBM] * 2,
         out_specs=VMEM,
         scratch_shapes=[
-            pltpu.VMEM((width, width), bf16),
-            pltpu.VMEM((2, width, units), bf16),
             pltpu.VMEM((2, units, width), bf16),
             pltpu.VMEM((width // LANES, 3 * EDGE, LANES), f32),
             pltpu.VMEM((rows, width), f32),
@@ -513,12 +542,10 @@
             pltpu.VMEM((rows, width), f32),
             pltpu.VMEM((2, rows, units), bf16),
             pltpu.VMEM((rows, width), f32),
-            pltpu.SemaphoreType.DMA,
-            pltpu.SemaphoreType.DMA((2, units // 512)),
             pltpu.SemaphoreType.DMA((2, width // 256)),
         ],
-        compiler_params=params(40),
-        cost_estimate=cost(rows * width * 9 * width, 18 * MIB),
+        compiler_params=params(20),
+        cost_estimate=cost(rows * width * 9 * width, 18 * MIB, LATE),
         name="tail",
     )(
         depth_sum, halo, w_depth, flags, first_res, row(gain_depth), row(gain_ffn),

time: 92.7 us -> 84.6 us (0.913)
  starting transfers between devices: 24.3 us -> 18.6 us
  local copies, waits for them, and re-layouts: 9.07 us -> 7.08 us
  Pallas kernels: 32.3 us -> 31.1 us
    ppermute x1, waiting for transfers between devices: 20.8 us -> 2.5 us  [on_device(): near_mine = lax.ppermute(sent, 'tm', [(i, i + 1) for i in range(tm - 1)])]
    ppermute x3, waiting for transfers between devices: 1.61 us -> 10.1 us  [the longest x1 10.1 us: on_device(): lax.ppermute(near_mine, 'tm', [(i, i + 1) for i in range(tm - 1)])]
    ppermute x1, waiting for transfers between devices: 0.01 us -> 5.11 us  [on_device(): near_theirs = lax.ppermute(near_mine, 'mp', swap)]
    ppermute x1, waiting for transfers between devices: 2.76 us -> 6.17 us  [on_device(): lax.ppermute(edge, ('tm', 'mp'), halo_pairs + [(b, a) for a, b in halo_pa...]
    ppermute x1, starting transfers between devices: 5.55 us -> 2.4 us  [on_device(): lax.ppermute(edge, ('tm', 'mp'), halo_pairs + [(b, a) for a, b in halo_pa...]
    ppermute x3, starting transfers between devices: 8.96 us -> 6.38 us  [the longest x1 2.41 us: on_device(): down_other = lax.ppermute(down_held, 'mp', swap)]
    unnamed x38, local copies, waits for them, and re-layouts: 9.03 us -> 7.08 us
    ppermute x1, waiting for transfers between devices: 0.01 us -> 1.7 us  [on_device(): far_theirs = lax.ppermute(far_mine, 'mp', swap)]
  transfers between devices with their start and end apart: 8 -> 8, of which waited for: 4 -> 6; matrix products, arithmetic and copies ran while one was open for 0% -> 0% of each run, Pallas kernels for 20% -> 23%
where the time goes in v2:
time: 84.6 us; the launch traced here: 84.2 us
  Pallas kernels  31.1 us (37%)
  waiting for transfers between devices  26.9 us (32%)
  starting transfers between devices  18.6 us (22%)
  local copies, waits for them, and re-layouts  7.08 us (8%)
    pallas_call x1, Pallas kernels, on_device(): pl.pallas_call(tail_kernel, out_shape=shape((rows, width), bf16), in_spec...  11.8 us
    ppermute x1, waiting for transfers between devices, on_device(): lax.ppermute(near_mine, 'tm', [(i, i + 1) for i in range(tm - 1)])  10.1 us
    unnamed x38, local copies, waits for them, and re-layouts  7.08 us
    ppermute x1, waiting for transfers between devices, on_device(): lax.ppermute(edge, ('tm', 'mp'), halo_pairs + [(b, a) for a, b in halo_pa...  6.17 us
    ppermute x1, waiting for transfers between devices, on_device(): near_theirs = lax.ppermute(near_mine, 'mp', swap)  5.11 us
    pallas_call x1, Pallas kernels, on_device(): pl.pallas_call(near_kernel, out_shape=partial, in_specs=[VMEM] * 8, out_s...  4.52 us
    pallas_call x1, Pallas kernels, on_device(): pl.pallas_call(far_kernel, out_shape=(shape((slab, local), bf16), shape((...  4.35 us
    ppermute x1, starting transfers between devices, on_device(): near_mine = lax.ppermute(sent, 'tm', [(i, i + 1) for i in range(tm - 1)])  3.4 us
  transfers between devices with their start and end apart: 8, of which 6 were waited for; matrix products, arithmetic and copies ran while one was open for 0% of the time, Pallas kernels for 23%

profile of v2, /device:TPU:256, one launch (start us, length us, event | category | flops | bytes accessed | tf_op | source)
XLA Modules:
  0.0 84.2 jit_solution(17253680909596972519)
XLA Ops:
  0.0 1.2 %copy-done = bf16[512,1024]{1,0:T(8,128)(2,1)S(1)} copy-done((bf16[512,1024]{1,0:T(8,128)(2,1)S(1)}, bf16[512,1024]{1,0:T(8,128)(2,1)}, u32[]{:S(2)}) %copy-start) | copy-done | bytes 1048600
  2.3 3.4 %collective-permute-start = (bf16[256,1024]{1,0:T(8,128)(2,1)S(1)}, bf16[256,1024]{1,0:T(8,128)(2,1)S(1)}, u32[]{:S(2)}, u32[]{:S(2)}) collective-permute-start(bf16[256,1024]{1,0:T(8,128)(2,1)S(1)} %send_norm.1), channel_id=1, source_target_pairs={{0,2},{2,4},{4,6},{6,8},{8,10},{10,12},{12,14},{14,16},{16,18},{18... | collective-permute-start | bytes 1572872 | tf_op jit(solution)/shard_map/ppermute | solution.py:426
  5.7 1.2 %copy-done.1 = bf16[512,1024]{1,0:T(8,128)(2,1)S(1)} copy-done((bf16[512,1024]{1,0:T(8,128)(2,1)S(1)}, bf16[512,1024]{1,0:T(8,128)(2,1)}, u32[]{:S(2)}) %copy-start.1) | copy-done | bytes 1048600
  6.9 1.9 %copy-done.3 = bf16[1024,3,512]{2,0,1:T(8,128)(2,1)S(1)} copy-done((bf16[1024,3,512]{2,0,1:T(8,128)(2,1)S(1)}, bf16[1024,3,512]{2,0,1:T(8,128)(2,1)}, u32[]{:S(2)}) %copy-start.3) | copy-done | bytes 3145752
  10.8 2.9 %own_qkv.1 = (bf16[3,512,512]{2,1,0:T(8,128)(2,1)S(1)}, f32[2,8,128]{2,1,0:T(8,128)S(1)}) custom-call(bf16[512,1024]{1,0:T(8,128)(2,1)S(1)} %copy-done.1, f32[1,1024]{1,0:T(1,128)S(1)} %bitcast.12, bf16[3,1024,512]{2,1,0:T(8,128)(2,1)S(1)} %bitcast.8, s32[1,128]{1,0:T(1,128)S(1)} %bitcast.13, s32[1,128]{1,0:T(1,128)S(1)} %bitcast.14), custom_call_target="tpu_custom_call" | custom-call | flops 1610612 | bytes 3145 | tf_op jit(solution)/shard_map/own_qkv/pallas_call | solution.py:427
  13.7 2.6 %own_attention.1 = (f32[512,512]{1,0:T(8,128)S(1)}, f32[512,512]{1,0:T(8,128)S(1)}, f32[512,512]{1,0:T(8,128)S(1)}) custom-call(bf16[3,512,512]{2,1,0:T(8,128)(2,1)S(1)} %get-tuple-element.34.qkv_ref, f32[2,8,128]{2,1,0:T(8,128)S(1)} %get-tuple-element.36.flags_ref), custom_call_target="tpu_custom_call" | custom-call | flops 1342177 | bytes 4194 | tf_op jit(solution)/shard_map/own_attention/pallas_call | solution.py:448
  16.3 2.1 %collective-permute-start.6 = (bf16[1024,2048]{1,0:T(8,128)(2,1)}, bf16[1024,2048]{1,0:T(8,128)(2,1)S(1)}, u32[]{:S(2)}, u32[]{:S(2)}) collective-permute-start(bf16[1024,2048]{1,0:T(8,128)(2,1)} %up_own_ref.1), channel_id=1, source_target_pairs={{0,1},{1,0},{2,3},{3,2},{4,5},{5,4},{6,7},{7,6},{8,9},{9,8},{10,11... | collective-permute-start | bytes 12582920 | tf_op jit(solution)/shard_map/ppermute | solution.py:458
  18.4 2.4 %collective-permute-start.7 = (bf16[2048,1024]{1,0:T(8,128)(2,1)}, bf16[2048,1024]{1,0:T(8,128)(2,1)S(1)}, u32[]{:S(2)}, u32[]{:S(2)}) collective-permute-start(bf16[2048,1024]{1,0:T(8,128)(2,1)} %down_own_ref.1), channel_id=1, source_target_pairs={{0,1},{1,0},{2,3},{3,2},{4,5},{5,4},{6,7},{7,6},{8,9},{9,8},{10,11... | collective-permute-start | bytes 12582920 | tf_op jit(solution)/shard_map/ppermute | solution.py:459
  20.8 2.5 %collective-permute-done.mine_ref = bf16[256,1024]{1,0:T(8,128)(2,1)S(1)} collective-permute-done((bf16[256,1024]{1,0:T(8,128)(2,1)S(1)}, bf16[256,1024]{1,0:T(8,128)(2,1)S(1)}, u32[]{:S(2)}, u32[]{:S(2)}) %collective-permute-start) | collective-permute-done | bytes 524320 | tf_op jit(solution)/shard_map/ppermute | solution.py:426
  23.3 1.9 %collective-permute-start.2 = (bf16[256,1024]{1,0:T(8,128)(2,1)S(1)}, bf16[256,1024]{1,0:T(8,128)(2,1)S(1)}, u32[]{:S(2)}, u32[]{:S(2)}) collective-permute-start(bf16[256,1024]{1,0:T(8,128)(2,1)S(1)} %collective-permute-done.mine_ref), channel_id=1, source_target_pairs={{0,1},{1,0},{2,3},{3,2},{4,5},{5,4},{6,7},{7,6},{8,9},{9,8},{10,11... | collective-permute-start | bytes 1572872 | tf_op jit(solution)/shard_map/ppermute | solution.py:462
  25.2 1.9 %collective-permute-start.1 = (bf16[256,1024]{1,0:T(8,128)(2,1)S(1)}, bf16[256,1024]{1,0:T(8,128)(2,1)S(1)}, u32[]{:S(2)}, u32[]{:S(2)}) collective-permute-start(bf16[256,1024]{1,0:T(8,128)(2,1)S(1)} %collective-permute-done.mine_ref), channel_id=1, source_target_pairs={{0,2},{2,4},{4,6},{6,8},{8,10},{10,12},{12,14},{14,16},{16,18},{18... | collective-permute-start | bytes 1572872 | tf_op jit(solution)/shard_map/ppermute | solution.py:461
  27.1 5.1 %collective-permute-done.2.theirs_ref = bf16[256,1024]{1,0:T(8,128)(2,1)S(1)} collective-permute-done((bf16[256,1024]{1,0:T(8,128)(2,1)S(1)}, bf16[256,1024]{1,0:T(8,128)(2,1)S(1)}, u32[]{:S(2)}, u32[]{:S(2)}) %collective-permute-start.2) | collective-permute-done | bytes 524320 | tf_op jit(solution)/shard_map/ppermute | solution.py:462
  32.3 4.5 %near_attention.1 = (f32[512,512]{1,0:T(8,128)S(1)}, f32[512,512]{1,0:T(8,128)S(1)}, f32[512,512]{1,0:T(8,128)S(1)}) custom-call(bf16[3,512,512]{2,1,0:T(8,128)(2,1)S(1)} %get-tuple-element.34.qkv_ref, bf16[256,1024]{1,0:T(8,128)(2,1)S(1)} %collective-permute-done.mine_ref, bf16[256,1024]{1,0:T(8,128)(2,1)S(1)} %collective-permute-done.2.theirs_ref, ...), custom_call_target="tpu_custom_call" | custom-call | flops 12884901888 | bytes 33554432 | tf_op jit(solution)/shard_map/near_attention/pallas_call | solution.py:463
  36.8 10.1 %collective-permute-done.1.mine_ref = bf16[256,1024]{1,0:T(8,128)(2,1)S(1)} collective-permute-done((bf16[256,1024]{1,0:T(8,128)(2,1)S(1)}, bf16[256,1024]{1,0:T(8,128)(2,1)S(1)}, u32[]{:S(2)}, u32[]{:S(2)}) %collective-permute-start.1) | collective-permute-done | bytes 524320 | tf_op jit(solution)/shard_map/ppermute | solution.py:461
  46.9 2.2 %collective-permute-start.3 = (bf16[256,1024]{1,0:T(8,128)(2,1)S(1)}, bf16[256,1024]{1,0:T(8,128)(2,1)S(1)}, u32[]{:S(2)}, u32[]{:S(2)}) collective-permute-start(bf16[256,1024]{1,0:T(8,128)(2,1)S(1)} %collective-permute-done.1.mine_ref), channel_id=1, source_target_pairs={{0,1},{1,0},{2,3},{3,2},{4,5},{5,4},{6,7},{7,6},{8,9},{9,8},{10,11... | collective-permute-start | bytes 1572872 | tf_op jit(solution)/shard_map/ppermute | solution.py:478
  49.1 1.7 %collective-permute-done.3.theirs_ref = bf16[256,1024]{1,0:T(8,128)(2,1)S(1)} collective-permute-done((bf16[256,1024]{1,0:T(8,128)(2,1)S(1)}, bf16[256,1024]{1,0:T(8,128)(2,1)S(1)}, u32[]{:S(2)}, u32[]{:S(2)}) %collective-permute-start.3) | collective-permute-done | bytes 524320 | tf_op jit(solution)/shard_map/ppermute | solution.py:478
  50.8 4.4 %far_attention.1 = (bf16[512,512]{1,0:T(8,128)(2,1)S(1)}, bf16[272,1024]{1,0:T(8,128)(2,1)S(1)}) custom-call(bf16[3,512,512]{2,1,0:T(8,128)(2,1)S(1)} %get-tuple-element.34.qkv_ref, bf16[256,1024]{1,0:T(8,128)(2,1)S(1)} %collective-permute-done.1.mine_ref, bf16[256,1024]{1,0:T(8,128)(2,1)S(1)} %collective-permute-done.3.theirs_ref, ...), custom_call_target="tpu_custom_call" | custom-call | flops 7516192768 | bytes 41943040 | tf_op jit(solution)/shard_map/far_attention/pallas_call | solution.py:479
  55.2 2.3 %collective-permute-start.4 = (bf16[272,1024]{1,0:T(8,128)(2,1)S(1)}, bf16[272,1024]{1,0:T(8,128)(2,1)S(1)}, u32[]{:S(2)}, u32[]{:S(2)}) collective-permute-start(bf16[272,1024]{1,0:T(8,128)(2,1)S(1)} %get-tuple-element.55), channel_id=1, source_target_pairs={{0,1},{1,0},{2,3},{3,2},{4,5},{5,4},{6,7},{7,6},{8,9},{9,8},{10,11... | collective-permute-start | bytes 1671176 | tf_op jit(solution)/shard_map/ppermute | solution.py:493
  58.0 1.3 %collective-permute-done.4.got_ref = bf16[272,1024]{1,0:T(8,128)(2,1)S(1)} collective-permute-done((bf16[272,1024]{1,0:T(8,128)(2,1)S(1)}, bf16[272,1024]{1,0:T(8,128)(2,1)S(1)}, u32[]{:S(2)}, u32[]{:S(2)}) %collective-permute-start.4) | collective-permute-done | bytes 557088 | tf_op jit(solution)/shard_map/ppermute | solution.py:493
  59.4 1.8 %gated_units.1 = (bf16[272,1024]{1,0:T(8,128)(2,1)S(1)}, bf16[16,1024]{1,0:T(8,128)(2,1)S(1)}, f32[256,1024]{1,0:T(8,128)S(1)}) custom-call(f32[272,1024]{1,0:T(8,128)S(1)} %out_projection.1.base_ref, bf16[272,1024]{1,0:T(8,128)(2,1)S(1)} %collective-permute-done.4.got_ref, f32[1,1024]{1,0:T(1,128)S(1)} %bitcast.15, bf16[1024,2048]{1,0:T(8,128)(2,1)S(1)} %copy-done.9), custom_call_target="tpu_custom_call" | custom-call | flops 4563402752 | bytes 20971520 | tf_op jit(solution)/shard_map/gated_units/pallas_call | solution.py:503
  61.2 2.4 %collective-permute-start.5 = (bf16[16,1024]{1,0:T(8,128)(2,1)S(1)}, bf16[16,1024]{1,0:T(8,128)(2,1)S(1)}, u32[]{:S(2)}, u32[]{:S(2)}) collective-permute-start(bf16[16,1024]{1,0:T(8,128)(2,1)S(1)} %get-tuple-element.57), channel_id=1, source_target_pairs={{1,2},{3,4},{5,6},{7,8},{9,10},{11,12},{13,14},{15,16},{17,18},{19... | collective-permute-start | bytes 98312 | tf_op jit(solution)/shard_map/ppermute | solution.py:518
  63.6 2.3 %depthwise.1.sum_ref = f32[256,1024]{1,0:T(8,128)S(1)} custom-call(bf16[272,1024]{1,0:T(8,128)(2,1)S(1)} %get-tuple-element.56.gated_ref, bf16[31,1024]{1,0:T(8,128)(2,1)S(1)} %copy-done.14, f32[2,8,128]{2,1,0:T(8,128)S(1)} %get-tuple-element.36.flags_ref), custom_call_target="tpu_custom_call" | custom-call | flops 1073741824 | bytes 4194304 | tf_op jit(solution)/shard_map/depthwise/pallas_call | solution.py:519
  66.0 6.2 %collective-permute-done.5.halo_ref = bf16[16,1024]{1,0:T(8,128)(2,1)S(1)} collective-permute-done((bf16[16,1024]{1,0:T(8,128)(2,1)S(1)}, bf16[16,1024]{1,0:T(8,128)(2,1)S(1)}, u32[]{:S(2)}, u32[]{:S(2)}) %collective-permute-start.5) | collective-permute-done | bytes 32800 | tf_op jit(solution)/shard_map/ppermute | solution.py:518
  72.2 11.8 %tail.1 = bf16[256,1024]{1,0:T(8,128)(2,1)} custom-call(f32[256,1024]{1,0:T(8,128)S(1)} %depthwise.1.sum_ref, bf16[16,1024]{1,0:T(8,128)(2,1)S(1)} %collective-permute-done.5.halo_ref, bf16[31,1024]{1,0:T(8,128)(2,1)S(1)} %copy-done.14, f32[2,8,128]{2,1,0:T(8,128)S(1)} %get-tuple-element.36.flags_ref, f32[256,1024]{1,0:T(8,128)S(1)} %get-tuple-element.58.first_ref, ...), custom_call_target="tpu_custom_call" | custom-call | flops 19327352832 | bytes 75497472 | tf_op jit(solution)/shard_map/tail/pallas_call | solution.py:532
  (39 shorter events, 3.6 us)
Async XLA Ops:
  0.0 1.2 %copy-start = (bf16[512,1024]{1,0:T(8,128)(2,1)S(1)}, bf16[512,1024]{1,0:T(8,128)(2,1)}, u32[]{:S(2)}) copy-start(bf16[512,1024]{1,0:T(8,128)(2,1)} %frames_ref.4) | copy-start | bytes 3145732
  1.2 0.7 copy-start.5
  2.3 21.0 %collective-permute-start = (bf16[256,1024]{1,0:T(8,128)(2,1)S(1)}, bf16[256,1024]{1,0:T(8,128)(2,1)S(1)}, u32[]{:S(2)}, u32[]{:S(2)}) collective-permute-start(bf16[256,1024]{1,0:T(8,128)(2,1)S(1)} %send_norm.1), channel_id=1, source_target_pairs={{0,2},{2,4},{4,6},{6,8},{8,10},{10,12},{12,14},{14,16},{16,18},{18... | collective-permute-start | bytes 1572872 | tf_op jit(solution)/shard_map/ppermute | solution.py:426
  5.7 1.2 %copy-start.1 = (bf16[512,1024]{1,0:T(8,128)(2,1)S(1)}, bf16[512,1024]{1,0:T(8,128)(2,1)}, u32[]{:S(2)}) copy-start(bf16[512,1024]{1,0:T(8,128)(2,1)} %frames_ref.4) | copy-start | bytes 3145732
  6.9 1.9 %copy-start.3 = (bf16[1024,3,512]{2,0,1:T(8,128)(2,1)S(1)}, bf16[1024,3,512]{2,0,1:T(8,128)(2,1)}, u32[]{:S(2)}) copy-start(bf16[1024,3,512]{2,0,1:T(8,128)(2,1)} %param.17) | copy-start | bytes 9437188
  10.8 21.4 %copy-start.4 = (bf16[1024,3,512]{2,0,1:T(8,128)(2,1)S(1)}, bf16[1024,3,512]{2,0,1:T(8,128)(2,1)}, u32[]{:S(2)}) copy-start(bf16[1024,3,512]{2,0,1:T(8,128)(2,1)} %param.17) | copy-start | bytes 9437188
  16.3 34.5 %copy-start.13 = (bf16[512,1024]{1,0:T(8,128)(2,1)S(1)}, bf16[512,1024]{1,0:T(8,128)(2,1)}, u32[]{:S(2)}) copy-start(bf16[512,1024]{1,0:T(8,128)(2,1)} %w_out_ref.3) | copy-start | bytes 3145732
  16.3 55.8 %collective-permute-start.6 = (bf16[1024,2048]{1,0:T(8,128)(2,1)}, bf16[1024,2048]{1,0:T(8,128)(2,1)S(1)}, u32[]{:S(2)}, u32[]{:S(2)}) collective-permute-start(bf16[1024,2048]{1,0:T(8,128)(2,1)} %up_own_ref.1), channel_id=1, source_target_pairs={{0,1},{1,0},{2,3},{3,2},{4,5},{5,4},{6,7},{7,6},{8,9},{9,8},{10,11... | collective-permute-start | bytes 12582920 | tf_op jit(solution)/shard_map/ppermute | solution.py:458
  18.4 53.8 %collective-permute-start.7 = (bf16[2048,1024]{1,0:T(8,128)(2,1)}, bf16[2048,1024]{1,0:T(8,128)(2,1)S(1)}, u32[]{:S(2)}, u32[]{:S(2)}) collective-permute-start(bf16[2048,1024]{1,0:T(8,128)(2,1)} %down_own_ref.1), channel_id=1, source_target_pairs={{0,1},{1,0},{2,3},{3,2},{4,5},{5,4},{6,7},{7,6},{8,9},{9,8},{10,11... | collective-permute-start | bytes 12582920 | tf_op jit(solution)/shard_map/ppermute | solution.py:459
  23.3 9.0 %collective-permute-start.2 = (bf16[256,1024]{1,0:T(8,128)(2,1)S(1)}, bf16[256,1024]{1,0:T(8,128)(2,1)S(1)}, u32[]{:S(2)}, u32[]{:S(2)}) collective-permute-start(bf16[256,1024]{1,0:T(8,128)(2,1)S(1)} %collective-permute-done.mine_ref), channel_id=1, source_target_pairs={{0,1},{1,0},{2,3},{3,2},{4,5},{5,4},{6,7},{7,6},{8,9},{9,8},{10,11... | collective-permute-start | bytes 1572872 | tf_op jit(solution)/shard_map/ppermute | solution.py:462
  25.2 21.6 %collective-permute-start.1 = (bf16[256,1024]{1,0:T(8,128)(2,1)S(1)}, bf16[256,1024]{1,0:T(8,128)(2,1)S(1)}, u32[]{:S(2)}, u32[]{:S(2)}) collective-permute-start(bf16[256,1024]{1,0:T(8,128)(2,1)S(1)} %collective-permute-done.mine_ref), channel_id=1, source_target_pairs={{0,2},{2,4},{4,6},{6,8},{8,10},{10,12},{12,14},{14,16},{16,18},{18... | collective-permute-start | bytes 1572872 | tf_op jit(solution)/shard_map/ppermute | solution.py:461
  46.9 10.6 %copy-start.2 = (bf16[512,1024]{1,0:T(8,128)(2,1)S(1)}, bf16[512,1024]{1,0:T(8,128)(2,1)}, u32[]{:S(2)}) copy-start(bf16[512,1024]{1,0:T(8,128)(2,1)} %frames_ref.4) | copy-start | bytes 3145732
  46.9 3.9 %collective-permute-start.3 = (bf16[256,1024]{1,0:T(8,128)(2,1)S(1)}, bf16[256,1024]{1,0:T(8,128)(2,1)S(1)}, u32[]{:S(2)}, u32[]{:S(2)}) collective-permute-start(bf16[256,1024]{1,0:T(8,128)(2,1)S(1)} %collective-permute-done.1.mine_ref), channel_id=1, source_target_pairs={{0,1},{1,0},{2,3},{3,2},{4,5},{5,4},{6,7},{7,6},{8,9},{9,8},{10,11... | collective-permute-start | bytes 1572872 | tf_op jit(solution)/shard_map/ppermute | solution.py:478
  55.2 4.1 %copy-start.9 = (bf16[1024,2048]{1,0:T(8,128)(2,1)S(1)}, bf16[1024,2048]{1,0:T(8,128)(2,1)}, u32[]{:S(2)}) copy-start(bf16[1024,2048]{1,0:T(8,128)(2,1)} %w_ref.1) | copy-start | bytes 12582916
  55.2 4.1 %copy-start.15 = (f32[1024]{0:T(1024)S(1)}, f32[1024]{0:T(1024)}, u32[]{:S(2)}) copy-start(f32[1024]{0:T(1024)} %param.19) | copy-start | bytes 12292
  55.2 4.1 %collective-permute-start.4 = (bf16[272,1024]{1,0:T(8,128)(2,1)S(1)}, bf16[272,1024]{1,0:T(8,128)(2,1)S(1)}, u32[]{:S(2)}, u32[]{:S(2)}) collective-permute-start(bf16[272,1024]{1,0:T(8,128)(2,1)S(1)} %get-tuple-element.55), channel_id=1, source_target_pairs={{0,1},{1,0},{2,3},{3,2},{4,5},{5,4},{6,7},{7,6},{8,9},{9,8},{10,11... | collective-permute-start | bytes 1671176 | tf_op jit(solution)/shard_map/ppermute | solution.py:493
  59.3 4.3 %copy-start.14 = (bf16[31,1024]{1,0:T(8,128)(2,1)S(1)}, bf16[31,1024]{1,0:T(8,128)(2,1)}, u32[]{:S(2)}) copy-start(bf16[31,1024]{1,0:T(8,128)(2,1)} %taps_ref.3) | copy-start | bytes 190468
  59.3 12.8 %copy-start.10 = (bf16[1024,2048]{1,0:T(8,128)(2,1)S(1)}, bf16[1024,2048]{1,0:T(8,128)(2,1)}, u32[]{:S(2)}) copy-start(bf16[1024,2048]{1,0:T(8,128)(2,1)} %up_own_ref.1) | copy-start | bytes 12582916
  59.3 12.8 %copy-start.11 = (bf16[2048,1024]{1,0:T(8,128)(2,1)S(1)}, bf16[2048,1024]{1,0:T(8,128)(2,1)}, u32[]{:S(2)}) copy-start(bf16[2048,1024]{1,0:T(8,128)(2,1)} %down_own_ref.1) | copy-start | bytes 12582916
  59.3 12.8 %copy-start.12 = (bf16[1024,1024]{1,0:T(8,128)(2,1)S(1)}, bf16[1024,1024]{1,0:T(8,128)(2,1)}, u32[]{:S(2)}) copy-start(bf16[1024,1024]{1,0:T(8,128)(2,1)} %w_point_ref.1) | copy-start | bytes 6291460
  59.3 12.8 %copy-start.16 = (f32[1024]{0:T(1024)S(1)}, f32[1024]{0:T(1024)}, u32[]{:S(2)}) copy-start(f32[1024]{0:T(1024)} %param.22) | copy-start | bytes 12292
  59.3 12.8 %copy-start.17 = (f32[1024]{0:T(1024)S(1)}, f32[1024]{0:T(1024)}, u32[]{:S(2)}) copy-start(f32[1024]{0:T(1024)} %param.24) | copy-start | bytes 12292
  59.4 12.8 %copy-start.18 = (f32[1024]{0:T(1024)S(1)}, f32[1024]{0:T(1024)}, u32[]{:S(2)}) copy-start(f32[1024]{0:T(1024)} %param.27) | copy-start | bytes 12292
  61.2 10.9 %collective-permute-start.5 = (bf16[16,1024]{1,0:T(8,128)(2,1)S(1)}, bf16[16,1024]{1,0:T(8,128)(2,1)S(1)}, u32[]{:S(2)}, u32[]{:S(2)}) collective-permute-start(bf16[16,1024]{1,0:T(8,128)(2,1)S(1)} %get-tuple-element.57), channel_id=1, source_target_pairs={{1,2},{3,4},{5,6},{7,8},{9,10},{11,12},{13,14},{15,16},{17,18},{19... | collective-permute-start | bytes 98312 | tf_op jit(solution)/shard_map/ppermute | solution.py:518
  (3 other events, 2.0 us)

commit v3 on v2

--- a/solution.py
+++ b/solution.py
@@ -14,6 +14,7 @@
 MIB = 1 << 20
 EARLY = 0.001
 LATE = 4.0
+MIDDLE = 4.0
 VMEM = pl.BlockSpec(memory_space=pltpu.VMEM)
 HBM = pl.BlockSpec(memory_space=pltpu.HBM)
 
@@ -43,36 +44,25 @@
         body(slice(first, first + step))
 
 
-def send_kernel(frames_ref, gain_ref, out_ref, held, gain, sem):
-    rows = out_ref.shape[0]
+def send_kernel(frames_ref, gain_ref, sent_ref, normed_ref):
+    rows = sent_ref.shape[0]
+
+    def body(part):
+        normed_ref[part] = norm_rows(
+            frames_ref[part].astype(jnp.float32), gain_ref[...]
+        ).astype(jnp.bfloat16)
+
+    each(normed_ref.shape[0], 16, body)
     first = pl.multiple_of(lax.axis_index("mp") * rows, rows)
-    copies = [
-        pltpu.make_async_copy(gain_ref, gain, sem.at[0]),
-        pltpu.make_async_copy(frames_ref.at[pl.ds(first, rows)], held, sem.at[1]),
-    ]
-    for copy in copies:
-        copy.start()
-    for copy in copies:
-        copy.wait()
-
-    def body(part):
-        out_ref[part] = norm_rows(held[part].astype(jnp.float32), gain[...]).astype(jnp.bfloat16)
-
-    each(rows, 16, body)
-
-
-def own_kernel(frames_ref, gain_ref, w_ref, lengths_ref, context_ref, qkv_ref, flags_ref, normed):
-    rows = frames_ref.shape[0]
+    sent_ref[...] = normed_ref[pl.ds(first, rows)]
+
+
+def own_kernel(normed_ref, w_ref, lengths_ref, context_ref, qkv_ref, flags_ref):
+    rows = normed_ref.shape[0]
     step = pl.program_id(0)
 
     @pl.when(step == 0)
     def _():
-        def body(part):
-            normed[part] = norm_rows(
-                frames_ref[part].astype(jnp.float32), gain_ref[...]
-            ).astype(jnp.bfloat16)
-
-        each(rows, 16, body)
         count = lengths_ref.shape[1]
         lengths = jnp.broadcast_to(lengths_ref[...], (8, count))
         before = (
@@ -101,7 +91,7 @@
 
     scale = jnp.where(step == 0, HD**-0.5, 1.0)
     qkv_ref[0] = (
-        jnp.dot(normed[...], w_ref[0], preferred_element_type=jnp.float32) * scale
+        jnp.dot(normed_ref[...], w_ref[0], preferred_element_type=jnp.float32) * scale
     ).astype(jnp.bfloat16)
 
 
@@ -111,28 +101,43 @@
     )
 
 
+def attend_all(queries, keys, values, biases):
+    first_head = lax.broadcasted_iota(jnp.int32, (C, LANES), 1) < HD
+    zero = jnp.zeros_like(queries[0])
+    stacked = []
+    for query in queries:
+        stacked += [jnp.where(first_head, query, zero), jnp.where(first_head, zero, query)]
+    scores = lax.dot_general(
+        jnp.concatenate(stacked, axis=0),
+        keys,
+        (((1,), (1,)), ((), ())),
+        preferred_element_type=jnp.float32,
+    )
+    raised, tops = [], []
+    for i, bias in enumerate(biases):
+        part = scores[2 * i * C : 2 * (i + 1) * C] + bias
+        highest = jnp.max(part, axis=1, keepdims=True)
+        raised.append(jnp.exp(part - highest).astype(jnp.bfloat16))
+        tops.append(highest)
+    wide = jnp.concatenate([values, jnp.ones_like(values)], axis=1)
+    mixed = jnp.dot(jnp.concatenate(raised, axis=0), wide, preferred_element_type=jnp.float32)
+    found = []
+    for i, highest in enumerate(tops):
+        one = mixed[2 * i * C : (2 * i + 1) * C]
+        two = mixed[(2 * i + 1) * C : 2 * (i + 1) * C]
+        total = jnp.where(first_head, one[:, :LANES], two[:, :LANES])
+        weight = jnp.where(first_head, one[:, LANES:], two[:, LANES:])
+        top = jnp.where(
+            first_head,
+            jnp.broadcast_to(highest[:C], (C, LANES)),
+            jnp.broadcast_to(highest[C:], (C, LANES)),
+        )
+        found.append((total, top, weight))
+    return found
+
+
 def attend(query, keys, values, bias):
-    first_head = lax.broadcasted_iota(jnp.int32, (C, LANES), 1) < HD
-    zero = jnp.zeros_like(query)
-    both = jnp.concatenate(
-        [jnp.where(first_head, query, zero), jnp.where(first_head, zero, query)], axis=0
-    )
-    scores = lax.dot_general(
-        both, keys, (((1,), (1,)), ((), ())), preferred_element_type=jnp.float32
-    )
-    scores = scores + bias
-    highest = jnp.max(scores, axis=1, keepdims=True)
-    raised = jnp.exp(scores - highest).astype(jnp.bfloat16)
-    wide = jnp.concatenate([values, jnp.ones_like(values)], axis=1)
-    mixed = jnp.dot(raised, wide, preferred_element_type=jnp.float32)
-    total = jnp.where(first_head, mixed[:C, :LANES], mixed[C:, :LANES])
-    weight = jnp.where(first_head, mixed[:C, LANES:], mixed[C:, LANES:])
-    top = jnp.where(
-        first_head,
-        jnp.broadcast_to(highest[:C], (C, LANES)),
-        jnp.broadcast_to(highest[C:], (C, LANES)),
-    )
-    return total, top, weight
+    return attend_all([query], keys, values, [bias])[0]
 
 
 def place(normed, mine_ref, theirs_ref):
@@ -185,15 +190,18 @@
         jnp.bfloat16
     )
     first = lax.axis_index("tm") * count - count
-    for i in range(count):
-        rows = slice(i * C, (i + 1) * C)
-        lowest = flags_ref[0, 2 + i : 3 + i, :]
-        bias = bias_row(lowest, [(first + n).astype(jnp.float32) for n in range(count)])
-        for pair in range(width // LANES):
-            cols = slice(pair * LANES, (pair + 1) * LANES)
+    every = [slice(i * C, (i + 1) * C) for i in range(count)]
+    seen = [(first + n).astype(jnp.float32) for n in range(count)]
+    biases = [bias_row(flags_ref[0, 2 + i : 3 + i, :], seen) for i in range(count)]
+    for pair in range(width // LANES):
+        cols = slice(pair * LANES, (pair + 1) * LANES)
+        found = attend_all(
+            [qkv_ref[0, rows, cols] for rows in every], keys[:, cols], values[:, cols], biases
+        )
+        for rows, part in zip(every, found):
             parts = own_total_ref[rows, cols], own_top_ref[rows, cols], own_weight_ref[rows, cols]
             total_ref[rows, cols], top_ref[rows, cols], weight_ref[rows, cols] = merged(
-                parts, *attend(qkv_ref[0, rows, cols], keys[:, cols], values[:, cols], bias)
+                parts, *part
             )
 
 
@@ -304,23 +312,12 @@
     sum_ref, halo_ref, taps_ref, flags_ref, first_ref, gain_depth_ref, gain_ffn_ref, gain_final_ref,
     w_point_ref, up_own_ref, up_other_ref, down_own_ref, down_other_ref,
     out_ref,
-    down, around, depth, normed, second, hidden, feed, down_sem,
+    around, depth, normed, second, hidden, feed,
 ):
     rows, width = sum_ref.shape
     half = (taps_ref.shape[0] - 1) // 2
     units = up_own_ref.shape[1]
     step = 512
-    down_copies = []
-    for part in range(width // 256):
-        for group, ref in enumerate((down_own_ref, down_other_ref)):
-            copy = pltpu.make_async_copy(
-                ref.at[:, part * 256 : (part + 1) * 256],
-                down.at[group, :, part * 256 : (part + 1) * 256],
-                down_sem.at[group, part],
-            )
-            copy.start()
-            down_copies.append(copy)
-
     core = lax.axis_index("mp")
     at = 2 + 3 * core
     same = jnp.where(
@@ -364,10 +361,9 @@
     for part in range(width // 256):
         cols = slice(part * 256, (part + 1) * 256)
         total = 0.0
-        for group in range(2):
-            down_copies[2 * part + group].wait()
+        for group, ref in enumerate((down_own_ref, down_other_ref)):
             total = total + jnp.dot(
-                hidden[group], down[group, :, cols], preferred_element_type=jnp.float32
+                hidden[group], ref[:, cols], preferred_element_type=jnp.float32
             ).astype(jnp.bfloat16).astype(jnp.float32)
         feed[:, cols] = second[:, cols] + 0.5 * total
 
@@ -408,21 +404,15 @@
         return vec.reshape(1, -1)
 
     w_planes = jnp.transpose(w_qkv, (1, 0, 2))
-    sent = pl.pallas_call(
+    sent, normed = pl.pallas_call(
         send_kernel,
-        out_shape=shape((rows, width), bf16),
-        in_specs=[HBM, HBM],
-        out_specs=VMEM,
-        scratch_shapes=[
-            pltpu.VMEM((rows, width), bf16),
-            pltpu.VMEM((1, width), f32),
-            pltpu.SemaphoreType.DMA((2,)),
-        ],
+        out_shape=(shape((rows, width), bf16), shape((slab, width), bf16)),
+        in_specs=[VMEM] * 2,
+        out_specs=(VMEM,) * 2,
         compiler_params=params(8),
         cost_estimate=cost(0, 2 * rows * width * 2),
         name="send_norm",
     )(frames, row(gain_attn))
-    own_frames, sent = lax.optimization_barrier((frames, sent))
     near_mine = lax.ppermute(sent, "tm", [(i, i + 1) for i in range(tm - 1)])
     qkv, flags = pl.pallas_call(
         own_kernel,
@@ -430,7 +420,6 @@
         out_shape=(shape((3, slab, local), bf16), shape((2, 8, LANES), f32)),
         in_specs=[
             pl.BlockSpec((slab, width), lambda i: (0, 0)),
-            pl.BlockSpec((1, width), lambda i: (0, 0)),
             pl.BlockSpec((1, width, local), lambda i: (i, 0, 0)),
             pl.BlockSpec((1, lengths.shape[0]), lambda i: (0, 0)),
             pl.BlockSpec((1, lengths.shape[0]), lambda i: (0, 0)),
@@ -439,11 +428,10 @@
             pl.BlockSpec((1, slab, local), lambda i: (i, 0, 0)),
             pl.BlockSpec((2, 8, LANES), lambda i: (0, 0, 0)),
         ),
-        scratch_shapes=[pltpu.VMEM((slab, width), bf16)],
         compiler_params=params(16),
         cost_estimate=cost(slab * width * 3 * local, width * 3 * local * 2, EARLY),
         name="own_qkv",
-    )(own_frames, row(gain_attn), w_planes, row(lengths), row(context))
+    )(normed, w_planes, row(lengths), row(context))
     partial = (shape((slab, local), f32),) * 3
     own_parts = pl.pallas_call(
         self_kernel,
@@ -471,7 +459,7 @@
             pltpu.VMEM((slab, local), bf16),
         ],
         compiler_params=params(16),
-        cost_estimate=cost(slab * width * 2 * local + 8 * slab * slab * local, 8 * MIB, LATE),
+        cost_estimate=cost(slab * width * 2 * local + 8 * slab * slab * local, 8 * MIB, MIDDLE),
         name="near_attention",
     )(qkv, near_mine, near_theirs, w_planes, flags, *own_parts)
     far_mine, near_parts = lax.optimization_barrier((far_mine, near_parts))
@@ -532,19 +520,17 @@
     return pl.pallas_call(
         tail_kernel,
         out_shape=shape((rows, width), bf16),
-        in_specs=[VMEM] * 11 + [HBM] * 2,
+        in_specs=[VMEM] * 13,
         out_specs=VMEM,
         scratch_shapes=[
-            pltpu.VMEM((2, units, width), bf16),
             pltpu.VMEM((width // LANES, 3 * EDGE, LANES), f32),
             pltpu.VMEM((rows, width), f32),
             pltpu.VMEM((rows, width), bf16),
             pltpu.VMEM((rows, width), f32),
             pltpu.VMEM((2, rows, units), bf16),
             pltpu.VMEM((rows, width), f32),
-            pltpu.SemaphoreType.DMA((2, width // 256)),
         ],
-        compiler_params=params(20),
+        compiler_params=params(12),
         cost_estimate=cost(rows * width * 9 * width, 18 * MIB, LATE),
         name="tail",
     )(

time: 84.6 us -> 80.2 us (0.948)
  Pallas kernels: 31.1 us -> 26.5 us
  waiting for transfers between devices: 26.9 us -> 29.2 us
  local copies, waits for them, and re-layouts: 7.08 us -> 5.17 us
    pallas_call x1, Pallas kernels: 11.8 us -> 7.2 us  [on_device(): pl.pallas_call(tail_kernel, out_shape=shape((rows, width), bf16), in_spec...]
    ppermute x1, waiting for transfers between devices: 2.5 us -> 4.91 us  [on_device(): near_mine = lax.ppermute(sent, 'tm', [(i, i + 1) for i in range(tm - 1)])]
    ppermute x1, waiting for transfers between devices: 5.11 us -> 2.7 us  [on_device(): near_theirs = lax.ppermute(near_mine, 'mp', swap)]
    ppermute x1, waiting for transfers between devices: 10.1 us -> 12.4 us  [on_device(): lax.ppermute(near_mine, 'tm', [(i, i + 1) for i in range(tm - 1)])]
    unnamed x38 -> x34, local copies, waits for them, and re-layouts: 7.08 us -> 5.17 us
where the time goes in v3:
time: 80.2 us; the launch traced here: 79.8 us
  waiting for transfers between devices  29.2 us (36%)
  Pallas kernels  26.5 us (33%)
  starting transfers between devices  18.6 us (23%)
  local copies, waits for them, and re-layouts  5.17 us (6%)
    ppermute x1, waiting for transfers between devices, on_device(): lax.ppermute(near_mine, 'tm', [(i, i + 1) for i in range(tm - 1)])  12.4 us
    pallas_call x1, Pallas kernels, on_device(): pl.pallas_call(tail_kernel, out_shape=shape((rows, width), bf16), in_spec...  7.2 us
    ppermute x1, waiting for transfers between devices, on_device(): lax.ppermute(edge, ('tm', 'mp'), halo_pairs + [(b, a) for a, b in halo_pa...  6.17 us
    unnamed x34, local copies, waits for them, and re-layouts  5.17 us
    ppermute x1, waiting for transfers between devices, on_device(): near_mine = lax.ppermute(sent, 'tm', [(i, i + 1) for i in range(tm - 1)])  4.91 us
    pallas_call x1, Pallas kernels, on_device(): pl.pallas_call(near_kernel, out_shape=partial, in_specs=[VMEM] * 8, out_s...  4.57 us
    pallas_call x1, Pallas kernels, on_device(): pl.pallas_call(far_kernel, out_shape=(shape((slab, local), bf16), shape((...  4.38 us
    ppermute x1, starting transfers between devices, on_device(): near_mine = lax.ppermute(sent, 'tm', [(i, i + 1) for i in range(tm - 1)])  3.4 us
  transfers between devices with their start and end apart: 8, of which 6 were waited for; matrix products, arithmetic and copies ran while one was open for 0% of the time, Pallas kernels for 23%

profile of v3, /device:TPU:256, one launch (start us, length us, event | category | flops | bytes accessed | tf_op | source)
XLA Modules:
  0.0 79.8 jit_solution(13432129125868849369)
XLA Ops:
  0.0 1.2 %copy-done.2 = bf16[512,1024]{1,0:T(8,128)(2,1)S(1)} copy-done((bf16[512,1024]{1,0:T(8,128)(2,1)S(1)}, bf16[512,1024]{1,0:T(8,128)(2,1)}, u32[]{:S(2)}) %copy-start.2) | copy-done | bytes 1048600
  1.9 0.7 send_norm.1
  2.7 3.4 %collective-permute-start = (bf16[256,1024]{1,0:T(8,128)(2,1)S(1)}, bf16[256,1024]{1,0:T(8,128)(2,1)S(1)}, u32[]{:S(2)}, u32[]{:S(2)}) collective-permute-start(bf16[256,1024]{1,0:T(8,128)(2,1)S(1)} %get-tuple-element.35), channel_id=1, source_target_pairs={{0,2},{2,4},{4,6},{6,8},{8,10},{10,12},{12,14},{14,16},{16,18},{18... | collective-permute-start | bytes 1572872 | tf_op jit(solution)/shard_map/ppermute | solution.py:416
  6.1 1.9 %copy-done = bf16[1024,3,512]{2,0,1:T(8,128)(2,1)S(1)} copy-done((bf16[1024,3,512]{2,0,1:T(8,128)(2,1)S(1)}, bf16[1024,3,512]{2,0,1:T(8,128)(2,1)}, u32[]{:S(2)}) %copy-start) | copy-done | bytes 3145752
  9.3 2.4 %own_qkv.1 = (bf16[3,512,512]{2,1,0:T(8,128)(2,1)S(1)}, f32[2,8,128]{2,1,0:T(8,128)S(1)}) custom-call(bf16[512,1024]{1,0:T(8,128)(2,1)S(1)} %get-tuple-element.33.normed_ref, bf16[3,1024,512]{2,1,0:T(8,128)(2,1)S(1)} %bitcast.8, s32[1,128]{1,0:T(1,128)S(1)} %bitcast.12, s32[1,128]{1,0:T(1,128)S(1)} %bitcast.13), custom_call_target="tpu_custom_call" | custom-call | flops 1610612 | bytes 3145 | tf_op jit(solution)/shard_map/own_qkv/pallas_call | solution.py:417
  11.6 2.6 %own_attention.1 = (f32[512,512]{1,0:T(8,128)S(1)}, f32[512,512]{1,0:T(8,128)S(1)}, f32[512,512]{1,0:T(8,128)S(1)}) custom-call(bf16[3,512,512]{2,1,0:T(8,128)(2,1)S(1)} %get-tuple-element.34.qkv_ref, f32[2,8,128]{2,1,0:T(8,128)S(1)} %get-tuple-element.36.flags_ref), custom_call_target="tpu_custom_call" | custom-call | flops 1342177 | bytes 4194 | tf_op jit(solution)/shard_map/own_attention/pallas_call | solution.py:436
  14.3 2.1 %collective-permute-start.6 = (bf16[1024,2048]{1,0:T(8,128)(2,1)}, bf16[1024,2048]{1,0:T(8,128)(2,1)S(1)}, u32[]{:S(2)}, u32[]{:S(2)}) collective-permute-start(bf16[1024,2048]{1,0:T(8,128)(2,1)} %up_own_ref.1), channel_id=1, source_target_pairs={{0,1},{1,0},{2,3},{3,2},{4,5},{5,4},{6,7},{7,6},{8,9},{9,8},{10,11... | collective-permute-start | bytes 12582920 | tf_op jit(solution)/shard_map/ppermute | solution.py:446
  16.3 2.4 %collective-permute-start.7 = (bf16[2048,1024]{1,0:T(8,128)(2,1)}, bf16[2048,1024]{1,0:T(8,128)(2,1)S(1)}, u32[]{:S(2)}, u32[]{:S(2)}) collective-permute-start(bf16[2048,1024]{1,0:T(8,128)(2,1)} %down_own_ref.1), channel_id=1, source_target_pairs={{0,1},{1,0},{2,3},{3,2},{4,5},{5,4},{6,7},{7,6},{8,9},{9,8},{10,11... | collective-permute-start | bytes 12582920 | tf_op jit(solution)/shard_map/ppermute | solution.py:447
  18.7 4.9 %collective-permute-done.mine_ref = bf16[256,1024]{1,0:T(8,128)(2,1)S(1)} collective-permute-done((bf16[256,1024]{1,0:T(8,128)(2,1)S(1)}, bf16[256,1024]{1,0:T(8,128)(2,1)S(1)}, u32[]{:S(2)}, u32[]{:S(2)}) %collective-permute-start) | collective-permute-done | bytes 524320 | tf_op jit(solution)/shard_map/ppermute | solution.py:416
  23.7 1.9 %collective-permute-start.2 = (bf16[256,1024]{1,0:T(8,128)(2,1)S(1)}, bf16[256,1024]{1,0:T(8,128)(2,1)S(1)}, u32[]{:S(2)}, u32[]{:S(2)}) collective-permute-start(bf16[256,1024]{1,0:T(8,128)(2,1)S(1)} %collective-permute-done.mine_ref), channel_id=1, source_target_pairs={{0,1},{1,0},{2,3},{3,2},{4,5},{5,4},{6,7},{7,6},{8,9},{9,8},{10,11... | collective-permute-start | bytes 1572872 | tf_op jit(solution)/shard_map/ppermute | solution.py:450
  25.6 1.9 %collective-permute-start.1 = (bf16[256,1024]{1,0:T(8,128)(2,1)S(1)}, bf16[256,1024]{1,0:T(8,128)(2,1)S(1)}, u32[]{:S(2)}, u32[]{:S(2)}) collective-permute-start(bf16[256,1024]{1,0:T(8,128)(2,1)S(1)} %collective-permute-done.mine_ref), channel_id=1, source_target_pairs={{0,2},{2,4},{4,6},{6,8},{8,10},{10,12},{12,14},{14,16},{16,18},{18... | collective-permute-start | bytes 1572872 | tf_op jit(solution)/shard_map/ppermute | solution.py:449
  27.5 2.7 %collective-permute-done.2.theirs_ref = bf16[256,1024]{1,0:T(8,128)(2,1)S(1)} collective-permute-done((bf16[256,1024]{1,0:T(8,128)(2,1)S(1)}, bf16[256,1024]{1,0:T(8,128)(2,1)S(1)}, u32[]{:S(2)}, u32[]{:S(2)}) %collective-permute-start.2) | collective-permute-done | bytes 524320 | tf_op jit(solution)/shard_map/ppermute | solution.py:450
  30.2 4.6 %near_attention.1 = (f32[512,512]{1,0:T(8,128)S(1)}, f32[512,512]{1,0:T(8,128)S(1)}, f32[512,512]{1,0:T(8,128)S(1)}) custom-call(bf16[3,512,512]{2,1,0:T(8,128)(2,1)S(1)} %get-tuple-element.34.qkv_ref, bf16[256,1024]{1,0:T(8,128)(2,1)S(1)} %collective-permute-done.mine_ref, bf16[256,1024]{1,0:T(8,128)(2,1)S(1)} %collective-permute-done.2.theirs_ref, ...), custom_call_target="tpu_custom_call" | custom-call | flops 12884901888 | bytes 33554432 | tf_op jit(solution)/shard_map/near_attention/pallas_call | solution.py:451
  34.8 12.4 %collective-permute-done.1.mine_ref = bf16[256,1024]{1,0:T(8,128)(2,1)S(1)} collective-permute-done((bf16[256,1024]{1,0:T(8,128)(2,1)S(1)}, bf16[256,1024]{1,0:T(8,128)(2,1)S(1)}, u32[]{:S(2)}, u32[]{:S(2)}) %collective-permute-start.1) | collective-permute-done | bytes 524320 | tf_op jit(solution)/shard_map/ppermute | solution.py:449
  47.2 2.2 %collective-permute-start.3 = (bf16[256,1024]{1,0:T(8,128)(2,1)S(1)}, bf16[256,1024]{1,0:T(8,128)(2,1)S(1)}, u32[]{:S(2)}, u32[]{:S(2)}) collective-permute-start(bf16[256,1024]{1,0:T(8,128)(2,1)S(1)} %collective-permute-done.1.mine_ref), channel_id=1, source_target_pairs={{0,1},{1,0},{2,3},{3,2},{4,5},{5,4},{6,7},{7,6},{8,9},{9,8},{10,11... | collective-permute-start | bytes 1572872 | tf_op jit(solution)/shard_map/ppermute | solution.py:466
  49.4 1.7 %collective-permute-done.3.theirs_ref = bf16[256,1024]{1,0:T(8,128)(2,1)S(1)} collective-permute-done((bf16[256,1024]{1,0:T(8,128)(2,1)S(1)}, bf16[256,1024]{1,0:T(8,128)(2,1)S(1)}, u32[]{:S(2)}, u32[]{:S(2)}) %collective-permute-start.3) | collective-permute-done | bytes 524320 | tf_op jit(solution)/shard_map/ppermute | solution.py:466
  51.1 4.4 %far_attention.1 = (bf16[512,512]{1,0:T(8,128)(2,1)S(1)}, bf16[272,1024]{1,0:T(8,128)(2,1)S(1)}) custom-call(bf16[3,512,512]{2,1,0:T(8,128)(2,1)S(1)} %get-tuple-element.34.qkv_ref, bf16[256,1024]{1,0:T(8,128)(2,1)S(1)} %collective-permute-done.1.mine_ref, bf16[256,1024]{1,0:T(8,128)(2,1)S(1)} %collective-permute-done.3.theirs_ref, ...), custom_call_target="tpu_custom_call" | custom-call | flops 7516192768 | bytes 41943040 | tf_op jit(solution)/shard_map/far_attention/pallas_call | solution.py:467
  55.6 2.3 %collective-permute-start.4 = (bf16[272,1024]{1,0:T(8,128)(2,1)S(1)}, bf16[272,1024]{1,0:T(8,128)(2,1)S(1)}, u32[]{:S(2)}, u32[]{:S(2)}) collective-permute-start(bf16[272,1024]{1,0:T(8,128)(2,1)S(1)} %get-tuple-element.55), channel_id=1, source_target_pairs={{0,1},{1,0},{2,3},{3,2},{4,5},{5,4},{6,7},{7,6},{8,9},{9,8},{10,11... | collective-permute-start | bytes 1671176 | tf_op jit(solution)/shard_map/ppermute | solution.py:481
  58.4 1.3 %collective-permute-done.4.got_ref = bf16[272,1024]{1,0:T(8,128)(2,1)S(1)} collective-permute-done((bf16[272,1024]{1,0:T(8,128)(2,1)S(1)}, bf16[272,1024]{1,0:T(8,128)(2,1)S(1)}, u32[]{:S(2)}, u32[]{:S(2)}) %collective-permute-start.4) | collective-permute-done | bytes 557088 | tf_op jit(solution)/shard_map/ppermute | solution.py:481
  59.8 1.8 %gated_units.1 = (bf16[272,1024]{1,0:T(8,128)(2,1)S(1)}, bf16[16,1024]{1,0:T(8,128)(2,1)S(1)}, f32[256,1024]{1,0:T(8,128)S(1)}) custom-call(f32[272,1024]{1,0:T(8,128)S(1)} %out_projection.1.base_ref, bf16[272,1024]{1,0:T(8,128)(2,1)S(1)} %collective-permute-done.4.got_ref, f32[1,1024]{1,0:T(1,128)S(1)} %bitcast.14, bf16[1024,2048]{1,0:T(8,128)(2,1)S(1)} %copy-done.7), custom_call_target="tpu_custom_call" | custom-call | flops 4563402752 | bytes 20971520 | tf_op jit(solution)/shard_map/gated_units/pallas_call | solution.py:491
  61.6 2.4 %collective-permute-start.5 = (bf16[16,1024]{1,0:T(8,128)(2,1)S(1)}, bf16[16,1024]{1,0:T(8,128)(2,1)S(1)}, u32[]{:S(2)}, u32[]{:S(2)}) collective-permute-start(bf16[16,1024]{1,0:T(8,128)(2,1)S(1)} %get-tuple-element.57), channel_id=1, source_target_pairs={{1,2},{3,4},{5,6},{7,8},{9,10},{11,12},{13,14},{15,16},{17,18},{19... | collective-permute-start | bytes 98312 | tf_op jit(solution)/shard_map/ppermute | solution.py:506
  64.0 2.3 %depthwise.1.sum_ref = f32[256,1024]{1,0:T(8,128)S(1)} custom-call(bf16[272,1024]{1,0:T(8,128)(2,1)S(1)} %get-tuple-element.56.gated_ref, bf16[31,1024]{1,0:T(8,128)(2,1)S(1)} %copy-done.12, f32[2,8,128]{2,1,0:T(8,128)S(1)} %get-tuple-element.36.flags_ref), custom_call_target="tpu_custom_call" | custom-call | flops 1073741824 | bytes 4194304 | tf_op jit(solution)/shard_map/depthwise/pallas_call | solution.py:507
  66.3 6.2 %collective-permute-done.5.halo_ref = bf16[16,1024]{1,0:T(8,128)(2,1)S(1)} collective-permute-done((bf16[16,1024]{1,0:T(8,128)(2,1)S(1)}, bf16[16,1024]{1,0:T(8,128)(2,1)S(1)}, u32[]{:S(2)}, u32[]{:S(2)}) %collective-permute-start.5) | collective-permute-done | bytes 32800 | tf_op jit(solution)/shard_map/ppermute | solution.py:506
  72.6 7.2 %tail.1 = bf16[256,1024]{1,0:T(8,128)(2,1)} custom-call(f32[256,1024]{1,0:T(8,128)S(1)} %depthwise.1.sum_ref, bf16[16,1024]{1,0:T(8,128)(2,1)S(1)} %collective-permute-done.5.halo_ref, bf16[31,1024]{1,0:T(8,128)(2,1)S(1)} %copy-done.12, f32[2,8,128]{2,1,0:T(8,128)S(1)} %get-tuple-element.36.flags_ref, f32[256,1024]{1,0:T(8,128)S(1)} %get-tuple-element.58.first_ref, ...), custom_call_target="tpu_custom_call" | custom-call | flops 19327352832 | bytes 75497472 | tf_op jit(solution)/shard_map/tail/pallas_call | solution.py:520
  (35 shorter events, 2.5 us)
Async XLA Ops:
  0.0 1.2 %copy-start.2 = (bf16[512,1024]{1,0:T(8,128)(2,1)S(1)}, bf16[512,1024]{1,0:T(8,128)(2,1)}, u32[]{:S(2)}) copy-start(bf16[512,1024]{1,0:T(8,128)(2,1)} %frames_ref.3) | copy-start | bytes 3145732
  1.2 0.7 copy-start.4
  2.7 21.0 %collective-permute-start = (bf16[256,1024]{1,0:T(8,128)(2,1)S(1)}, bf16[256,1024]{1,0:T(8,128)(2,1)S(1)}, u32[]{:S(2)}, u32[]{:S(2)}) collective-permute-start(bf16[256,1024]{1,0:T(8,128)(2,1)S(1)} %get-tuple-element.35), channel_id=1, source_target_pairs={{0,2},{2,4},{4,6},{6,8},{8,10},{10,12},{12,14},{14,16},{16,18},{18... | collective-permute-start | bytes 1572872 | tf_op jit(solution)/shard_map/ppermute | solution.py:416
  6.1 1.9 %copy-start = (bf16[1024,3,512]{2,0,1:T(8,128)(2,1)S(1)}, bf16[1024,3,512]{2,0,1:T(8,128)(2,1)}, u32[]{:S(2)}) copy-start(bf16[1024,3,512]{2,0,1:T(8,128)(2,1)} %param.17) | copy-start | bytes 9437188
  8.0 0.7 copy-start.5
  9.3 20.9 %copy-start.1 = (bf16[1024,3,512]{2,0,1:T(8,128)(2,1)S(1)}, bf16[1024,3,512]{2,0,1:T(8,128)(2,1)}, u32[]{:S(2)}) copy-start(bf16[1024,3,512]{2,0,1:T(8,128)(2,1)} %param.17) | copy-start | bytes 9437188
  14.2 36.9 %copy-start.11 = (bf16[512,1024]{1,0:T(8,128)(2,1)S(1)}, bf16[512,1024]{1,0:T(8,128)(2,1)}, u32[]{:S(2)}) copy-start(bf16[512,1024]{1,0:T(8,128)(2,1)} %w_out_ref.3) | copy-start | bytes 3145732
  14.3 58.3 %collective-permute-start.6 = (bf16[1024,2048]{1,0:T(8,128)(2,1)}, bf16[1024,2048]{1,0:T(8,128)(2,1)S(1)}, u32[]{:S(2)}, u32[]{:S(2)}) collective-permute-start(bf16[1024,2048]{1,0:T(8,128)(2,1)} %up_own_ref.1), channel_id=1, source_target_pairs={{0,1},{1,0},{2,3},{3,2},{4,5},{5,4},{6,7},{7,6},{8,9},{9,8},{10,11... | collective-permute-start | bytes 12582920 | tf_op jit(solution)/shard_map/ppermute | solution.py:446
  16.3 56.2 %collective-permute-start.7 = (bf16[2048,1024]{1,0:T(8,128)(2,1)}, bf16[2048,1024]{1,0:T(8,128)(2,1)S(1)}, u32[]{:S(2)}, u32[]{:S(2)}) collective-permute-start(bf16[2048,1024]{1,0:T(8,128)(2,1)} %down_own_ref.1), channel_id=1, source_target_pairs={{0,1},{1,0},{2,3},{3,2},{4,5},{5,4},{6,7},{7,6},{8,9},{9,8},{10,11... | collective-permute-start | bytes 12582920 | tf_op jit(solution)/shard_map/ppermute | solution.py:447
  23.7 6.5 %collective-permute-start.2 = (bf16[256,1024]{1,0:T(8,128)(2,1)S(1)}, bf16[256,1024]{1,0:T(8,128)(2,1)S(1)}, u32[]{:S(2)}, u32[]{:S(2)}) collective-permute-start(bf16[256,1024]{1,0:T(8,128)(2,1)S(1)} %collective-permute-done.mine_ref), channel_id=1, source_target_pairs={{0,1},{1,0},{2,3},{3,2},{4,5},{5,4},{6,7},{7,6},{8,9},{9,8},{10,11... | collective-permute-start | bytes 1572872 | tf_op jit(solution)/shard_map/ppermute | solution.py:450
  25.6 21.6 %collective-permute-start.1 = (bf16[256,1024]{1,0:T(8,128)(2,1)S(1)}, bf16[256,1024]{1,0:T(8,128)(2,1)S(1)}, u32[]{:S(2)}, u32[]{:S(2)}) collective-permute-start(bf16[256,1024]{1,0:T(8,128)(2,1)S(1)} %collective-permute-done.mine_ref), channel_id=1, source_target_pairs={{0,2},{2,4},{4,6},{6,8},{8,10},{10,12},{12,14},{14,16},{16,18},{18... | collective-permute-start | bytes 1572872 | tf_op jit(solution)/shard_map/ppermute | solution.py:449
  47.2 10.7 %copy-start.3 = (bf16[512,1024]{1,0:T(8,128)(2,1)S(1)}, bf16[512,1024]{1,0:T(8,128)(2,1)}, u32[]{:S(2)}) copy-start(bf16[512,1024]{1,0:T(8,128)(2,1)} %frames_ref.3) | copy-start | bytes 3145732
  47.2 3.9 %collective-permute-start.3 = (bf16[256,1024]{1,0:T(8,128)(2,1)S(1)}, bf16[256,1024]{1,0:T(8,128)(2,1)S(1)}, u32[]{:S(2)}, u32[]{:S(2)}) collective-permute-start(bf16[256,1024]{1,0:T(8,128)(2,1)S(1)} %collective-permute-done.1.mine_ref), channel_id=1, source_target_pairs={{0,1},{1,0},{2,3},{3,2},{4,5},{5,4},{6,7},{7,6},{8,9},{9,8},{10,11... | collective-permute-start | bytes 1572872 | tf_op jit(solution)/shard_map/ppermute | solution.py:466
  55.5 4.1 %copy-start.7 = (bf16[1024,2048]{1,0:T(8,128)(2,1)S(1)}, bf16[1024,2048]{1,0:T(8,128)(2,1)}, u32[]{:S(2)}) copy-start(bf16[1024,2048]{1,0:T(8,128)(2,1)} %w_ref.1) | copy-start | bytes 12582916
  55.6 4.1 %copy-start.13 = (f32[1024]{0:T(1024)S(1)}, f32[1024]{0:T(1024)}, u32[]{:S(2)}) copy-start(f32[1024]{0:T(1024)} %param.19) | copy-start | bytes 12292
  55.6 4.1 %collective-permute-start.4 = (bf16[272,1024]{1,0:T(8,128)(2,1)S(1)}, bf16[272,1024]{1,0:T(8,128)(2,1)S(1)}, u32[]{:S(2)}, u32[]{:S(2)}) collective-permute-start(bf16[272,1024]{1,0:T(8,128)(2,1)S(1)} %get-tuple-element.55), channel_id=1, source_target_pairs={{0,1},{1,0},{2,3},{3,2},{4,5},{5,4},{6,7},{7,6},{8,9},{9,8},{10,11... | collective-permute-start | bytes 1671176 | tf_op jit(solution)/shard_map/ppermute | solution.py:481
  59.7 4.3 %copy-start.12 = (bf16[31,1024]{1,0:T(8,128)(2,1)S(1)}, bf16[31,1024]{1,0:T(8,128)(2,1)}, u32[]{:S(2)}) copy-start(bf16[31,1024]{1,0:T(8,128)(2,1)} %taps_ref.3) | copy-start | bytes 190468
  59.7 12.8 %copy-start.8 = (bf16[1024,2048]{1,0:T(8,128)(2,1)S(1)}, bf16[1024,2048]{1,0:T(8,128)(2,1)}, u32[]{:S(2)}) copy-start(bf16[1024,2048]{1,0:T(8,128)(2,1)} %up_own_ref.1) | copy-start | bytes 12582916
  59.7 12.8 %copy-start.9 = (bf16[2048,1024]{1,0:T(8,128)(2,1)S(1)}, bf16[2048,1024]{1,0:T(8,128)(2,1)}, u32[]{:S(2)}) copy-start(bf16[2048,1024]{1,0:T(8,128)(2,1)} %down_own_ref.1) | copy-start | bytes 12582916
  59.7 12.8 %copy-start.10 = (bf16[1024,1024]{1,0:T(8,128)(2,1)S(1)}, bf16[1024,1024]{1,0:T(8,128)(2,1)}, u32[]{:S(2)}) copy-start(bf16[1024,1024]{1,0:T(8,128)(2,1)} %w_point_ref.1) | copy-start | bytes 6291460
  59.7 12.8 %copy-start.14 = (f32[1024]{0:T(1024)S(1)}, f32[1024]{0:T(1024)}, u32[]{:S(2)}) copy-start(f32[1024]{0:T(1024)} %param.22) | copy-start | bytes 12292
  59.7 12.8 %copy-start.15 = (f32[1024]{0:T(1024)S(1)}, f32[1024]{0:T(1024)}, u32[]{:S(2)}) copy-start(f32[1024]{0:T(1024)} %param.24) | copy-start | bytes 12292
  59.7 12.8 %copy-start.16 = (f32[1024]{0:T(1024)S(1)}, f32[1024]{0:T(1024)}, u32[]{:S(2)}) copy-start(f32[1024]{0:T(1024)} %param.27) | copy-start | bytes 12292
  61.6 10.9 %collective-permute-start.5 = (bf16[16,1024]{1,0:T(8,128)(2,1)S(1)}, bf16[16,1024]{1,0:T(8,128)(2,1)S(1)}, u32[]{:S(2)}, u32[]{:S(2)}) collective-permute-start(bf16[16,1024]{1,0:T(8,128)(2,1)S(1)} %get-tuple-element.57), channel_id=1, source_target_pairs={{1,2},{3,4},{5,6},{7,8},{9,10},{11,12},{13,14},{15,16},{17,18},{19... | collective-permute-start | bytes 98312 | tf_op jit(solution)/shard_map/ppermute | solution.py:506
  (1 other events, 0.7 us)

commit v4 on v3

--- a/solution.py
+++ b/solution.py
@@ -13,8 +13,8 @@
 EDGE = 16
 MIB = 1 << 20
 EARLY = 0.001
-LATE = 4.0
-MIDDLE = 4.0
+LATE = 8.0
+MIDDLE = 1.0
 VMEM = pl.BlockSpec(memory_space=pltpu.VMEM)
 HBM = pl.BlockSpec(memory_space=pltpu.HBM)
 
@@ -414,6 +414,7 @@
         name="send_norm",
     )(frames, row(gain_attn))
     near_mine = lax.ppermute(sent, "tm", [(i, i + 1) for i in range(tm - 1)])
+    far_mine = lax.ppermute(sent, "tm", [(i, i + 2) for i in range(tm - 2)])
     qkv, flags = pl.pallas_call(
         own_kernel,
         grid=(3,),
@@ -445,8 +446,7 @@
     up_held, down_held, own_parts = lax.optimization_barrier((w_up, w_down, own_parts))
     up_other = lax.ppermute(up_held, "mp", swap)
     down_other = lax.ppermute(down_held, "mp", swap)
-    near_mine, own_parts = lax.optimization_barrier((near_mine, own_parts))
-    far_mine = lax.ppermute(near_mine, "tm", [(i, i + 1) for i in range(tm - 1)])
+    near_mine, far_mine, own_parts = lax.optimization_barrier((near_mine, far_mine, own_parts))
     near_theirs = lax.ppermute(near_mine, "mp", swap)
     near_parts = pl.pallas_call(
         near_kernel,
@@ -462,7 +462,6 @@
         cost_estimate=cost(slab * width * 2 * local + 8 * slab * slab * local, 8 * MIB, MIDDLE),
         name="near_attention",
     )(qkv, near_mine, near_theirs, w_planes, flags, *own_parts)
-    far_mine, near_parts = lax.optimization_barrier((far_mine, near_parts))
     far_theirs = lax.ppermute(far_mine, "mp", swap)
     heads, to_other = pl.pallas_call(
         far_kernel,

time: 80.2 us -> 74 us (0.923)
  waiting for transfers between devices: 29.2 us -> 19.8 us
  starting transfers between devices: 18.6 us -> 21.6 us
    ppermute x1, waiting for transfers between devices: 12.4 us -> 1.54 us  [on_device(): far_mine = lax.ppermute(sent, 'tm', [(i, i + 2) for i in range(tm - 2)])]
    ppermute x1, waiting for transfers between devices: 4.91 us -> 11.5 us  [on_device(): near_mine = lax.ppermute(sent, 'tm', [(i, i + 1) for i in range(tm - 1)])]
    ppermute x1, starting transfers between devices: 1.92 us -> 4.93 us  [on_device(): far_mine = lax.ppermute(sent, 'tm', [(i, i + 2) for i in range(tm - 2)])]
    ppermute x1, waiting for transfers between devices: 2.7 us -> 0.01 us  [on_device(): near_theirs = lax.ppermute(near_mine, 'mp', swap)]
    ppermute x1, waiting for transfers between devices: 1.7 us -> 0.01 us  [on_device(): far_theirs = lax.ppermute(far_mine, 'mp', swap)]
    ppermute x1, starting transfers between devices: 3.4 us -> 2.5 us  [on_device(): near_mine = lax.ppermute(sent, 'tm', [(i, i + 1) for i in range(tm - 1)])]
    ppermute x1, waiting for transfers between devices: 6.17 us -> 5.33 us  [on_device(): lax.ppermute(edge, ('tm', 'mp'), halo_pairs + [(b, a) for a, b in halo_pa...]
    ppermute x1, starting transfers between devices: 2.4 us -> 3.25 us  [on_device(): lax.ppermute(edge, ('tm', 'mp'), halo_pairs + [(b, a) for a, b in halo_pa...]
  transfers between devices with their start and end apart: 8 -> 8, of which waited for: 6 -> 4; matrix products, arithmetic and copies ran while one was open for 0% -> 0% of each run, Pallas kernels for 23% -> 25%
where the time goes in v4:
time: 74 us; the launch traced here: 73.6 us
  Pallas kernels  26.5 us (36%)
  starting transfers between devices  21.6 us (29%)
  waiting for transfers between devices  19.8 us (27%)
  local copies, waits for them, and re-layouts  5.45 us (7%)
    ppermute x1, waiting for transfers between devices, on_device(): near_mine = lax.ppermute(sent, 'tm', [(i, i + 1) for i in range(tm - 1)])  11.5 us
    pallas_call x1, Pallas kernels, on_device(): pl.pallas_call(tail_kernel, out_shape=shape((rows, width), bf16), in_spec...  7.22 us
    unnamed x34, local copies, waits for them, and re-layouts  5.45 us
    ppermute x1, waiting for transfers between devices, on_device(): lax.ppermute(edge, ('tm', 'mp'), halo_pairs + [(b, a) for a, b in halo_pa...  5.33 us
    ppermute x1, starting transfers between devices, on_device(): far_mine = lax.ppermute(sent, 'tm', [(i, i + 2) for i in range(tm - 2)])  4.93 us
    pallas_call x1, Pallas kernels, on_device(): pl.pallas_call(near_kernel, out_shape=partial, in_specs=[VMEM] * 8, out_s...  4.58 us
    pallas_call x1, Pallas kernels, on_device(): pl.pallas_call(far_kernel, out_shape=(shape((slab, local), bf16), shape((...  4.35 us
    ppermute x1, starting transfers between devices, on_device(): lax.ppermute(edge, ('tm', 'mp'), halo_pairs + [(b, a) for a, b in halo_pa...  3.25 us
  transfers between devices with their start and end apart: 8, of which 4 were waited for; matrix products, arithmetic and copies ran while one was open for 0% of the time, Pallas kernels for 25%

profile of v4, /device:TPU:256, one launch (start us, length us, event | category | flops | bytes accessed | tf_op | source)
XLA Modules:
  0.0 73.6 jit_solution(15271169515974722480)
XLA Ops:
  0.0 1.2 %copy-done.2 = bf16[512,1024]{1,0:T(8,128)(2,1)S(1)} copy-done((bf16[512,1024]{1,0:T(8,128)(2,1)S(1)}, bf16[512,1024]{1,0:T(8,128)(2,1)}, u32[]{:S(2)}) %copy-start.2) | copy-done | bytes 1048600
  1.2 0.7 copy-done.4
  1.9 0.7 %send_norm.1 = (bf16[256,1024]{1,0:T(8,128)(2,1)S(1)}, bf16[512,1024]{1,0:T(8,128)(2,1)S(1)}) custom-call(bf16[512,1024]{1,0:T(8,128)(2,1)S(1)} %copy-done.2, f32[1,1024]{1,0:T(1,128)S(1)} %bitcast.11), custom_call_target="tpu_custom_call" | custom-call | bytes 1048576 | tf_op jit(solution)/shard_map/send_norm/pallas_call | solution.py:407
  2.7 4.9 %collective-permute-start.1 = (bf16[256,1024]{1,0:T(8,128)(2,1)S(1)}, bf16[256,1024]{1,0:T(8,128)(2,1)S(1)}, u32[]{:S(2)}, u32[]{:S(2)}) collective-permute-start(bf16[256,1024]{1,0:T(8,128)(2,1)S(1)} %get-tuple-element.32), channel_id=1, source_target_pairs={{0,4},{2,6},{4,8},{6,10},{8,12},{10,14},{12,16},{14,18},{16,20},{1... | collective-permute-start | bytes 1572872 | tf_op jit(solution)/shard_map/ppermute | solution.py:417
  7.6 2.5 %collective-permute-start = (bf16[256,1024]{1,0:T(8,128)(2,1)S(1)}, bf16[256,1024]{1,0:T(8,128)(2,1)S(1)}, u32[]{:S(2)}, u32[]{:S(2)}) collective-permute-start(bf16[256,1024]{1,0:T(8,128)(2,1)S(1)} %get-tuple-element.32), channel_id=1, source_target_pairs={{0,2},{2,4},{4,6},{6,8},{8,10},{10,12},{12,14},{14,16},{16,18},{18... | collective-permute-start | bytes 1572872 | tf_op jit(solution)/shard_map/ppermute | solution.py:416
  10.1 1.9 %copy-done = bf16[1024,3,512]{2,0,1:T(8,128)(2,1)S(1)} copy-done((bf16[1024,3,512]{2,0,1:T(8,128)(2,1)S(1)}, bf16[1024,3,512]{2,0,1:T(8,128)(2,1)}, u32[]{:S(2)}) %copy-start) | copy-done | bytes 3145752
  12.0 0.7 copy-done.5
  13.3 2.4 %own_qkv.1 = (bf16[3,512,512]{2,1,0:T(8,128)(2,1)S(1)}, f32[2,8,128]{2,1,0:T(8,128)S(1)}) custom-call(bf16[512,1024]{1,0:T(8,128)(2,1)S(1)} %get-tuple-element.30.normed_ref, bf16[3,1024,512]{2,1,0:T(8,128)(2,1)S(1)} %bitcast.8, s32[1,128]{1,0:T(1,128)S(1)} %bitcast.12, s32[1,128]{1,0:T(1,128)S(1)} %bitcast.13), custom_call_target="tpu_custom_call" | custom-call | flops 1610612 | bytes 3145 | tf_op jit(solution)/shard_map/own_qkv/pallas_call | solution.py:418
  15.7 2.6 %own_attention.1 = (f32[512,512]{1,0:T(8,128)S(1)}, f32[512,512]{1,0:T(8,128)S(1)}, f32[512,512]{1,0:T(8,128)S(1)}) custom-call(bf16[3,512,512]{2,1,0:T(8,128)(2,1)S(1)} %get-tuple-element.31.qkv_ref, f32[2,8,128]{2,1,0:T(8,128)S(1)} %get-tuple-element.33.flags_ref), custom_call_target="tpu_custom_call" | custom-call | flops 1342177 | bytes 4194 | tf_op jit(solution)/shard_map/own_attention/pallas_call | solution.py:437
  18.3 2.1 %collective-permute-start.6 = (bf16[1024,2048]{1,0:T(8,128)(2,1)}, bf16[1024,2048]{1,0:T(8,128)(2,1)S(1)}, u32[]{:S(2)}, u32[]{:S(2)}) collective-permute-start(bf16[1024,2048]{1,0:T(8,128)(2,1)} %up_own_ref.1), channel_id=1, source_target_pairs={{0,1},{1,0},{2,3},{3,2},{4,5},{5,4},{6,7},{7,6},{8,9},{9,8},{10,11... | collective-permute-start | bytes 12582920 | tf_op jit(solution)/shard_map/ppermute | solution.py:447
  20.4 2.4 %collective-permute-start.7 = (bf16[2048,1024]{1,0:T(8,128)(2,1)}, bf16[2048,1024]{1,0:T(8,128)(2,1)S(1)}, u32[]{:S(2)}, u32[]{:S(2)}) collective-permute-start(bf16[2048,1024]{1,0:T(8,128)(2,1)} %down_own_ref.1), channel_id=1, source_target_pairs={{0,1},{1,0},{2,3},{3,2},{4,5},{5,4},{6,7},{7,6},{8,9},{9,8},{10,11... | collective-permute-start | bytes 12582920 | tf_op jit(solution)/shard_map/ppermute | solution.py:448
  22.8 1.5 %collective-permute-done.1.mine_ref = bf16[256,1024]{1,0:T(8,128)(2,1)S(1)} collective-permute-done((bf16[256,1024]{1,0:T(8,128)(2,1)S(1)}, bf16[256,1024]{1,0:T(8,128)(2,1)S(1)}, u32[]{:S(2)}, u32[]{:S(2)}) %collective-permute-start.1) | collective-permute-done | bytes 524320 | tf_op jit(solution)/shard_map/ppermute | solution.py:417
  24.3 11.5 %collective-permute-done.mine_ref = bf16[256,1024]{1,0:T(8,128)(2,1)S(1)} collective-permute-done((bf16[256,1024]{1,0:T(8,128)(2,1)S(1)}, bf16[256,1024]{1,0:T(8,128)(2,1)S(1)}, u32[]{:S(2)}, u32[]{:S(2)}) %collective-permute-start) | collective-permute-done | bytes 524320 | tf_op jit(solution)/shard_map/ppermute | solution.py:416
  35.8 1.9 %collective-permute-start.3 = (bf16[256,1024]{1,0:T(8,128)(2,1)S(1)}, bf16[256,1024]{1,0:T(8,128)(2,1)S(1)}, u32[]{:S(2)}, u32[]{:S(2)}) collective-permute-start(bf16[256,1024]{1,0:T(8,128)(2,1)S(1)} %collective-permute-done.mine_ref), channel_id=1, source_target_pairs={{0,1},{1,0},{2,3},{3,2},{4,5},{5,4},{6,7},{7,6},{8,9},{9,8},{10,11... | collective-permute-start | bytes 1572872 | tf_op jit(solution)/shard_map/ppermute | solution.py:450
  37.7 2.6 %collective-permute-start.2 = (bf16[256,1024]{1,0:T(8,128)(2,1)S(1)}, bf16[256,1024]{1,0:T(8,128)(2,1)S(1)}, u32[]{:S(2)}, u32[]{:S(2)}) collective-permute-start(bf16[256,1024]{1,0:T(8,128)(2,1)S(1)} %collective-permute-done.1.mine_ref), channel_id=1, source_target_pairs={{0,1},{1,0},{2,3},{3,2},{4,5},{5,4},{6,7},{7,6},{8,9},{9,8},{10,11... | collective-permute-start | bytes 1572872 | tf_op jit(solution)/shard_map/ppermute | solution.py:465
  40.3 4.6 %near_attention.1 = (f32[512,512]{1,0:T(8,128)S(1)}, f32[512,512]{1,0:T(8,128)S(1)}, f32[512,512]{1,0:T(8,128)S(1)}) custom-call(bf16[3,512,512]{2,1,0:T(8,128)(2,1)S(1)} %get-tuple-element.31.qkv_ref, bf16[256,1024]{1,0:T(8,128)(2,1)S(1)} %collective-permute-done.mine_ref, bf16[256,1024]{1,0:T(8,128)(2,1)S(1)} %collective-permute-done.3.theirs_ref, ...), custom_call_target="tpu_custom_call" | custom-call | flops 3221225472 | bytes 8388608 | tf_op jit(solution)/shard_map/near_attention/pallas_call | solution.py:451
  45.0 4.4 %far_attention.1 = (bf16[512,512]{1,0:T(8,128)(2,1)S(1)}, bf16[272,1024]{1,0:T(8,128)(2,1)S(1)}) custom-call(bf16[3,512,512]{2,1,0:T(8,128)(2,1)S(1)} %get-tuple-element.31.qkv_ref, bf16[256,1024]{1,0:T(8,128)(2,1)S(1)} %collective-permute-done.1.mine_ref, bf16[256,1024]{1,0:T(8,128)(2,1)S(1)} %collective-permute-done.2.theirs_ref, ...), custom_call_target="tpu_custom_call" | custom-call | flops 15032385536 | bytes 83886080 | tf_op jit(solution)/shard_map/far_attention/pallas_call | solution.py:466
  49.3 1.9 %collective-permute-start.4 = (bf16[272,1024]{1,0:T(8,128)(2,1)S(1)}, bf16[272,1024]{1,0:T(8,128)(2,1)S(1)}, u32[]{:S(2)}, u32[]{:S(2)}) collective-permute-start(bf16[272,1024]{1,0:T(8,128)(2,1)S(1)} %get-tuple-element.49), channel_id=1, source_target_pairs={{0,1},{1,0},{2,3},{3,2},{4,5},{5,4},{6,7},{7,6},{8,9},{9,8},{10,11... | collective-permute-start | bytes 1671176 | tf_op jit(solution)/shard_map/ppermute | solution.py:480
  51.8 1.4 %collective-permute-done.4.got_ref = bf16[272,1024]{1,0:T(8,128)(2,1)S(1)} collective-permute-done((bf16[272,1024]{1,0:T(8,128)(2,1)S(1)}, bf16[272,1024]{1,0:T(8,128)(2,1)S(1)}, u32[]{:S(2)}, u32[]{:S(2)}) %collective-permute-start.4) | collective-permute-done | bytes 557088 | tf_op jit(solution)/shard_map/ppermute | solution.py:480
  53.5 1.8 %gated_units.1 = (bf16[272,1024]{1,0:T(8,128)(2,1)S(1)}, bf16[16,1024]{1,0:T(8,128)(2,1)S(1)}, f32[256,1024]{1,0:T(8,128)S(1)}) custom-call(f32[272,1024]{1,0:T(8,128)S(1)} %out_projection.1.base_ref, bf16[272,1024]{1,0:T(8,128)(2,1)S(1)} %collective-permute-done.4.got_ref, f32[1,1024]{1,0:T(1,128)S(1)} %bitcast.14, bf16[1024,2048]{1,0:T(8,128)(2,1)S(1)} %copy-done.7), custom_call_target="tpu_custom_call" | custom-call | flops 9126805504 | bytes 41943040 | tf_op jit(solution)/shard_map/gated_units/pallas_call | solution.py:490
  55.4 3.2 %collective-permute-start.5 = (bf16[16,1024]{1,0:T(8,128)(2,1)S(1)}, bf16[16,1024]{1,0:T(8,128)(2,1)S(1)}, u32[]{:S(2)}, u32[]{:S(2)}) collective-permute-start(bf16[16,1024]{1,0:T(8,128)(2,1)S(1)} %get-tuple-element.51), channel_id=1, source_target_pairs={{1,2},{3,4},{5,6},{7,8},{9,10},{11,12},{13,14},{15,16},{17,18},{19... | collective-permute-start | bytes 98312 | tf_op jit(solution)/shard_map/ppermute | solution.py:505
  58.6 2.3 %depthwise.1.sum_ref = f32[256,1024]{1,0:T(8,128)S(1)} custom-call(bf16[272,1024]{1,0:T(8,128)(2,1)S(1)} %get-tuple-element.50.gated_ref, bf16[31,1024]{1,0:T(8,128)(2,1)S(1)} %copy-done.12, f32[2,8,128]{2,1,0:T(8,128)S(1)} %get-tuple-element.33.flags_ref), custom_call_target="tpu_custom_call" | custom-call | flops 2147483648 | bytes 8388608 | tf_op jit(solution)/shard_map/depthwise/pallas_call | solution.py:506
  61.0 5.3 %collective-permute-done.5.halo_ref = bf16[16,1024]{1,0:T(8,128)(2,1)S(1)} collective-permute-done((bf16[16,1024]{1,0:T(8,128)(2,1)S(1)}, bf16[16,1024]{1,0:T(8,128)(2,1)S(1)}, u32[]{:S(2)}, u32[]{:S(2)}) %collective-permute-start.5) | collective-permute-done | bytes 32800 | tf_op jit(solution)/shard_map/ppermute | solution.py:505
  66.4 7.2 %tail.1 = bf16[256,1024]{1,0:T(8,128)(2,1)} custom-call(f32[256,1024]{1,0:T(8,128)S(1)} %depthwise.1.sum_ref, bf16[16,1024]{1,0:T(8,128)(2,1)S(1)} %collective-permute-done.5.halo_ref, bf16[31,1024]{1,0:T(8,128)(2,1)S(1)} %copy-done.12, f32[2,8,128]{2,1,0:T(8,128)S(1)} %get-tuple-element.33.flags_ref, f32[256,1024]{1,0:T(8,128)S(1)} %get-tuple-element.52.first_ref, ...), custom_call_target="tpu_custom_call" | custom-call | flops 38654705664 | bytes 150994944 | tf_op jit(solution)/shard_map/tail/pallas_call | solution.py:519
  (35 shorter events, 1.5 us)
Async XLA Ops:
  0.0 1.2 %copy-start.2 = (bf16[512,1024]{1,0:T(8,128)(2,1)S(1)}, bf16[512,1024]{1,0:T(8,128)(2,1)}, u32[]{:S(2)}) copy-start(bf16[512,1024]{1,0:T(8,128)(2,1)} %frames_ref.3) | copy-start | bytes 3145732
  1.2 0.7 copy-start.4
  2.7 21.7 %collective-permute-start.1 = (bf16[256,1024]{1,0:T(8,128)(2,1)S(1)}, bf16[256,1024]{1,0:T(8,128)(2,1)S(1)}, u32[]{:S(2)}, u32[]{:S(2)}) collective-permute-start(bf16[256,1024]{1,0:T(8,128)(2,1)S(1)} %get-tuple-element.32), channel_id=1, source_target_pairs={{0,4},{2,6},{4,8},{6,10},{8,12},{10,14},{12,16},{14,18},{16,20},{1... | collective-permute-start | bytes 1572872 | tf_op jit(solution)/shard_map/ppermute | solution.py:417
  7.6 28.2 %collective-permute-start = (bf16[256,1024]{1,0:T(8,128)(2,1)S(1)}, bf16[256,1024]{1,0:T(8,128)(2,1)S(1)}, u32[]{:S(2)}, u32[]{:S(2)}) collective-permute-start(bf16[256,1024]{1,0:T(8,128)(2,1)S(1)} %get-tuple-element.32), channel_id=1, source_target_pairs={{0,2},{2,4},{4,6},{6,8},{8,10},{10,12},{12,14},{14,16},{16,18},{18... | collective-permute-start | bytes 1572872 | tf_op jit(solution)/shard_map/ppermute | solution.py:416
  10.1 1.9 %copy-start = (bf16[1024,3,512]{2,0,1:T(8,128)(2,1)S(1)}, bf16[1024,3,512]{2,0,1:T(8,128)(2,1)}, u32[]{:S(2)}) copy-start(bf16[1024,3,512]{2,0,1:T(8,128)(2,1)} %param.17) | copy-start | bytes 9437188
  12.0 0.7 copy-start.5
  13.3 27.0 %copy-start.1 = (bf16[1024,3,512]{2,0,1:T(8,128)(2,1)S(1)}, bf16[1024,3,512]{2,0,1:T(8,128)(2,1)}, u32[]{:S(2)}) copy-start(bf16[1024,3,512]{2,0,1:T(8,128)(2,1)} %param.17) | copy-start | bytes 9437188
  18.3 26.7 %copy-start.11 = (bf16[512,1024]{1,0:T(8,128)(2,1)S(1)}, bf16[512,1024]{1,0:T(8,128)(2,1)}, u32[]{:S(2)}) copy-start(bf16[512,1024]{1,0:T(8,128)(2,1)} %w_out_ref.3) | copy-start | bytes 3145732
  18.3 48.0 %collective-permute-start.6 = (bf16[1024,2048]{1,0:T(8,128)(2,1)}, bf16[1024,2048]{1,0:T(8,128)(2,1)S(1)}, u32[]{:S(2)}, u32[]{:S(2)}) collective-permute-start(bf16[1024,2048]{1,0:T(8,128)(2,1)} %up_own_ref.1), channel_id=1, source_target_pairs={{0,1},{1,0},{2,3},{3,2},{4,5},{5,4},{6,7},{7,6},{8,9},{9,8},{10,11... | collective-permute-start | bytes 12582920 | tf_op jit(solution)/shard_map/ppermute | solution.py:447
  20.4 45.9 %collective-permute-start.7 = (bf16[2048,1024]{1,0:T(8,128)(2,1)}, bf16[2048,1024]{1,0:T(8,128)(2,1)S(1)}, u32[]{:S(2)}, u32[]{:S(2)}) collective-permute-start(bf16[2048,1024]{1,0:T(8,128)(2,1)} %down_own_ref.1), channel_id=1, source_target_pairs={{0,1},{1,0},{2,3},{3,2},{4,5},{5,4},{6,7},{7,6},{8,9},{9,8},{10,11... | collective-permute-start | bytes 12582920 | tf_op jit(solution)/shard_map/ppermute | solution.py:448
  35.8 4.5 %collective-permute-start.3 = (bf16[256,1024]{1,0:T(8,128)(2,1)S(1)}, bf16[256,1024]{1,0:T(8,128)(2,1)S(1)}, u32[]{:S(2)}, u32[]{:S(2)}) collective-permute-start(bf16[256,1024]{1,0:T(8,128)(2,1)S(1)} %collective-permute-done.mine_ref), channel_id=1, source_target_pairs={{0,1},{1,0},{2,3},{3,2},{4,5},{5,4},{6,7},{7,6},{8,9},{9,8},{10,11... | collective-permute-start | bytes 1572872 | tf_op jit(solution)/shard_map/ppermute | solution.py:450
  37.7 7.2 %collective-permute-start.2 = (bf16[256,1024]{1,0:T(8,128)(2,1)S(1)}, bf16[256,1024]{1,0:T(8,128)(2,1)S(1)}, u32[]{:S(2)}, u32[]{:S(2)}) collective-permute-start(bf16[256,1024]{1,0:T(8,128)(2,1)S(1)} %collective-permute-done.1.mine_ref), channel_id=1, source_target_pairs={{0,1},{1,0},{2,3},{3,2},{4,5},{5,4},{6,7},{7,6},{8,9},{9,8},{10,11... | collective-permute-start | bytes 1572872 | tf_op jit(solution)/shard_map/ppermute | solution.py:465
  45.0 6.3 %copy-start.3 = (bf16[512,1024]{1,0:T(8,128)(2,1)S(1)}, bf16[512,1024]{1,0:T(8,128)(2,1)}, u32[]{:S(2)}) copy-start(bf16[512,1024]{1,0:T(8,128)(2,1)} %frames_ref.3) | copy-start | bytes 3145732
  49.3 3.9 %collective-permute-start.4 = (bf16[272,1024]{1,0:T(8,128)(2,1)S(1)}, bf16[272,1024]{1,0:T(8,128)(2,1)S(1)}, u32[]{:S(2)}, u32[]{:S(2)}) collective-permute-start(bf16[272,1024]{1,0:T(8,128)(2,1)S(1)} %get-tuple-element.49), channel_id=1, source_target_pairs={{0,1},{1,0},{2,3},{3,2},{4,5},{5,4},{6,7},{7,6},{8,9},{9,8},{10,11... | collective-permute-start | bytes 1671176 | tf_op jit(solution)/shard_map/ppermute | solution.py:480
  51.3 2.2 %copy-start.7 = (bf16[1024,2048]{1,0:T(8,128)(2,1)S(1)}, bf16[1024,2048]{1,0:T(8,128)(2,1)}, u32[]{:S(2)}) copy-start(bf16[1024,2048]{1,0:T(8,128)(2,1)} %w_ref.1) | copy-start | bytes 12582916
  51.3 2.2 %copy-start.13 = (f32[1024]{0:T(1024)S(1)}, f32[1024]{0:T(1024)}, u32[]{:S(2)}) copy-start(f32[1024]{0:T(1024)} %param.19) | copy-start | bytes 12292
  53.5 5.2 %copy-start.12 = (bf16[31,1024]{1,0:T(8,128)(2,1)S(1)}, bf16[31,1024]{1,0:T(8,128)(2,1)}, u32[]{:S(2)}) copy-start(bf16[31,1024]{1,0:T(8,128)(2,1)} %taps_ref.3) | copy-start | bytes 190468
  53.5 12.8 %copy-start.9 = (bf16[2048,1024]{1,0:T(8,128)(2,1)S(1)}, bf16[2048,1024]{1,0:T(8,128)(2,1)}, u32[]{:S(2)}) copy-start(bf16[2048,1024]{1,0:T(8,128)(2,1)} %down_own_ref.1) | copy-start | bytes 12582916
  55.3 11.0 %copy-start.8 = (bf16[1024,2048]{1,0:T(8,128)(2,1)S(1)}, bf16[1024,2048]{1,0:T(8,128)(2,1)}, u32[]{:S(2)}) copy-start(bf16[1024,2048]{1,0:T(8,128)(2,1)} %up_own_ref.1) | copy-start | bytes 12582916
  55.3 11.0 %copy-start.10 = (bf16[1024,1024]{1,0:T(8,128)(2,1)S(1)}, bf16[1024,1024]{1,0:T(8,128)(2,1)}, u32[]{:S(2)}) copy-start(bf16[1024,1024]{1,0:T(8,128)(2,1)} %w_point_ref.1) | copy-start | bytes 6291460
  55.3 11.0 %copy-start.14 = (f32[1024]{0:T(1024)S(1)}, f32[1024]{0:T(1024)}, u32[]{:S(2)}) copy-start(f32[1024]{0:T(1024)} %param.22) | copy-start | bytes 12292
  55.3 11.0 %copy-start.15 = (f32[1024]{0:T(1024)S(1)}, f32[1024]{0:T(1024)}, u32[]{:S(2)}) copy-start(f32[1024]{0:T(1024)} %param.24) | copy-start | bytes 12292
  55.4 11.0 %copy-start.16 = (f32[1024]{0:T(1024)S(1)}, f32[1024]{0:T(1024)}, u32[]{:S(2)}) copy-start(f32[1024]{0:T(1024)} %param.27) | copy-start | bytes 12292
  55.4 10.9 %collective-permute-start.5 = (bf16[16,1024]{1,0:T(8,128)(2,1)S(1)}, bf16[16,1024]{1,0:T(8,128)(2,1)S(1)}, u32[]{:S(2)}, u32[]{:S(2)}) collective-permute-start(bf16[16,1024]{1,0:T(8,128)(2,1)S(1)} %get-tuple-element.51), channel_id=1, source_target_pairs={{1,2},{3,4},{5,6},{7,8},{9,10},{11,12},{13,14},{15,16},{17,18},{19... | collective-permute-start | bytes 98312 | tf_op jit(solution)/shard_map/ppermute | solution.py:505
  (1 other events, 0.7 us)

commit v5 on v3

--- a/solution.py
+++ b/solution.py
@@ -13,8 +13,8 @@
 EDGE = 16
 MIB = 1 << 20
 EARLY = 0.001
-LATE = 4.0
-MIDDLE = 4.0
+LATE = 14.5
+MIDDLE = 0.1
 VMEM = pl.BlockSpec(memory_space=pltpu.VMEM)
 HBM = pl.BlockSpec(memory_space=pltpu.HBM)
 
@@ -140,11 +140,14 @@
     return attend_all([query], keys, values, [bias])[0]
 
 
-def place(normed, mine_ref, theirs_ref):
+def place(normed, mine_ref, *theirs_refs):
     rows = mine_ref.shape[0]
     core = lax.axis_index("mp")
     normed[pl.ds(pl.multiple_of(core * rows, rows), rows)] = mine_ref[...]
-    normed[pl.ds(pl.multiple_of((1 - core) * rows, rows), rows)] = theirs_ref[...]
+    first = pl.multiple_of((1 - core) * rows, rows)
+    for ref in theirs_refs:
+        normed[pl.ds(first, ref.shape[0])] = ref[...]
+        first = pl.multiple_of(first + ref.shape[0], EDGE)
 
 
 def merged(parts, total, top, weight):
@@ -176,13 +179,14 @@
 
 
 def near_kernel(
-    qkv_ref, mine_ref, theirs_ref, w_ref, flags_ref, own_total_ref, own_top_ref, own_weight_ref,
+    qkv_ref, mine_ref, first_ref, second_ref, w_ref, flags_ref,
+    own_total_ref, own_top_ref, own_weight_ref,
     total_ref, top_ref, weight_ref,
     normed, keys, values,
 ):
     slab, width = qkv_ref.shape[1:]
     count = slab // C
-    place(normed, mine_ref, theirs_ref)
+    place(normed, mine_ref, first_ref, second_ref)
     keys[...] = jnp.dot(normed[...], w_ref[1], preferred_element_type=jnp.float32).astype(
         jnp.bfloat16
     )
@@ -413,7 +417,11 @@
         cost_estimate=cost(0, 2 * rows * width * 2),
         name="send_norm",
     )(frames, row(gain_attn))
+    up_held, down_held, sent = lax.optimization_barrier((w_up, w_down, sent))
+    up_other = lax.ppermute(up_held, "mp", swap)
+    down_other = lax.ppermute(down_held, "mp", swap)
     near_mine = lax.ppermute(sent, "tm", [(i, i + 1) for i in range(tm - 1)])
+    far_mine = lax.ppermute(sent, "tm", [(i, i + 2) for i in range(tm - 2)])
     qkv, flags = pl.pallas_call(
         own_kernel,
         grid=(3,),
@@ -442,16 +450,12 @@
         cost_estimate=cost(5 * slab * slab * local, 4 * MIB, EARLY),
         name="own_attention",
     )(qkv, flags)
-    up_held, down_held, own_parts = lax.optimization_barrier((w_up, w_down, own_parts))
-    up_other = lax.ppermute(up_held, "mp", swap)
-    down_other = lax.ppermute(down_held, "mp", swap)
     near_mine, own_parts = lax.optimization_barrier((near_mine, own_parts))
-    far_mine = lax.ppermute(near_mine, "tm", [(i, i + 1) for i in range(tm - 1)])
-    near_theirs = lax.ppermute(near_mine, "mp", swap)
+    near_theirs = [lax.ppermute(near_mine[at : at + C], "mp", swap) for at in range(0, rows, C)]
     near_parts = pl.pallas_call(
         near_kernel,
         out_shape=partial,
-        in_specs=[VMEM] * 8,
+        in_specs=[VMEM] * 9,
         out_specs=(VMEM,) * 3,
         scratch_shapes=[
             pltpu.VMEM((slab, width), bf16),
@@ -461,7 +465,7 @@
         compiler_params=params(16),
         cost_estimate=cost(slab * width * 2 * local + 8 * slab * slab * local, 8 * MIB, MIDDLE),
         name="near_attention",
-    )(qkv, near_mine, near_theirs, w_planes, flags, *own_parts)
+    )(qkv, near_mine, *near_theirs, w_planes, flags, *own_parts)
     far_mine, near_parts = lax.optimization_barrier((far_mine, near_parts))
     far_theirs = lax.ppermute(far_mine, "mp", swap)
     heads, to_other = pl.pallas_call(
@@ -485,7 +489,7 @@
         in_specs=[VMEM] * 3,
         out_specs=VMEM,
         compiler_params=params(12),
-        cost_estimate=cost(window * width * local, 3 * MIB, LATE),
+        cost_estimate=cost(window * width * local, 3 * MIB),
         name="out_projection",
     )(heads, w_out, frames)
     gated, edge, first_res = pl.pallas_call(
@@ -499,7 +503,7 @@
         out_specs=(VMEM,) * 3,
         scratch_shapes=[pltpu.VMEM((window, width), bf16), pltpu.VMEM((window, width), f32)],
         compiler_params=params(16),
-        cost_estimate=cost(window * width * 2 * width, 5 * MIB, LATE),
+        cost_estimate=cost(window * width * 2 * width, 5 * MIB),
         name="gated_units",
     )(base, from_other, row(gain_conv), w_point_in)
     halo_pairs = [(2 * i + 1, 2 * i + 2) for i in range(tm - 1)]
@@ -514,7 +518,7 @@
             pltpu.VMEM((width // LANES, C + 2 * EDGE, LANES), f32),
         ],
         compiler_params=params(12),
-        cost_estimate=cost(rows * width * 512, MIB, LATE),
+        cost_estimate=cost(rows * width * 512, MIB),
         name="depthwise",
     )(gated, w_depth, flags)
     return pl.pallas_call(
@@ -531,7 +535,7 @@
             pltpu.VMEM((rows, width), f32),
         ],
         compiler_params=params(12),
-        cost_estimate=cost(rows * width * 9 * width, 18 * MIB, LATE),
+        cost_estimate=cost(rows * width * 9 * width, 18 * MIB),
         name="tail",
     )(
         depth_sum, halo, w_depth, flags, first_res, row(gain_depth), row(gain_ffn),

time: 80.2 us -> 74.1 us (0.924)
  waiting for transfers between devices: 29.2 us -> 15.1 us
  starting transfers between devices: 18.6 us -> 26.6 us
    ppermute x2 -> x3, waiting for transfers between devices: 15.1 us -> 1.13 us  [the longest x2 1.13 us: on_device(): lax.ppermute(near_mine[at:at + C], 'mp', swap)]
    ppermute x2 -> x3, starting transfers between devices: 3.83 us -> 9.1 us  [the longest x1 4.64 us: on_device(): far_mine = lax.ppermute(sent, 'tm', [(i, i + 2) for i in range(tm - 2)])]
    ppermute x1, waiting for transfers between devices: 4.91 us -> 8.21 us  [on_device(): near_mine = lax.ppermute(sent, 'tm', [(i, i + 1) for i in range(tm - 1)])]
    ppermute x1, waiting for transfers between devices: 6.17 us -> 3.44 us  [on_device(): lax.ppermute(edge, ('tm', 'mp'), halo_pairs + [(b, a) for a, b in halo_pa...]
    ppermute x1, starting transfers between devices: 2.4 us -> 4.87 us  [on_device(): lax.ppermute(edge, ('tm', 'mp'), halo_pairs + [(b, a) for a, b in halo_pa...]
  transfers between devices with their start and end apart: 8 -> 9, of which waited for: 6 -> 5; matrix products, arithmetic and copies ran while one was open for 0% -> 0% of each run, Pallas kernels for 23% -> 25%
where the time goes in v5:
time: 74.1 us; the launch traced here: 73.7 us
  starting transfers between devices  26.6 us (36%)
  Pallas kernels  26.5 us (36%)
  waiting for transfers between devices  15.1 us (20%)
  local copies, waits for them, and re-layouts  5.21 us (7%)
    ppermute x1, waiting for transfers between devices, on_device(): near_mine = lax.ppermute(sent, 'tm', [(i, i + 1) for i in range(tm - 1)])  8.21 us
    pallas_call x1, Pallas kernels, on_device(): pl.pallas_call(tail_kernel, out_shape=shape((rows, width), bf16), in_spec...  7.22 us
    unnamed x34, local copies, waits for them, and re-layouts  5.18 us
    ppermute x1, starting transfers between devices, on_device(): lax.ppermute(edge, ('tm', 'mp'), halo_pairs + [(b, a) for a, b in halo_pa...  4.87 us
    ppermute x1, starting transfers between devices, on_device(): far_mine = lax.ppermute(sent, 'tm', [(i, i + 2) for i in range(tm - 2)])  4.64 us
    pallas_call x1, Pallas kernels, on_device(): pl.pallas_call(near_kernel, out_shape=partial, in_specs=[VMEM] * 9, out_s...  4.54 us
    ppermute x2, starting transfers between devices, on_device(): lax.ppermute(near_mine[at:at + C], 'mp', swap)  4.46 us
    pallas_call x1, Pallas kernels, on_device(): pl.pallas_call(far_kernel, out_shape=(shape((slab, local), bf16), shape((...  4.36 us
  transfers between devices with their start and end apart: 9, of which 5 were waited for; matrix products, arithmetic and copies ran while one was open for 0% of the time, Pallas kernels for 25%

profile of v5, /device:TPU:256, one launch (start us, length us, event | category | flops | bytes accessed | tf_op | source)
XLA Modules:
  0.0 73.7 jit_solution(12042629993281171641)
XLA Ops:
  0.0 1.2 %copy-done.4 = bf16[512,1024]{1,0:T(8,128)(2,1)S(1)} copy-done((bf16[512,1024]{1,0:T(8,128)(2,1)S(1)}, bf16[512,1024]{1,0:T(8,128)(2,1)}, u32[]{:S(2)}) %copy-start.4) | copy-done | bytes 1048600
  1.9 0.7 %send_norm.1 = (bf16[256,1024]{1,0:T(8,128)(2,1)S(1)}, bf16[512,1024]{1,0:T(8,128)(2,1)S(1)}) custom-call(bf16[512,1024]{1,0:T(8,128)(2,1)S(1)} %copy-done.4, f32[1,1024]{1,0:T(1,128)S(1)} %bitcast.11), custom_call_target="tpu_custom_call" | custom-call | bytes 1048576 | tf_op jit(solution)/shard_map/send_norm/pallas_call | solution.py:411
  2.7 3.4 %collective-permute-start.1 = (bf16[256,1024]{1,0:T(8,128)(2,1)S(1)}, bf16[256,1024]{1,0:T(8,128)(2,1)S(1)}, u32[]{:S(2)}, u32[]{:S(2)}) collective-permute-start(bf16[256,1024]{1,0:T(8,128)(2,1)S(1)} %get-tuple-element.34), channel_id=1, source_target_pairs={{0,2},{2,4},{4,6},{6,8},{8,10},{10,12},{12,14},{14,16},{16,18},{18... | collective-permute-start | bytes 1572872 | tf_op jit(solution)/shard_map/ppermute | solution.py:423
  6.1 4.6 %collective-permute-start = (bf16[256,1024]{1,0:T(8,128)(2,1)S(1)}, bf16[256,1024]{1,0:T(8,128)(2,1)S(1)}, u32[]{:S(2)}, u32[]{:S(2)}) collective-permute-start(bf16[256,1024]{1,0:T(8,128)(2,1)S(1)} %get-tuple-element.34), channel_id=1, source_target_pairs={{0,4},{2,6},{4,8},{6,10},{8,12},{10,14},{12,16},{14,18},{16,20},{1... | collective-permute-start | bytes 1572872 | tf_op jit(solution)/shard_map/ppermute | solution.py:424
  10.7 1.9 %collective-permute-start.7 = (bf16[1024,2048]{1,0:T(8,128)(2,1)}, bf16[1024,2048]{1,0:T(8,128)(2,1)S(1)}, u32[]{:S(2)}, u32[]{:S(2)}) collective-permute-start(bf16[1024,2048]{1,0:T(8,128)(2,1)} %up_own_ref.1), channel_id=1, source_target_pairs={{0,1},{1,0},{2,3},{3,2},{4,5},{5,4},{6,7},{7,6},{8,9},{9,8},{10,11... | collective-permute-start | bytes 12582920 | tf_op jit(solution)/shard_map/ppermute | solution.py:421
  12.6 2.4 %collective-permute-start.8 = (bf16[2048,1024]{1,0:T(8,128)(2,1)}, bf16[2048,1024]{1,0:T(8,128)(2,1)S(1)}, u32[]{:S(2)}, u32[]{:S(2)}) collective-permute-start(bf16[2048,1024]{1,0:T(8,128)(2,1)} %down_own_ref.1), channel_id=1, source_target_pairs={{0,1},{1,0},{2,3},{3,2},{4,5},{5,4},{6,7},{7,6},{8,9},{9,8},{10,11... | collective-permute-start | bytes 12582920 | tf_op jit(solution)/shard_map/ppermute | solution.py:422
  15.1 1.9 %copy-done = bf16[1024,3,512]{2,0,1:T(8,128)(2,1)S(1)} copy-done((bf16[1024,3,512]{2,0,1:T(8,128)(2,1)S(1)}, bf16[1024,3,512]{2,0,1:T(8,128)(2,1)}, u32[]{:S(2)}) %copy-start) | copy-done | bytes 3145752
  18.3 2.4 %own_qkv.1 = (bf16[3,512,512]{2,1,0:T(8,128)(2,1)S(1)}, f32[2,8,128]{2,1,0:T(8,128)S(1)}) custom-call(bf16[512,1024]{1,0:T(8,128)(2,1)S(1)} %get-tuple-element.31.normed_ref, bf16[3,1024,512]{2,1,0:T(8,128)(2,1)S(1)} %bitcast.8, s32[1,128]{1,0:T(1,128)S(1)} %bitcast.16, s32[1,128]{1,0:T(1,128)S(1)} %bitcast.17), custom_call_target="tpu_custom_call" | custom-call | flops 1610612 | bytes 3145 | tf_op jit(solution)/shard_map/own_qkv/pallas_call | solution.py:425
  20.6 2.6 %own_attention.1 = (f32[512,512]{1,0:T(8,128)S(1)}, f32[512,512]{1,0:T(8,128)S(1)}, f32[512,512]{1,0:T(8,128)S(1)}) custom-call(bf16[3,512,512]{2,1,0:T(8,128)(2,1)S(1)} %get-tuple-element.32.qkv_ref, f32[2,8,128]{2,1,0:T(8,128)S(1)} %get-tuple-element.35.flags_ref), custom_call_target="tpu_custom_call" | custom-call | flops 1342177 | bytes 4194 | tf_op jit(solution)/shard_map/own_attention/pallas_call | solution.py:444
  23.2 8.2 %collective-permute-done.1.mine_ref = bf16[256,1024]{1,0:T(8,128)(2,1)S(1)} collective-permute-done((bf16[256,1024]{1,0:T(8,128)(2,1)S(1)}, bf16[256,1024]{1,0:T(8,128)(2,1)S(1)}, u32[]{:S(2)}, u32[]{:S(2)}) %collective-permute-start.1) | collective-permute-done | bytes 524320 | tf_op jit(solution)/shard_map/ppermute | solution.py:423
  31.5 1.9 %collective-permute-start.3 = (bf16[128,1024]{1,0:T(8,128)(2,1)S(1)}, bf16[128,1024]{1,0:T(8,128)(2,1)S(1)}, u32[]{:S(2)}, u32[]{:S(2)}) collective-permute-start(bf16[128,1024]{1,0:T(8,128)(2,1)S(1)} %get-tuple-element.57), channel_id=1, source_target_pairs={{0,1},{1,0},{2,3},{3,2},{4,5},{5,4},{6,7},{7,6},{8,9},{9,8},{10,11... | collective-permute-start | bytes 786440 | tf_op jit(solution)/shard_map/ppermute | solution.py:454
  33.4 2.5 %collective-permute-start.2 = (bf16[128,1024]{1,0:T(8,128)(2,1)S(1)}, bf16[128,1024]{1,0:T(8,128)(2,1)S(1)}, u32[]{:S(2)}, u32[]{:S(2)}) collective-permute-start(bf16[128,1024]{1,0:T(8,128)(2,1)S(1)} %get-tuple-element.58), channel_id=1, source_target_pairs={{0,1},{1,0},{2,3},{3,2},{4,5},{5,4},{6,7},{7,6},{8,9},{9,8},{10,11... | collective-permute-start | bytes 786440 | tf_op jit(solution)/shard_map/ppermute | solution.py:454
  36.0 1.1 %collective-permute-done.2.first_ref = bf16[128,1024]{1,0:T(8,128)(2,1)S(1)} collective-permute-done((bf16[128,1024]{1,0:T(8,128)(2,1)S(1)}, bf16[128,1024]{1,0:T(8,128)(2,1)S(1)}, u32[]{:S(2)}, u32[]{:S(2)}) %collective-permute-start.2) | collective-permute-done | bytes 262176 | tf_op jit(solution)/shard_map/ppermute | solution.py:454
  37.1 4.5 %near_attention.1 = (f32[512,512]{1,0:T(8,128)S(1)}, f32[512,512]{1,0:T(8,128)S(1)}, f32[512,512]{1,0:T(8,128)S(1)}) custom-call(bf16[3,512,512]{2,1,0:T(8,128)(2,1)S(1)} %get-tuple-element.32.qkv_ref, bf16[256,1024]{1,0:T(8,128)(2,1)S(1)} %collective-permute-done.1.mine_ref, bf16[128,1024]{1,0:T(8,128)(2,1)S(1)} %collective-permute-done.2.first_ref, ...), custom_call_target="tpu_custom_call" | custom-call | flops 322122560 | bytes 838860 | tf_op jit(solution)/shard_map/near_attention/pallas_call | solution.py:455
  41.7 2.6 %collective-permute-start.4 = (bf16[256,1024]{1,0:T(8,128)(2,1)S(1)}, bf16[256,1024]{1,0:T(8,128)(2,1)S(1)}, u32[]{:S(2)}, u32[]{:S(2)}) collective-permute-start(bf16[256,1024]{1,0:T(8,128)(2,1)S(1)} %collective-permute-done.mine_ref), channel_id=1, source_target_pairs={{0,1},{1,0},{2,3},{3,2},{4,5},{5,4},{6,7},{7,6},{8,9},{9,8},{10,11... | collective-permute-start | bytes 1572872 | tf_op jit(solution)/shard_map/ppermute | solution.py:470
  44.3 1.3 %collective-permute-done.4.theirs_ref = bf16[256,1024]{1,0:T(8,128)(2,1)S(1)} collective-permute-done((bf16[256,1024]{1,0:T(8,128)(2,1)S(1)}, bf16[256,1024]{1,0:T(8,128)(2,1)S(1)}, u32[]{:S(2)}, u32[]{:S(2)}) %collective-permute-start.4) | collective-permute-done | bytes 524320 | tf_op jit(solution)/shard_map/ppermute | solution.py:470
  45.6 4.4 %far_attention.1 = (bf16[512,512]{1,0:T(8,128)(2,1)S(1)}, bf16[272,1024]{1,0:T(8,128)(2,1)S(1)}) custom-call(bf16[3,512,512]{2,1,0:T(8,128)(2,1)S(1)} %get-tuple-element.32.qkv_ref, bf16[256,1024]{1,0:T(8,128)(2,1)S(1)} %collective-permute-done.mine_ref, bf16[256,1024]{1,0:T(8,128)(2,1)S(1)} %collective-permute-done.4.theirs_ref, ...), custom_call_target="tpu_custom_call" | custom-call | flops 27246198784 | bytes 152043520 | tf_op jit(solution)/shard_map/far_attention/pallas_call | solution.py:471
  50.0 2.3 %collective-permute-start.5 = (bf16[272,1024]{1,0:T(8,128)(2,1)S(1)}, bf16[272,1024]{1,0:T(8,128)(2,1)S(1)}, u32[]{:S(2)}, u32[]{:S(2)}) collective-permute-start(bf16[272,1024]{1,0:T(8,128)(2,1)S(1)} %get-tuple-element.51), channel_id=1, source_target_pairs={{0,1},{1,0},{2,3},{3,2},{4,5},{5,4},{6,7},{7,6},{8,9},{9,8},{10,11... | collective-permute-start | bytes 1671176 | tf_op jit(solution)/shard_map/ppermute | solution.py:485
  52.9 1.0 %collective-permute-done.5.got_ref = bf16[272,1024]{1,0:T(8,128)(2,1)S(1)} collective-permute-done((bf16[272,1024]{1,0:T(8,128)(2,1)S(1)}, bf16[272,1024]{1,0:T(8,128)(2,1)S(1)}, u32[]{:S(2)}, u32[]{:S(2)}) %collective-permute-start.5) | collective-permute-done | bytes 557088 | tf_op jit(solution)/shard_map/ppermute | solution.py:485
  53.9 1.9 %gated_units.1 = (bf16[272,1024]{1,0:T(8,128)(2,1)S(1)}, bf16[16,1024]{1,0:T(8,128)(2,1)S(1)}, f32[256,1024]{1,0:T(8,128)S(1)}) custom-call(f32[272,1024]{1,0:T(8,128)S(1)} %out_projection.1.base_ref, bf16[272,1024]{1,0:T(8,128)(2,1)S(1)} %collective-permute-done.5.got_ref, f32[1,1024]{1,0:T(1,128)S(1)} %bitcast.12, bf16[1024,2048]{1,0:T(8,128)(2,1)S(1)} %copy-done.6), custom_call_target="tpu_custom_call" | custom-call | flops 1140850688 | bytes 5242880 | tf_op jit(solution)/shard_map/gated_units/pallas_call | solution.py:495
  55.7 4.9 %collective-permute-start.6 = (bf16[16,1024]{1,0:T(8,128)(2,1)S(1)}, bf16[16,1024]{1,0:T(8,128)(2,1)S(1)}, u32[]{:S(2)}, u32[]{:S(2)}) collective-permute-start(bf16[16,1024]{1,0:T(8,128)(2,1)S(1)} %get-tuple-element.53), channel_id=1, source_target_pairs={{1,2},{3,4},{5,6},{7,8},{9,10},{11,12},{13,14},{15,16},{17,18},{19... | collective-permute-start | bytes 98312 | tf_op jit(solution)/shard_map/ppermute | solution.py:510
  60.6 2.3 %depthwise.1.sum_ref = f32[256,1024]{1,0:T(8,128)S(1)} custom-call(bf16[272,1024]{1,0:T(8,128)(2,1)S(1)} %get-tuple-element.52.gated_ref, bf16[31,1024]{1,0:T(8,128)(2,1)S(1)} %copy-done.9, f32[2,8,128]{2,1,0:T(8,128)S(1)} %get-tuple-element.35.flags_ref), custom_call_target="tpu_custom_call" | custom-call | flops 268435456 | bytes 1048576 | tf_op jit(solution)/shard_map/depthwise/pallas_call | solution.py:511
  63.0 3.4 %collective-permute-done.6.halo_ref = bf16[16,1024]{1,0:T(8,128)(2,1)S(1)} collective-permute-done((bf16[16,1024]{1,0:T(8,128)(2,1)S(1)}, bf16[16,1024]{1,0:T(8,128)(2,1)S(1)}, u32[]{:S(2)}, u32[]{:S(2)}) %collective-permute-start.6) | collective-permute-done | bytes 32800 | tf_op jit(solution)/shard_map/ppermute | solution.py:510
  66.5 7.2 %tail.1 = bf16[256,1024]{1,0:T(8,128)(2,1)} custom-call(f32[256,1024]{1,0:T(8,128)S(1)} %depthwise.1.sum_ref, bf16[16,1024]{1,0:T(8,128)(2,1)S(1)} %collective-permute-done.6.halo_ref, bf16[31,1024]{1,0:T(8,128)(2,1)S(1)} %copy-done.9, f32[2,8,128]{2,1,0:T(8,128)S(1)} %get-tuple-element.35.flags_ref, f32[256,1024]{1,0:T(8,128)S(1)} %get-tuple-element.54.first_ref, ...), custom_call_target="tpu_custom_call" | custom-call | flops 4831838208 | bytes 18874368 | tf_op jit(solution)/shard_map/tail/pallas_call | solution.py:524
  (38 shorter events, 2.6 us)
Async XLA Ops:
  0.0 1.2 %copy-start.4 = (bf16[512,1024]{1,0:T(8,128)(2,1)S(1)}, bf16[512,1024]{1,0:T(8,128)(2,1)}, u32[]{:S(2)}) copy-start(bf16[512,1024]{1,0:T(8,128)(2,1)} %frames_ref.3) | copy-start | bytes 3145732
  1.2 0.7 copy-start.10
  2.7 28.8 %collective-permute-start.1 = (bf16[256,1024]{1,0:T(8,128)(2,1)S(1)}, bf16[256,1024]{1,0:T(8,128)(2,1)S(1)}, u32[]{:S(2)}, u32[]{:S(2)}) collective-permute-start(bf16[256,1024]{1,0:T(8,128)(2,1)S(1)} %get-tuple-element.34), channel_id=1, source_target_pairs={{0,2},{2,4},{4,6},{6,8},{8,10},{10,12},{12,14},{14,16},{16,18},{18... | collective-permute-start | bytes 1572872 | tf_op jit(solution)/shard_map/ppermute | solution.py:423
  6.1 35.6 %collective-permute-start = (bf16[256,1024]{1,0:T(8,128)(2,1)S(1)}, bf16[256,1024]{1,0:T(8,128)(2,1)S(1)}, u32[]{:S(2)}, u32[]{:S(2)}) collective-permute-start(bf16[256,1024]{1,0:T(8,128)(2,1)S(1)} %get-tuple-element.34), channel_id=1, source_target_pairs={{0,4},{2,6},{4,8},{6,10},{8,12},{10,14},{12,16},{14,18},{16,20},{1... | collective-permute-start | bytes 1572872 | tf_op jit(solution)/shard_map/ppermute | solution.py:424
  10.7 55.7 %collective-permute-start.7 = (bf16[1024,2048]{1,0:T(8,128)(2,1)}, bf16[1024,2048]{1,0:T(8,128)(2,1)S(1)}, u32[]{:S(2)}, u32[]{:S(2)}) collective-permute-start(bf16[1024,2048]{1,0:T(8,128)(2,1)} %up_own_ref.1), channel_id=1, source_target_pairs={{0,1},{1,0},{2,3},{3,2},{4,5},{5,4},{6,7},{7,6},{8,9},{9,8},{10,11... | collective-permute-start | bytes 12582920 | tf_op jit(solution)/shard_map/ppermute | solution.py:421
  12.6 53.8 %collective-permute-start.8 = (bf16[2048,1024]{1,0:T(8,128)(2,1)}, bf16[2048,1024]{1,0:T(8,128)(2,1)S(1)}, u32[]{:S(2)}, u32[]{:S(2)}) collective-permute-start(bf16[2048,1024]{1,0:T(8,128)(2,1)} %down_own_ref.1), channel_id=1, source_target_pairs={{0,1},{1,0},{2,3},{3,2},{4,5},{5,4},{6,7},{7,6},{8,9},{9,8},{10,11... | collective-permute-start | bytes 12582920 | tf_op jit(solution)/shard_map/ppermute | solution.py:422
  15.1 1.9 %copy-start = (bf16[1024,3,512]{2,0,1:T(8,128)(2,1)S(1)}, bf16[1024,3,512]{2,0,1:T(8,128)(2,1)}, u32[]{:S(2)}) copy-start(bf16[1024,3,512]{2,0,1:T(8,128)(2,1)} %param.17) | copy-start | bytes 9437188
  18.3 18.9 %copy-start.1 = (bf16[1024,3,512]{2,0,1:T(8,128)(2,1)S(1)}, bf16[1024,3,512]{2,0,1:T(8,128)(2,1)}, u32[]{:S(2)}) copy-start(bf16[1024,3,512]{2,0,1:T(8,128)(2,1)} %param.17) | copy-start | bytes 9437188
  31.5 4.5 %collective-permute-start.3 = (bf16[128,1024]{1,0:T(8,128)(2,1)S(1)}, bf16[128,1024]{1,0:T(8,128)(2,1)S(1)}, u32[]{:S(2)}, u32[]{:S(2)}) collective-permute-start(bf16[128,1024]{1,0:T(8,128)(2,1)S(1)} %get-tuple-element.57), channel_id=1, source_target_pairs={{0,1},{1,0},{2,3},{3,2},{4,5},{5,4},{6,7},{7,6},{8,9},{9,8},{10,11... | collective-permute-start | bytes 786440 | tf_op jit(solution)/shard_map/ppermute | solution.py:454
  33.4 12.2 %copy-start.8 = (bf16[512,1024]{1,0:T(8,128)(2,1)S(1)}, bf16[512,1024]{1,0:T(8,128)(2,1)}, u32[]{:S(2)}) copy-start(bf16[512,1024]{1,0:T(8,128)(2,1)} %w_out_ref.3) | copy-start | bytes 3145732
  33.4 3.7 %collective-permute-start.2 = (bf16[128,1024]{1,0:T(8,128)(2,1)S(1)}, bf16[128,1024]{1,0:T(8,128)(2,1)S(1)}, u32[]{:S(2)}, u32[]{:S(2)}) collective-permute-start(bf16[128,1024]{1,0:T(8,128)(2,1)S(1)} %get-tuple-element.58), channel_id=1, source_target_pairs={{0,1},{1,0},{2,3},{3,2},{4,5},{5,4},{6,7},{7,6},{8,9},{9,8},{10,11... | collective-permute-start | bytes 786440 | tf_op jit(solution)/shard_map/ppermute | solution.py:454
  41.7 10.6 %copy-start.5 = (bf16[512,1024]{1,0:T(8,128)(2,1)S(1)}, bf16[512,1024]{1,0:T(8,128)(2,1)}, u32[]{:S(2)}) copy-start(bf16[512,1024]{1,0:T(8,128)(2,1)} %frames_ref.3) | copy-start | bytes 3145732
  41.7 12.2 %copy-start.11 = (f32[1024]{0:T(1024)S(1)}, f32[1024]{0:T(1024)}, u32[]{:S(2)}) copy-start(f32[1024]{0:T(1024)} %param.19) | copy-start | bytes 12292
  41.7 3.9 %collective-permute-start.4 = (bf16[256,1024]{1,0:T(8,128)(2,1)S(1)}, bf16[256,1024]{1,0:T(8,128)(2,1)S(1)}, u32[]{:S(2)}, u32[]{:S(2)}) collective-permute-start(bf16[256,1024]{1,0:T(8,128)(2,1)S(1)} %collective-permute-done.mine_ref), channel_id=1, source_target_pairs={{0,1},{1,0},{2,3},{3,2},{4,5},{5,4},{6,7},{7,6},{8,9},{9,8},{10,11... | collective-permute-start | bytes 1572872 | tf_op jit(solution)/shard_map/ppermute | solution.py:470
  45.6 8.2 %copy-start.6 = (bf16[1024,2048]{1,0:T(8,128)(2,1)S(1)}, bf16[1024,2048]{1,0:T(8,128)(2,1)}, u32[]{:S(2)}) copy-start(bf16[1024,2048]{1,0:T(8,128)(2,1)} %w_ref.1) | copy-start | bytes 12582916
  50.0 3.9 %collective-permute-start.5 = (bf16[272,1024]{1,0:T(8,128)(2,1)S(1)}, bf16[272,1024]{1,0:T(8,128)(2,1)S(1)}, u32[]{:S(2)}, u32[]{:S(2)}) collective-permute-start(bf16[272,1024]{1,0:T(8,128)(2,1)S(1)} %get-tuple-element.51), channel_id=1, source_target_pairs={{0,1},{1,0},{2,3},{3,2},{4,5},{5,4},{6,7},{7,6},{8,9},{9,8},{10,11... | collective-permute-start | bytes 1671176 | tf_op jit(solution)/shard_map/ppermute | solution.py:485
  52.3 8.3 %copy-start.9 = (bf16[31,1024]{1,0:T(8,128)(2,1)S(1)}, bf16[31,1024]{1,0:T(8,128)(2,1)}, u32[]{:S(2)}) copy-start(bf16[31,1024]{1,0:T(8,128)(2,1)} %taps_ref.3) | copy-start | bytes 190468
  52.3 14.1 %copy-start.3 = (bf16[2048,1024]{1,0:T(8,128)(2,1)S(1)}, bf16[2048,1024]{1,0:T(8,128)(2,1)}, u32[]{:S(2)}) copy-start(bf16[2048,1024]{1,0:T(8,128)(2,1)} %down_own_ref.1) | copy-start | bytes 12582916
  52.8 13.6 %copy-start.2 = (bf16[1024,2048]{1,0:T(8,128)(2,1)S(1)}, bf16[1024,2048]{1,0:T(8,128)(2,1)}, u32[]{:S(2)}) copy-start(bf16[1024,2048]{1,0:T(8,128)(2,1)} %up_own_ref.1) | copy-start | bytes 12582916
  52.8 13.6 %copy-start.7 = (bf16[1024,1024]{1,0:T(8,128)(2,1)S(1)}, bf16[1024,1024]{1,0:T(8,128)(2,1)}, u32[]{:S(2)}) copy-start(bf16[1024,1024]{1,0:T(8,128)(2,1)} %w_point_ref.1) | copy-start | bytes 6291460
  52.8 13.6 %copy-start.12 = (f32[1024]{0:T(1024)S(1)}, f32[1024]{0:T(1024)}, u32[]{:S(2)}) copy-start(f32[1024]{0:T(1024)} %param.22) | copy-start | bytes 12292
  52.8 13.6 %copy-start.13 = (f32[1024]{0:T(1024)S(1)}, f32[1024]{0:T(1024)}, u32[]{:S(2)}) copy-start(f32[1024]{0:T(1024)} %param.24) | copy-start | bytes 12292
  52.8 13.6 %copy-start.14 = (f32[1024]{0:T(1024)S(1)}, f32[1024]{0:T(1024)}, u32[]{:S(2)}) copy-start(f32[1024]{0:T(1024)} %param.27) | copy-start | bytes 12292
  55.7 10.7 %collective-permute-start.6 = (bf16[16,1024]{1,0:T(8,128)(2,1)S(1)}, bf16[16,1024]{1,0:T(8,128)(2,1)S(1)}, u32[]{:S(2)}, u32[]{:S(2)}) collective-permute-start(bf16[16,1024]{1,0:T(8,128)(2,1)S(1)} %get-tuple-element.53), channel_id=1, source_target_pairs={{1,2},{3,4},{5,6},{7,8},{9,10},{11,12},{13,14},{15,16},{17,18},{19... | collective-permute-start | bytes 98312 | tf_op jit(solution)/shard_map/ppermute | solution.py:510
  (2 other events, 1.3 us)

commit v6 on v5

--- a/solution.py
+++ b/solution.py
@@ -13,10 +13,16 @@
 EDGE = 16
 MIB = 1 << 20
 EARLY = 0.001
-LATE = 14.5
-MIDDLE = 0.1
+LATE = 13.4
+MIDDLE = 0.001
+ROOMY = 16
+SPARE = 32
 VMEM = pl.BlockSpec(memory_space=pltpu.VMEM)
 HBM = pl.BlockSpec(memory_space=pltpu.HBM)
+
+
+def in_hbm(array):
+    return pltpu.with_memory_space_constraint(array, pltpu.HBM)
 
 
 def params(limit):
@@ -44,55 +50,75 @@
         body(slice(first, first + step))
 
 
-def send_kernel(frames_ref, gain_ref, sent_ref, normed_ref):
+def begin(pairs, sem):
+    copies = [
+        pltpu.make_async_copy(source, target, sem.at[number])
+        for number, (source, target) in enumerate(pairs)
+    ]
+    for copy in copies:
+        copy.start()
+    return copies
+
+
+def send_kernel(frames_ref, gain_ref, sent_ref, far_ref, normed_ref, frames, gain, sem):
     rows = sent_ref.shape[0]
+    parts = [slice(0, rows), slice(rows, 2 * rows)]
+    copies = begin(
+        [(gain_ref, gain)] + [(frames_ref.at[part], frames.at[part]) for part in parts], sem
+    )
 
     def body(part):
-        normed_ref[part] = norm_rows(
-            frames_ref[part].astype(jnp.float32), gain_ref[...]
-        ).astype(jnp.bfloat16)
-
-    each(normed_ref.shape[0], 16, body)
+        normed_ref[part] = norm_rows(frames[part].astype(jnp.float32), gain[...]).astype(
+            jnp.bfloat16
+        )
+
+    copies[0].wait()
+    for copy, whole in zip(copies[1:], parts):
+        copy.wait()
+        for first in range(whole.start, whole.stop, 16):
+            body(slice(first, first + 16))
     first = pl.multiple_of(lax.axis_index("mp") * rows, rows)
-    sent_ref[...] = normed_ref[pl.ds(first, rows)]
-
-
-def own_kernel(normed_ref, w_ref, lengths_ref, context_ref, qkv_ref, flags_ref):
+    half = normed_ref[pl.ds(first, rows)]
+    sent_ref[...] = half
+    far_ref[:rows] = half
+    far_ref[rows:] = half[: far_ref.shape[0] - rows]
+
+
+def own_kernel(
+    normed_ref, w_ref, lengths_ref, context_ref, qkv_ref, flags_ref, w, lengths, context, sem
+):
     rows = normed_ref.shape[0]
-    step = pl.program_id(0)
-
-    @pl.when(step == 0)
-    def _():
-        count = lengths_ref.shape[1]
-        lengths = jnp.broadcast_to(lengths_ref[...], (8, count))
-        before = (
-            lax.broadcasted_iota(jnp.int32, (count, count), 0)
-            < lax.broadcasted_iota(jnp.int32, (count, count), 1)
-        ).astype(jnp.float32).astype(jnp.bfloat16)
-        start = jnp.dot(
-            lengths.astype(jnp.float32).astype(jnp.bfloat16),
-            before,
-            preferred_element_type=jnp.float32,
-        )
-        stretch = (
-            lax.axis_index("tm") * (rows // C)
-            - 2
-            + lax.broadcasted_iota(jnp.int32, (8, count), 0)
-        ).astype(jnp.float32)
-        end = start + lengths.astype(jnp.float32)
-        member = jnp.where((start <= stretch) & (stretch < end), 1.0, 0.0)
-        context = jnp.broadcast_to(context_ref[...], (8, count)).astype(jnp.float32)
-        number = lax.broadcasted_iota(jnp.int32, (8, count), 1).astype(jnp.float32) + 1.0
-        opening = jnp.sum(member * start, axis=1, keepdims=True)
-        reached = jnp.sum(member * context, axis=1, keepdims=True)
-        label = jnp.sum(member * number, axis=1, keepdims=True)
-        flags_ref[0] = jnp.maximum(stretch[:, :LANES] - reached, opening)
-        flags_ref[1] = jnp.broadcast_to(label, (8, LANES))
-
-    scale = jnp.where(step == 0, HD**-0.5, 1.0)
-    qkv_ref[0] = (
-        jnp.dot(normed_ref[...], w_ref[0], preferred_element_type=jnp.float32) * scale
-    ).astype(jnp.bfloat16)
+    copies = begin(
+        [(lengths_ref, lengths), (context_ref, context)]
+        + [(w_ref.at[plane], w.at[plane]) for plane in range(3)],
+        sem,
+    )
+    copies[0].wait()
+    copies[1].wait()
+    count = lengths.shape[1]
+    sizes = jnp.broadcast_to(lengths[...], (8, count)).astype(jnp.float32)
+    before = (
+        lax.broadcasted_iota(jnp.int32, (count, count), 0)
+        < lax.broadcasted_iota(jnp.int32, (count, count), 1)
+    ).astype(jnp.float32).astype(jnp.bfloat16)
+    start = jnp.dot(sizes.astype(jnp.bfloat16), before, preferred_element_type=jnp.float32)
+    stretch = (
+        lax.axis_index("tm") * (rows // C) - 2 + lax.broadcasted_iota(jnp.int32, (8, count), 0)
+    ).astype(jnp.float32)
+    member = jnp.where((start <= stretch) & (stretch < start + sizes), 1.0, 0.0)
+    allowed = jnp.broadcast_to(context[...], (8, count)).astype(jnp.float32)
+    number = lax.broadcasted_iota(jnp.int32, (8, count), 1).astype(jnp.float32) + 1.0
+    opening = jnp.sum(member * start, axis=1, keepdims=True)
+    reached = jnp.sum(member * allowed, axis=1, keepdims=True)
+    label = jnp.sum(member * number, axis=1, keepdims=True)
+    flags_ref[0] = jnp.maximum(stretch[:, :LANES] - reached, opening)
+    flags_ref[1] = jnp.broadcast_to(label, (8, LANES))
+    for plane in range(3):
+        copies[2 + plane].wait()
+        product = jnp.dot(normed_ref[...], w[plane], preferred_element_type=jnp.float32)
+        if plane == 0:
+            product = product * HD**-0.5
+        qkv_ref[plane] = product.astype(jnp.bfloat16)
 
 
 def bias_row(lowest, stretches):
@@ -140,14 +166,11 @@
     return attend_all([query], keys, values, [bias])[0]
 
 
-def place(normed, mine_ref, *theirs_refs):
-    rows = mine_ref.shape[0]
+def place(normed, mine_ref, theirs_ref):
+    rows = normed.shape[0] // 2
     core = lax.axis_index("mp")
-    normed[pl.ds(pl.multiple_of(core * rows, rows), rows)] = mine_ref[...]
-    first = pl.multiple_of((1 - core) * rows, rows)
-    for ref in theirs_refs:
-        normed[pl.ds(first, ref.shape[0])] = ref[...]
-        first = pl.multiple_of(first + ref.shape[0], EDGE)
+    normed[pl.ds(pl.multiple_of(core * rows, rows), rows)] = mine_ref[:rows]
+    normed[pl.ds(pl.multiple_of((1 - core) * rows, rows), rows)] = theirs_ref[:rows]
 
 
 def merged(parts, total, top, weight):
@@ -179,14 +202,14 @@
 
 
 def near_kernel(
-    qkv_ref, mine_ref, first_ref, second_ref, w_ref, flags_ref,
+    qkv_ref, mine_ref, theirs_ref, w_ref, flags_ref,
     own_total_ref, own_top_ref, own_weight_ref,
     total_ref, top_ref, weight_ref,
     normed, keys, values,
 ):
     slab, width = qkv_ref.shape[1:]
     count = slab // C
-    place(normed, mine_ref, first_ref, second_ref)
+    place(normed, mine_ref, theirs_ref)
     keys[...] = jnp.dot(normed[...], w_ref[1], preferred_element_type=jnp.float32).astype(
         jnp.bfloat16
     )
@@ -408,38 +431,44 @@
         return vec.reshape(1, -1)
 
     w_planes = jnp.transpose(w_qkv, (1, 0, 2))
-    sent, normed = pl.pallas_call(
+    sent, sent_far, normed = pl.pallas_call(
         send_kernel,
-        out_shape=(shape((rows, width), bf16), shape((slab, width), bf16)),
-        in_specs=[VMEM] * 2,
-        out_specs=(VMEM,) * 2,
+        out_shape=(
+            shape((rows, width), bf16),
+            shape((rows + SPARE, width), bf16),
+            shape((slab, width), bf16),
+        ),
+        in_specs=[HBM] * 2,
+        out_specs=(VMEM,) * 3,
+        scratch_shapes=[
+            pltpu.VMEM((slab, width), bf16),
+            pltpu.VMEM((1, width), f32),
+            pltpu.SemaphoreType.DMA((3,)),
+        ],
         compiler_params=params(8),
         cost_estimate=cost(0, 2 * rows * width * 2),
         name="send_norm",
-    )(frames, row(gain_attn))
+    )(in_hbm(frames), in_hbm(row(gain_attn)))
     up_held, down_held, sent = lax.optimization_barrier((w_up, w_down, sent))
     up_other = lax.ppermute(up_held, "mp", swap)
     down_other = lax.ppermute(down_held, "mp", swap)
     near_mine = lax.ppermute(sent, "tm", [(i, i + 1) for i in range(tm - 1)])
-    far_mine = lax.ppermute(sent, "tm", [(i, i + 2) for i in range(tm - 2)])
+    far_mine = lax.ppermute(sent_far, "tm", [(i, i + 2) for i in range(tm - 2)])
     qkv, flags = pl.pallas_call(
         own_kernel,
-        grid=(3,),
         out_shape=(shape((3, slab, local), bf16), shape((2, 8, LANES), f32)),
-        in_specs=[
-            pl.BlockSpec((slab, width), lambda i: (0, 0)),
-            pl.BlockSpec((1, width, local), lambda i: (i, 0, 0)),
-            pl.BlockSpec((1, lengths.shape[0]), lambda i: (0, 0)),
-            pl.BlockSpec((1, lengths.shape[0]), lambda i: (0, 0)),
+        in_specs=[VMEM] + [HBM] * 3,
+        out_specs=(VMEM,) * 2,
+        scratch_shapes=[
+            pltpu.VMEM((3, width, local), bf16),
+            pltpu.VMEM((1, lengths.shape[0]), jnp.int32),
+            pltpu.VMEM((1, lengths.shape[0]), jnp.int32),
+            pltpu.SemaphoreType.DMA((5,)),
         ],
-        out_specs=(
-            pl.BlockSpec((1, slab, local), lambda i: (i, 0, 0)),
-            pl.BlockSpec((2, 8, LANES), lambda i: (0, 0, 0)),
-        ),
-        compiler_params=params(16),
+        compiler_params=params(ROOMY),
         cost_estimate=cost(slab * width * 3 * local, width * 3 * local * 2, EARLY),
         name="own_qkv",
-    )(normed, w_planes, row(lengths), row(context))
+    )(normed, in_hbm(w_planes), in_hbm(row(lengths)), in_hbm(row(context)))
     partial = (shape((slab, local), f32),) * 3
     own_parts = pl.pallas_call(
         self_kernel,
@@ -451,11 +480,11 @@
         name="own_attention",
     )(qkv, flags)
     near_mine, own_parts = lax.optimization_barrier((near_mine, own_parts))
-    near_theirs = [lax.ppermute(near_mine[at : at + C], "mp", swap) for at in range(0, rows, C)]
+    near_theirs = lax.ppermute(near_mine, "mp", swap)
     near_parts = pl.pallas_call(
         near_kernel,
         out_shape=partial,
-        in_specs=[VMEM] * 9,
+        in_specs=[VMEM] * 8,
         out_specs=(VMEM,) * 3,
         scratch_shapes=[
             pltpu.VMEM((slab, width), bf16),
@@ -465,7 +494,7 @@
         compiler_params=params(16),
         cost_estimate=cost(slab * width * 2 * local + 8 * slab * slab * local, 8 * MIB, MIDDLE),
         name="near_attention",
-    )(qkv, near_mine, *near_theirs, w_planes, flags, *own_parts)
+    )(qkv, near_mine, near_theirs, w_planes, flags, *own_parts)
     far_mine, near_parts = lax.optimization_barrier((far_mine, near_parts))
     far_theirs = lax.ppermute(far_mine, "mp", swap)
     heads, to_other = pl.pallas_call(

time: 74.1 us -> 71.8 us (0.969)
  local copies, waits for them, and re-layouts: 5.21 us -> 0.07 us
  Pallas kernels: 26.5 us -> 28.8 us
  waiting for transfers between devices: 15.1 us -> 17.4 us
  starting transfers between devices: 26.6 us -> 24.8 us
    unnamed x34 -> x24, local copies, waits for them, and re-layouts: 5.18 us -> 0.07 us
    ppermute x3 -> x2, starting transfers between devices: 9.1 us -> 6.68 us  [the longest x1 4.64 us: on_device(): far_mine = lax.ppermute(sent_far, 'tm', [(i, i + 2) for i in range(tm - 2)])]
    ppermute x1, waiting for transfers between devices: 8.21 us -> 10.3 us  [on_device(): near_mine = lax.ppermute(sent, 'tm', [(i, i + 1) for i in range(tm - 1)])]
    pallas_call x1, Pallas kernels: 0.74 us -> 1.98 us  [on_device(): pl.pallas_call(send_kernel, out_shape=(shape((rows, width), bf16), shape(...]
    ppermute x1, waiting for transfers between devices: 3.44 us -> 2.27 us  [on_device(): lax.ppermute(edge, ('tm', 'mp'), halo_pairs + [(b, a) for a, b in halo_pa...]
    ppermute x1, starting transfers between devices: 4.87 us -> 6.04 us  [on_device(): lax.ppermute(edge, ('tm', 'mp'), halo_pairs + [(b, a) for a, b in halo_pa...]
    pallas_call x2, Pallas kernels: 6.9 us -> 8.01 us  [the longest x1 4.56 us: on_device(): pl.pallas_call(near_kernel, out_shape=partial, in_specs=[VMEM] * 8, out_s...]
    ppermute x3 -> x2, waiting for transfers between devices: 1.13 us -> 1.88 us  [the longest x1 1.88 us: on_device(): near_theirs = lax.ppermute(near_mine, 'mp', swap)]
  transfers between devices with their start and end apart: 9 -> 8, of which waited for: 5 -> 5; matrix products, arithmetic and copies ran while one was open for 0% -> 0% of each run, Pallas kernels for 25% -> 27%
where the time goes in v6:
time: 71.8 us; the launch traced here: 71.4 us
  Pallas kernels  28.8 us (40%)
  starting transfers between devices  24.8 us (35%)
  waiting for transfers between devices  17.4 us (24%)
    ppermute x1, waiting for transfers between devices, on_device(): near_mine = lax.ppermute(sent, 'tm', [(i, i + 1) for i in range(tm - 1)])  10.3 us
    pallas_call x1, Pallas kernels, on_device(): pl.pallas_call(tail_kernel, out_shape=shape((rows, width), bf16), in_spec...  7.22 us
    ppermute x1, starting transfers between devices, on_device(): lax.ppermute(edge, ('tm', 'mp'), halo_pairs + [(b, a) for a, b in halo_pa...  6.04 us
    ppermute x1, starting transfers between devices, on_device(): far_mine = lax.ppermute(sent_far, 'tm', [(i, i + 2) for i in range(tm - 2)])  4.64 us
    pallas_call x1, Pallas kernels, on_device(): pl.pallas_call(near_kernel, out_shape=partial, in_specs=[VMEM] * 8, out_s...  4.56 us
    pallas_call x1, Pallas kernels, on_device(): pl.pallas_call(far_kernel, out_shape=(shape((slab, local), bf16), shape((...  4.38 us
    pallas_call x1, Pallas kernels, on_device(): pl.pallas_call(own_kernel, out_shape=(shape((3, slab, local), bf16), shap...  3.44 us
    ppermute x1, starting transfers between devices, on_device(): near_mine = lax.ppermute(sent, 'tm', [(i, i + 1) for i in range(tm - 1)])  3.4 us
  transfers between devices with their start and end apart: 8, of which 5 were waited for; matrix products, arithmetic and copies ran while one was open for 0% of the time, Pallas kernels for 27%

profile of v6, /device:TPU:256, one launch (start us, length us, event | category | flops | bytes accessed | tf_op | source)
XLA Modules:
  0.0 71.4 jit_solution(6677385538399947305)
XLA Ops:
  0.0 2.0 %send_norm.1 = (bf16[256,1024]{1,0:T(8,128)(2,1)S(1)}, bf16[288,1024]{1,0:T(8,128)(2,1)S(1)}, bf16[512,1024]{1,0:T(8,128)(2,1)S(1)}) custom-call(bf16[512,1024]{1,0:T(8,128)(2,1)} %frames_ref.3, f32[1,1024]{1,0:T(1,128)} %bitcast.15), custom_call_target="tpu_custom_call" | custom-call | bytes 1048576 | tf_op jit(solution)/shard_map/send_norm/pallas_call | solution.py:434
  2.0 3.4 %collective-permute-start.1 = (bf16[256,1024]{1,0:T(8,128)(2,1)S(1)}, bf16[256,1024]{1,0:T(8,128)(2,1)S(1)}, u32[]{:S(2)}, u32[]{:S(2)}) collective-permute-start(bf16[256,1024]{1,0:T(8,128)(2,1)S(1)} %get-tuple-element.36), channel_id=1, source_target_pairs={{0,2},{2,4},{4,6},{6,8},{8,10},{10,12},{12,14},{14,16},{16,18},{18... | collective-permute-start | bytes 1572872 | tf_op jit(solution)/shard_map/ppermute | solution.py:455
  5.4 4.6 %collective-permute-start = (bf16[288,1024]{1,0:T(8,128)(2,1)S(1)}, bf16[288,1024]{1,0:T(8,128)(2,1)S(1)}, u32[]{:S(2)}, u32[]{:S(2)}) collective-permute-start(bf16[288,1024]{1,0:T(8,128)(2,1)S(1)} %get-tuple-element.34), channel_id=1, source_target_pairs={{0,4},{2,6},{4,8},{6,10},{8,12},{10,14},{12,16},{14,18},{16,20},{1... | collective-permute-start | bytes 1769480 | tf_op jit(solution)/shard_map/ppermute | solution.py:456
  10.0 1.9 %collective-permute-start.6 = (bf16[1024,2048]{1,0:T(8,128)(2,1)}, bf16[1024,2048]{1,0:T(8,128)(2,1)S(1)}, u32[]{:S(2)}, u32[]{:S(2)}) collective-permute-start(bf16[1024,2048]{1,0:T(8,128)(2,1)} %up_own_ref.1), channel_id=1, source_target_pairs={{0,1},{1,0},{2,3},{3,2},{4,5},{5,4},{6,7},{7,6},{8,9},{9,8},{10,11... | collective-permute-start | bytes 12582920 | tf_op jit(solution)/shard_map/ppermute | solution.py:453
  12.0 2.4 %collective-permute-start.7 = (bf16[2048,1024]{1,0:T(8,128)(2,1)}, bf16[2048,1024]{1,0:T(8,128)(2,1)S(1)}, u32[]{:S(2)}, u32[]{:S(2)}) collective-permute-start(bf16[2048,1024]{1,0:T(8,128)(2,1)} %down_own_ref.1), channel_id=1, source_target_pairs={{0,1},{1,0},{2,3},{3,2},{4,5},{5,4},{6,7},{7,6},{8,9},{9,8},{10,11... | collective-permute-start | bytes 12582920 | tf_op jit(solution)/shard_map/ppermute | solution.py:454
  14.4 3.4 %own_qkv.1 = (bf16[3,512,512]{2,1,0:T(8,128)(2,1)S(1)}, f32[2,8,128]{2,1,0:T(8,128)S(1)}) custom-call(bf16[512,1024]{1,0:T(8,128)(2,1)S(1)} %get-tuple-element.32.normed_ref, bf16[3,1024,512]{2,1,0:T(8,128)(2,1)} %bitcast.8, s32[1,128]{1,0:T(1,128)} %bitcast.16, s32[1,128]{1,0:T(1,128)} %bitcast.17), custom_call_target="tpu_custom_call" | custom-call | flops 1610612 | bytes 3145 | tf_op jit(solution)/shard_map/own_qkv/pallas_call | solution.py:457
  17.8 2.6 %own_attention.1 = (f32[512,512]{1,0:T(8,128)S(1)}, f32[512,512]{1,0:T(8,128)S(1)}, f32[512,512]{1,0:T(8,128)S(1)}) custom-call(bf16[3,512,512]{2,1,0:T(8,128)(2,1)S(1)} %get-tuple-element.33.qkv_ref, f32[2,8,128]{2,1,0:T(8,128)S(1)} %get-tuple-element.37.flags_ref), custom_call_target="tpu_custom_call" | custom-call | flops 1342177 | bytes 4194 | tf_op jit(solution)/shard_map/own_attention/pallas_call | solution.py:473
  20.4 10.3 %collective-permute-done.1.mine_ref = bf16[256,1024]{1,0:T(8,128)(2,1)S(1)} collective-permute-done((bf16[256,1024]{1,0:T(8,128)(2,1)S(1)}, bf16[256,1024]{1,0:T(8,128)(2,1)S(1)}, u32[]{:S(2)}, u32[]{:S(2)}) %collective-permute-start.1) | collective-permute-done | bytes 524320 | tf_op jit(solution)/shard_map/ppermute | solution.py:455
  30.8 2.0 %collective-permute-start.2 = (bf16[256,1024]{1,0:T(8,128)(2,1)S(1)}, bf16[256,1024]{1,0:T(8,128)(2,1)S(1)}, u32[]{:S(2)}, u32[]{:S(2)}) collective-permute-start(bf16[256,1024]{1,0:T(8,128)(2,1)S(1)} %collective-permute-done.1.mine_ref), channel_id=1, source_target_pairs={{0,1},{1,0},{2,3},{3,2},{4,5},{5,4},{6,7},{7,6},{8,9},{9,8},{10,11... | collective-permute-start | bytes 1572872 | tf_op jit(solution)/shard_map/ppermute | solution.py:483
  32.8 1.9 %collective-permute-done.2.theirs_ref = bf16[256,1024]{1,0:T(8,128)(2,1)S(1)} collective-permute-done((bf16[256,1024]{1,0:T(8,128)(2,1)S(1)}, bf16[256,1024]{1,0:T(8,128)(2,1)S(1)}, u32[]{:S(2)}, u32[]{:S(2)}) %collective-permute-start.2) | collective-permute-done | bytes 524320 | tf_op jit(solution)/shard_map/ppermute | solution.py:483
  34.7 4.6 %near_attention.1 = (f32[512,512]{1,0:T(8,128)S(1)}, f32[512,512]{1,0:T(8,128)S(1)}, f32[512,512]{1,0:T(8,128)S(1)}) custom-call(bf16[3,512,512]{2,1,0:T(8,128)(2,1)S(1)} %get-tuple-element.33.qkv_ref, bf16[256,1024]{1,0:T(8,128)(2,1)S(1)} %collective-permute-done.1.mine_ref, bf16[256,1024]{1,0:T(8,128)(2,1)S(1)} %collective-permute-done.2.theirs_ref, ...), custom_call_target="tpu_custom_call" | custom-call | flops 3221225 | bytes 8388 | tf_op jit(solution)/shard_map/near_attention/pallas_call | solution.py:484
  39.3 0.0 copy-start.3
  39.3 2.3 %collective-permute-start.3 = (bf16[288,1024]{1,0:T(8,128)(2,1)S(1)}, bf16[288,1024]{1,0:T(8,128)(2,1)S(1)}, u32[]{:S(2)}, u32[]{:S(2)}) collective-permute-start(bf16[288,1024]{1,0:T(8,128)(2,1)S(1)} %collective-permute-done.mine_ref), channel_id=1, source_target_pairs={{0,1},{1,0},{2,3},{3,2},{4,5},{5,4},{6,7},{7,6},{8,9},{9,8},{10,11... | collective-permute-start | bytes 1769480 | tf_op jit(solution)/shard_map/ppermute | solution.py:499
  41.7 1.7 %collective-permute-done.3.theirs_ref = bf16[288,1024]{1,0:T(8,128)(2,1)S(1)} collective-permute-done((bf16[288,1024]{1,0:T(8,128)(2,1)S(1)}, bf16[288,1024]{1,0:T(8,128)(2,1)S(1)}, u32[]{:S(2)}, u32[]{:S(2)}) %collective-permute-start.3) | collective-permute-done | bytes 589856 | tf_op jit(solution)/shard_map/ppermute | solution.py:499
  43.4 4.4 %far_attention.1 = (bf16[512,512]{1,0:T(8,128)(2,1)S(1)}, bf16[272,1024]{1,0:T(8,128)(2,1)S(1)}) custom-call(bf16[3,512,512]{2,1,0:T(8,128)(2,1)S(1)} %get-tuple-element.33.qkv_ref, bf16[288,1024]{1,0:T(8,128)(2,1)S(1)} %collective-permute-done.mine_ref, bf16[288,1024]{1,0:T(8,128)(2,1)S(1)} %collective-permute-done.3.theirs_ref, ...), custom_call_target="tpu_custom_call" | custom-call | flops 25179246592 | bytes 140509184 | tf_op jit(solution)/shard_map/far_attention/pallas_call | solution.py:500
  47.7 2.0 %collective-permute-start.4 = (bf16[272,1024]{1,0:T(8,128)(2,1)S(1)}, bf16[272,1024]{1,0:T(8,128)(2,1)S(1)}, u32[]{:S(2)}, u32[]{:S(2)}) collective-permute-start(bf16[272,1024]{1,0:T(8,128)(2,1)S(1)} %get-tuple-element.53), channel_id=1, source_target_pairs={{0,1},{1,0},{2,3},{3,2},{4,5},{5,4},{6,7},{7,6},{8,9},{9,8},{10,11... | collective-permute-start | bytes 1671176 | tf_op jit(solution)/shard_map/ppermute | solution.py:514
  49.8 0.0 copy-start.2
  49.8 0.5 out_projection.1.base_ref
  50.4 1.2 %collective-permute-done.4.got_ref = bf16[272,1024]{1,0:T(8,128)(2,1)S(1)} collective-permute-done((bf16[272,1024]{1,0:T(8,128)(2,1)S(1)}, bf16[272,1024]{1,0:T(8,128)(2,1)S(1)}, u32[]{:S(2)}, u32[]{:S(2)}) %collective-permute-start.4) | collective-permute-done | bytes 557088 | tf_op jit(solution)/shard_map/ppermute | solution.py:514
  51.6 1.8 %gated_units.1 = (bf16[272,1024]{1,0:T(8,128)(2,1)S(1)}, bf16[16,1024]{1,0:T(8,128)(2,1)S(1)}, f32[256,1024]{1,0:T(8,128)S(1)}) custom-call(f32[272,1024]{1,0:T(8,128)S(1)} %out_projection.1.base_ref, bf16[272,1024]{1,0:T(8,128)(2,1)S(1)} %collective-permute-done.4.got_ref, f32[1,1024]{1,0:T(1,128)S(1)} %bitcast.11, bf16[1024,2048]{1,0:T(8,128)(2,1)S(1)} %copy-done.4), custom_call_target="tpu_custom_call" | custom-call | flops 1140850688 | bytes 5242880 | tf_op jit(solution)/shard_map/gated_units/pallas_call | solution.py:524
  53.4 6.0 %collective-permute-start.5 = (bf16[16,1024]{1,0:T(8,128)(2,1)S(1)}, bf16[16,1024]{1,0:T(8,128)(2,1)S(1)}, u32[]{:S(2)}, u32[]{:S(2)}) collective-permute-start(bf16[16,1024]{1,0:T(8,128)(2,1)S(1)} %get-tuple-element.55), channel_id=1, source_target_pairs={{1,2},{3,4},{5,6},{7,8},{9,10},{11,12},{13,14},{15,16},{17,18},{19... | collective-permute-start | bytes 98312 | tf_op jit(solution)/shard_map/ppermute | solution.py:539
  59.5 2.3 %depthwise.1.sum_ref = f32[256,1024]{1,0:T(8,128)S(1)} custom-call(bf16[272,1024]{1,0:T(8,128)(2,1)S(1)} %get-tuple-element.54.gated_ref, bf16[31,1024]{1,0:T(8,128)(2,1)S(1)} %copy-done.7, f32[2,8,128]{2,1,0:T(8,128)S(1)} %get-tuple-element.37.flags_ref), custom_call_target="tpu_custom_call" | custom-call | flops 268435456 | bytes 1048576 | tf_op jit(solution)/shard_map/depthwise/pallas_call | solution.py:540
  61.8 2.3 %collective-permute-done.5.halo_ref = bf16[16,1024]{1,0:T(8,128)(2,1)S(1)} collective-permute-done((bf16[16,1024]{1,0:T(8,128)(2,1)S(1)}, bf16[16,1024]{1,0:T(8,128)(2,1)S(1)}, u32[]{:S(2)}, u32[]{:S(2)}) %collective-permute-start.5) | collective-permute-done | bytes 32800 | tf_op jit(solution)/shard_map/ppermute | solution.py:539
  64.2 7.2 %tail.1 = bf16[256,1024]{1,0:T(8,128)(2,1)} custom-call(f32[256,1024]{1,0:T(8,128)S(1)} %depthwise.1.sum_ref, bf16[16,1024]{1,0:T(8,128)(2,1)S(1)} %collective-permute-done.5.halo_ref, bf16[31,1024]{1,0:T(8,128)(2,1)S(1)} %copy-done.7, f32[2,8,128]{2,1,0:T(8,128)S(1)} %get-tuple-element.37.flags_ref, f32[256,1024]{1,0:T(8,128)S(1)} %get-tuple-element.56.first_ref, ...), custom_call_target="tpu_custom_call" | custom-call | flops 4831838208 | bytes 18874368 | tf_op jit(solution)/shard_map/tail/pallas_call | solution.py:553
  (25 shorter events, 0.1 us)
Async XLA Ops:
  0.0 34.7 %copy-start = (bf16[1024,3,512]{2,0,1:T(8,128)(2,1)S(1)}, bf16[1024,3,512]{2,0,1:T(8,128)(2,1)}, u32[]{:S(2)}) copy-start(bf16[1024,3,512]{2,0,1:T(8,128)(2,1)} %param.17) | copy-start | bytes 9437188
  2.0 28.8 %collective-permute-start.1 = (bf16[256,1024]{1,0:T(8,128)(2,1)S(1)}, bf16[256,1024]{1,0:T(8,128)(2,1)S(1)}, u32[]{:S(2)}, u32[]{:S(2)}) collective-permute-start(bf16[256,1024]{1,0:T(8,128)(2,1)S(1)} %get-tuple-element.36), channel_id=1, source_target_pairs={{0,2},{2,4},{4,6},{6,8},{8,10},{10,12},{12,14},{14,16},{16,18},{18... | collective-permute-start | bytes 1572872 | tf_op jit(solution)/shard_map/ppermute | solution.py:455
  5.4 33.9 %collective-permute-start = (bf16[288,1024]{1,0:T(8,128)(2,1)S(1)}, bf16[288,1024]{1,0:T(8,128)(2,1)S(1)}, u32[]{:S(2)}, u32[]{:S(2)}) collective-permute-start(bf16[288,1024]{1,0:T(8,128)(2,1)S(1)} %get-tuple-element.34), channel_id=1, source_target_pairs={{0,4},{2,6},{4,8},{6,10},{8,12},{10,14},{12,16},{14,18},{16,20},{1... | collective-permute-start | bytes 1769480 | tf_op jit(solution)/shard_map/ppermute | solution.py:456
  10.0 54.1 %collective-permute-start.6 = (bf16[1024,2048]{1,0:T(8,128)(2,1)}, bf16[1024,2048]{1,0:T(8,128)(2,1)S(1)}, u32[]{:S(2)}, u32[]{:S(2)}) collective-permute-start(bf16[1024,2048]{1,0:T(8,128)(2,1)} %up_own_ref.1), channel_id=1, source_target_pairs={{0,1},{1,0},{2,3},{3,2},{4,5},{5,4},{6,7},{7,6},{8,9},{9,8},{10,11... | collective-permute-start | bytes 12582920 | tf_op jit(solution)/shard_map/ppermute | solution.py:453
  12.0 52.1 %collective-permute-start.7 = (bf16[2048,1024]{1,0:T(8,128)(2,1)}, bf16[2048,1024]{1,0:T(8,128)(2,1)S(1)}, u32[]{:S(2)}, u32[]{:S(2)}) collective-permute-start(bf16[2048,1024]{1,0:T(8,128)(2,1)} %down_own_ref.1), channel_id=1, source_target_pairs={{0,1},{1,0},{2,3},{3,2},{4,5},{5,4},{6,7},{7,6},{8,9},{9,8},{10,11... | collective-permute-start | bytes 12582920 | tf_op jit(solution)/shard_map/ppermute | solution.py:454
  30.8 12.6 %copy-start.6 = (bf16[512,1024]{1,0:T(8,128)(2,1)S(1)}, bf16[512,1024]{1,0:T(8,128)(2,1)}, u32[]{:S(2)}) copy-start(bf16[512,1024]{1,0:T(8,128)(2,1)} %w_out_ref.3) | copy-start | bytes 3145732
  30.8 3.9 %collective-permute-start.2 = (bf16[256,1024]{1,0:T(8,128)(2,1)S(1)}, bf16[256,1024]{1,0:T(8,128)(2,1)S(1)}, u32[]{:S(2)}, u32[]{:S(2)}) collective-permute-start(bf16[256,1024]{1,0:T(8,128)(2,1)S(1)} %collective-permute-done.1.mine_ref), channel_id=1, source_target_pairs={{0,1},{1,0},{2,3},{3,2},{4,5},{5,4},{6,7},{7,6},{8,9},{9,8},{10,11... | collective-permute-start | bytes 1572872 | tf_op jit(solution)/shard_map/ppermute | solution.py:483
  39.3 10.5 %copy-start.3 = (bf16[512,1024]{1,0:T(8,128)(2,1)S(1)}, bf16[512,1024]{1,0:T(8,128)(2,1)}, u32[]{:S(2)}) copy-start(bf16[512,1024]{1,0:T(8,128)(2,1)} %frames_ref.3) | copy-start | bytes 3145732
  39.3 12.3 %copy-start.8 = (f32[1024]{0:T(1024)S(1)}, f32[1024]{0:T(1024)}, u32[]{:S(2)}) copy-start(f32[1024]{0:T(1024)} %param.19) | copy-start | bytes 12292
  39.3 4.0 %collective-permute-start.3 = (bf16[288,1024]{1,0:T(8,128)(2,1)S(1)}, bf16[288,1024]{1,0:T(8,128)(2,1)S(1)}, u32[]{:S(2)}, u32[]{:S(2)}) collective-permute-start(bf16[288,1024]{1,0:T(8,128)(2,1)S(1)} %collective-permute-done.mine_ref), channel_id=1, source_target_pairs={{0,1},{1,0},{2,3},{3,2},{4,5},{5,4},{6,7},{7,6},{8,9},{9,8},{10,11... | collective-permute-start | bytes 1769480 | tf_op jit(solution)/shard_map/ppermute | solution.py:499
  43.4 8.2 %copy-start.4 = (bf16[1024,2048]{1,0:T(8,128)(2,1)S(1)}, bf16[1024,2048]{1,0:T(8,128)(2,1)}, u32[]{:S(2)}) copy-start(bf16[1024,2048]{1,0:T(8,128)(2,1)} %w_ref.1) | copy-start | bytes 12582916
  47.7 3.9 %collective-permute-start.4 = (bf16[272,1024]{1,0:T(8,128)(2,1)S(1)}, bf16[272,1024]{1,0:T(8,128)(2,1)S(1)}, u32[]{:S(2)}, u32[]{:S(2)}) collective-permute-start(bf16[272,1024]{1,0:T(8,128)(2,1)S(1)} %get-tuple-element.53), channel_id=1, source_target_pairs={{0,1},{1,0},{2,3},{3,2},{4,5},{5,4},{6,7},{7,6},{8,9},{9,8},{10,11... | collective-permute-start | bytes 1671176 | tf_op jit(solution)/shard_map/ppermute | solution.py:514
  49.8 9.7 %copy-start.7 = (bf16[31,1024]{1,0:T(8,128)(2,1)S(1)}, bf16[31,1024]{1,0:T(8,128)(2,1)}, u32[]{:S(2)}) copy-start(bf16[31,1024]{1,0:T(8,128)(2,1)} %taps_ref.3) | copy-start | bytes 190468
  49.8 14.3 %copy-start.2 = (bf16[2048,1024]{1,0:T(8,128)(2,1)S(1)}, bf16[2048,1024]{1,0:T(8,128)(2,1)}, u32[]{:S(2)}) copy-start(bf16[2048,1024]{1,0:T(8,128)(2,1)} %down_own_ref.1) | copy-start | bytes 12582916
  50.3 13.8 %copy-start.1 = (bf16[1024,2048]{1,0:T(8,128)(2,1)S(1)}, bf16[1024,2048]{1,0:T(8,128)(2,1)}, u32[]{:S(2)}) copy-start(bf16[1024,2048]{1,0:T(8,128)(2,1)} %up_own_ref.1) | copy-start | bytes 12582916
  50.3 13.8 %copy-start.5 = (bf16[1024,1024]{1,0:T(8,128)(2,1)S(1)}, bf16[1024,1024]{1,0:T(8,128)(2,1)}, u32[]{:S(2)}) copy-start(bf16[1024,1024]{1,0:T(8,128)(2,1)} %w_point_ref.1) | copy-start | bytes 6291460
  50.3 13.8 %copy-start.9 = (f32[1024]{0:T(1024)S(1)}, f32[1024]{0:T(1024)}, u32[]{:S(2)}) copy-start(f32[1024]{0:T(1024)} %param.22) | copy-start | bytes 12292
  50.3 13.8 %copy-start.10 = (f32[1024]{0:T(1024)S(1)}, f32[1024]{0:T(1024)}, u32[]{:S(2)}) copy-start(f32[1024]{0:T(1024)} %param.24) | copy-start | bytes 12292
  50.3 13.8 %copy-start.11 = (f32[1024]{0:T(1024)S(1)}, f32[1024]{0:T(1024)}, u32[]{:S(2)}) copy-start(f32[1024]{0:T(1024)} %param.27) | copy-start | bytes 12292
  53.4 10.7 %collective-permute-start.5 = (bf16[16,1024]{1,0:T(8,128)(2,1)S(1)}, bf16[16,1024]{1,0:T(8,128)(2,1)S(1)}, u32[]{:S(2)}, u32[]{:S(2)}) collective-permute-start(bf16[16,1024]{1,0:T(8,128)(2,1)S(1)} %get-tuple-element.55), channel_id=1, source_target_pairs={{1,2},{3,4},{5,6},{7,8},{9,10},{11,12},{13,14},{15,16},{17,18},{19... | collective-permute-start | bytes 98312 | tf_op jit(solution)/shard_map/ppermute | solution.py:539

commit v7 on v6

--- a/solution.py
+++ b/solution.py
@@ -1,3 +1,5 @@
+import functools
+
 import jax
 import jax.numpy as jnp
 from jax import lax
@@ -166,13 +168,6 @@
     return attend_all([query], keys, values, [bias])[0]
 
 
-def place(normed, mine_ref, theirs_ref):
-    rows = normed.shape[0] // 2
-    core = lax.axis_index("mp")
-    normed[pl.ds(pl.multiple_of(core * rows, rows), rows)] = mine_ref[:rows]
-    normed[pl.ds(pl.multiple_of((1 - core) * rows, rows), rows)] = theirs_ref[:rows]
-
-
 def merged(parts, total, top, weight):
     other_total, other_top, other_weight = parts
     highest = jnp.maximum(other_top, top)
@@ -202,23 +197,24 @@
 
 
 def near_kernel(
-    qkv_ref, mine_ref, theirs_ref, w_ref, flags_ref,
-    own_total_ref, own_top_ref, own_weight_ref,
+    theirs, qkv_ref, rows_ref, w_ref, flags_ref, own_total_ref, own_top_ref, own_weight_ref,
     total_ref, top_ref, weight_ref,
-    normed, keys, values,
+    keys, values,
 ):
     slab, width = qkv_ref.shape[1:]
     count = slab // C
-    place(normed, mine_ref, theirs_ref)
-    keys[...] = jnp.dot(normed[...], w_ref[1], preferred_element_type=jnp.float32).astype(
+    here = rows_ref.shape[0] // C
+    keys[...] = jnp.dot(rows_ref[...], w_ref[1], preferred_element_type=jnp.float32).astype(
         jnp.bfloat16
     )
-    values[...] = jnp.dot(normed[...], w_ref[2], preferred_element_type=jnp.float32).astype(
+    values[...] = jnp.dot(rows_ref[...], w_ref[2], preferred_element_type=jnp.float32).astype(
         jnp.bfloat16
     )
-    first = lax.axis_index("tm") * count - count
+    core = lax.axis_index("mp")
+    half = 1 - core if theirs else core
+    first = lax.axis_index("tm") * count - count + half * here
     every = [slice(i * C, (i + 1) * C) for i in range(count)]
-    seen = [(first + n).astype(jnp.float32) for n in range(count)]
+    seen = [(first + n).astype(jnp.float32) for n in range(here)]
     biases = [bias_row(flags_ref[0, 2 + i : 3 + i, :], seen) for i in range(count)]
     for pair in range(width // LANES):
         cols = slice(pair * LANES, (pair + 1) * LANES)
@@ -232,32 +228,65 @@
             )
 
 
-def far_kernel(
-    qkv_ref, mine_ref, theirs_ref, w_ref, flags_ref, total_ref, top_ref, weight_ref, w_out_ref,
-    heads_ref, sent_ref, normed, keys, values,
-):
+def far_half(theirs, qkv_ref, rows_ref, w_ref, flags_ref, parts_refs, keys, values, put):
     slab, width = qkv_ref.shape[1:]
     count = slab // C
-    place(normed, mine_ref, theirs_ref)
-    keys[...] = jnp.dot(normed[...], w_ref[1], preferred_element_type=jnp.float32).astype(
-        jnp.bfloat16
-    )
-    values[...] = jnp.dot(normed[...], w_ref[2], preferred_element_type=jnp.float32).astype(
-        jnp.bfloat16
-    )
+    here = keys.shape[0] // C
+    keys[...] = jnp.dot(
+        rows_ref[: here * C], w_ref[1], preferred_element_type=jnp.float32
+    ).astype(jnp.bfloat16)
+    values[...] = jnp.dot(
+        rows_ref[: here * C], w_ref[2], preferred_element_type=jnp.float32
+    ).astype(jnp.bfloat16)
+    core = lax.axis_index("mp")
+    half = 1 - core if theirs else core
     first = lax.axis_index("tm") * count - 2 * count
-    for i in range(count):
-        rows = slice(i * C, (i + 1) * C)
-        lowest = flags_ref[0, 2 + i : 3 + i, :]
-        bias = bias_row(lowest, [(first + n).astype(jnp.float32) for n in range(i, count)])
-        for pair in range(width // LANES):
-            cols = slice(pair * LANES, (pair + 1) * LANES)
-            total, top, weight = attend(
-                qkv_ref[0, rows, cols], keys[i * C :, cols], values[i * C :, cols], bias
-            )
-            parts = total_ref[rows, cols], top_ref[rows, cols], weight_ref[rows, cols]
-            total, _, weight = merged(parts, total, top, weight)
-            heads_ref[rows, cols] = (total / weight).astype(jnp.bfloat16)
+
+    def work(side):
+        for i in range(count):
+            rows = slice(i * C, (i + 1) * C)
+            skip = max(0, i - side * here)
+            seen = slice(skip * C, here * C)
+            lowest = flags_ref[0, 2 + i : 3 + i, :]
+            stretches = range(side * here + skip, (side + 1) * here)
+            for pair in range(width // LANES):
+                cols = slice(pair * LANES, (pair + 1) * LANES)
+                parts = tuple(ref[rows, cols] for ref in parts_refs)
+                if stretches:
+                    bias = bias_row(lowest, [(first + n).astype(jnp.float32) for n in stretches])
+                    found = attend(qkv_ref[0, rows, cols], keys[seen, cols], values[seen, cols], bias)
+                    parts = merged(parts, *found)
+                put(rows, cols, parts)
+
+    for side in range(2):
+        pl.when(half == side)(functools.partial(work, side))
+
+
+def far_mine_kernel(
+    qkv_ref, rows_ref, w_ref, flags_ref, near_total_ref, near_top_ref, near_weight_ref,
+    total_ref, top_ref, weight_ref,
+    keys, values,
+):
+    def put(rows, cols, parts):
+        total_ref[rows, cols], top_ref[rows, cols], weight_ref[rows, cols] = parts
+
+    near_refs = near_total_ref, near_top_ref, near_weight_ref
+    far_half(False, qkv_ref, rows_ref, w_ref, flags_ref, near_refs, keys, values, put)
+
+
+def far_theirs_kernel(
+    qkv_ref, rows_ref, w_ref, flags_ref, total_ref, top_ref, weight_ref, w_out_ref,
+    heads_ref, sent_ref,
+    keys, values,
+):
+    slab = qkv_ref.shape[1]
+
+    def put(rows, cols, parts):
+        total, _, weight = parts
+        heads_ref[rows, cols] = (total / weight).astype(jnp.bfloat16)
+
+    parts_refs = total_ref, top_ref, weight_ref
+    far_half(True, qkv_ref, rows_ref, w_ref, flags_ref, parts_refs, keys, values, put)
     window = sent_ref.shape[0]
     other = (1 - lax.axis_index("mp")) * (slab - window)
     sent_ref[...] = jnp.dot(
@@ -481,36 +510,46 @@
     )(qkv, flags)
     near_mine, own_parts = lax.optimization_barrier((near_mine, own_parts))
     near_theirs = lax.ppermute(near_mine, "mp", swap)
-    near_parts = pl.pallas_call(
-        near_kernel,
-        out_shape=partial,
-        in_specs=[VMEM] * 8,
-        out_specs=(VMEM,) * 3,
-        scratch_shapes=[
-            pltpu.VMEM((slab, width), bf16),
-            pltpu.VMEM((slab, local), bf16),
-            pltpu.VMEM((slab, local), bf16),
-        ],
-        compiler_params=params(16),
-        cost_estimate=cost(slab * width * 2 * local + 8 * slab * slab * local, 8 * MIB, MIDDLE),
-        name="near_attention",
-    )(qkv, near_mine, near_theirs, w_planes, flags, *own_parts)
+    near_parts = own_parts
+    for theirs, part in enumerate((near_mine, near_theirs)):
+        near_parts = pl.pallas_call(
+            functools.partial(near_kernel, bool(theirs)),
+            out_shape=partial,
+            in_specs=[VMEM] * 7,
+            out_specs=(VMEM,) * 3,
+            scratch_shapes=[
+                pltpu.VMEM((rows, local), bf16),
+                pltpu.VMEM((rows, local), bf16),
+            ],
+            compiler_params=params(16),
+            cost_estimate=cost(
+                slab * width * local + 4 * slab * slab * local, 8 * MIB, MIDDLE
+            ),
+            name="near_theirs" if theirs else "near_mine",
+        )(qkv, part, w_planes, flags, *near_parts)
     far_mine, near_parts = lax.optimization_barrier((far_mine, near_parts))
     far_theirs = lax.ppermute(far_mine, "mp", swap)
+    halves = [pltpu.VMEM((rows, local), bf16)] * 2
+    far_parts = pl.pallas_call(
+        far_mine_kernel,
+        out_shape=partial,
+        in_specs=[VMEM] * 7,
+        out_specs=(VMEM,) * 3,
+        scratch_shapes=halves,
+        compiler_params=params(16),
+        cost_estimate=cost(slab * width * local + 2 * slab * slab * local, 8 * MIB, MIDDLE),
+        name="far_mine",
+    )(qkv, far_mine, w_planes, flags, *near_parts)
     heads, to_other = pl.pallas_call(
-        far_kernel,
+        far_theirs_kernel,
         out_shape=(shape((slab, local), bf16), shape((window, width), bf16)),
-        in_specs=[VMEM] * 9,
+        in_specs=[VMEM] * 8,
         out_specs=(VMEM,) * 2,
-        scratch_shapes=[
-            pltpu.VMEM((slab, width), bf16),
-            pltpu.VMEM((slab, local), bf16),
-            pltpu.VMEM((slab, local), bf16),
-        ],
+        scratch_shapes=halves,
         compiler_params=params(16),
         cost_estimate=cost(slab * width * 2 * local + 3 * slab * slab * local, 10 * MIB, LATE),
-        name="far_attention",
-    )(qkv, far_mine, far_theirs, w_planes, flags, *near_parts, w_out)
+        name="far_theirs",
+    )(qkv, far_theirs, w_planes, flags, *far_parts, w_out)
     from_other = lax.ppermute(to_other, "mp", swap)
     base = pl.pallas_call(
         base_kernel,

time: 71.8 us -> 69.3 us (0.965)
  waiting for transfers between devices: 17.4 us -> 14 us
  Pallas kernels: 28.8 us -> 29.8 us
    ppermute x1, waiting for transfers between devices: 1.88 us -> 0.01 us  [on_device(): near_theirs = lax.ppermute(near_mine, 'mp', swap)]
    ppermute x1, waiting for transfers between devices: 1.67 us -> 0.01 us  [on_device(): far_theirs = lax.ppermute(far_mine, 'mp', swap)]
    pallas_call x2 -> x4, Pallas kernels: 8.94 us -> 9.91 us  [the longest x2 4.67 us: on_device(): pl.pallas_call(functools.partial(near_kernel, bool(theirs)), out_shape=pa...]
  transfers between devices with their start and end apart: 8 -> 8, of which waited for: 5 -> 3; matrix products, arithmetic and copies ran while one was open for 0% -> 0% of each run, Pallas kernels for 27% -> 30%
where the time goes in v7:
time: 69.3 us; the launch traced here: 69 us
  Pallas kernels  29.8 us (43%)
  starting transfers between devices  24.8 us (36%)
  waiting for transfers between devices  14 us (20%)
    ppermute x1, waiting for transfers between devices, on_device(): near_mine = lax.ppermute(sent, 'tm', [(i, i + 1) for i in range(tm - 1)])  10.3 us
    pallas_call x1, Pallas kernels, on_device(): pl.pallas_call(tail_kernel, out_shape=shape((rows, width), bf16), in_spec...  7.23 us
    ppermute x1, starting transfers between devices, on_device(): lax.ppermute(edge, ('tm', 'mp'), halo_pairs + [(b, a) for a, b in halo_pa...  6.04 us
    pallas_call x2, Pallas kernels, on_device(): pl.pallas_call(functools.partial(near_kernel, bool(theirs)), out_shape=pa...  4.67 us
    ppermute x1, starting transfers between devices, on_device(): far_mine = lax.ppermute(sent_far, 'tm', [(i, i + 2) for i in range(tm - 2)])  4.64 us
    pallas_call x1, Pallas kernels, on_device(): pl.pallas_call(own_kernel, out_shape=(shape((3, slab, local), bf16), shap...  3.44 us
    ppermute x1, starting transfers between devices, on_device(): near_mine = lax.ppermute(sent, 'tm', [(i, i + 1) for i in range(tm - 1)])  3.4 us
    pallas_call x1, Pallas kernels, on_device(): pl.pallas_call(far_theirs_kernel, out_shape=(shape((slab, local), bf16),...  3.15 us
  transfers between devices with their start and end apart: 8, of which 3 were waited for; matrix products, arithmetic and copies ran while one was open for 0% of the time, Pallas kernels for 30%

profile of v7, /device:TPU:256, one launch (start us, length us, event | category | flops | bytes accessed | tf_op | source)
XLA Modules:
  0.0 69.0 jit_solution(2907624383478790035)
XLA Ops:
  0.0 2.0 %send_norm.1 = (bf16[256,1024]{1,0:T(8,128)(2,1)S(1)}, bf16[288,1024]{1,0:T(8,128)(2,1)S(1)}, bf16[512,1024]{1,0:T(8,128)(2,1)S(1)}) custom-call(bf16[512,1024]{1,0:T(8,128)(2,1)} %frames_ref.3, f32[1,1024]{1,0:T(1,128)} %bitcast.17), custom_call_target="tpu_custom_call" | custom-call | bytes 1048576 | tf_op jit(solution)/shard_map/send_norm/pallas_call | solution.py:463
  2.0 3.4 %collective-permute-start.1 = (bf16[256,1024]{1,0:T(8,128)(2,1)S(1)}, bf16[256,1024]{1,0:T(8,128)(2,1)S(1)}, u32[]{:S(2)}, u32[]{:S(2)}) collective-permute-start(bf16[256,1024]{1,0:T(8,128)(2,1)S(1)} %get-tuple-element.42), channel_id=1, source_target_pairs={{0,2},{2,4},{4,6},{6,8},{8,10},{10,12},{12,14},{14,16},{16,18},{18... | collective-permute-start | bytes 1572872 | tf_op jit(solution)/shard_map/ppermute | solution.py:484
  5.4 4.6 %collective-permute-start = (bf16[288,1024]{1,0:T(8,128)(2,1)S(1)}, bf16[288,1024]{1,0:T(8,128)(2,1)S(1)}, u32[]{:S(2)}, u32[]{:S(2)}) collective-permute-start(bf16[288,1024]{1,0:T(8,128)(2,1)S(1)} %get-tuple-element.40), channel_id=1, source_target_pairs={{0,4},{2,6},{4,8},{6,10},{8,12},{10,14},{12,16},{14,18},{16,20},{1... | collective-permute-start | bytes 1769480 | tf_op jit(solution)/shard_map/ppermute | solution.py:485
  10.0 1.9 %collective-permute-start.6 = (bf16[1024,2048]{1,0:T(8,128)(2,1)}, bf16[1024,2048]{1,0:T(8,128)(2,1)S(1)}, u32[]{:S(2)}, u32[]{:S(2)}) collective-permute-start(bf16[1024,2048]{1,0:T(8,128)(2,1)} %up_own_ref.1), channel_id=1, source_target_pairs={{0,1},{1,0},{2,3},{3,2},{4,5},{5,4},{6,7},{7,6},{8,9},{9,8},{10,11... | collective-permute-start | bytes 12582920 | tf_op jit(solution)/shard_map/ppermute | solution.py:482
  12.0 2.4 %collective-permute-start.7 = (bf16[2048,1024]{1,0:T(8,128)(2,1)}, bf16[2048,1024]{1,0:T(8,128)(2,1)S(1)}, u32[]{:S(2)}, u32[]{:S(2)}) collective-permute-start(bf16[2048,1024]{1,0:T(8,128)(2,1)} %down_own_ref.1), channel_id=1, source_target_pairs={{0,1},{1,0},{2,3},{3,2},{4,5},{5,4},{6,7},{7,6},{8,9},{9,8},{10,11... | collective-permute-start | bytes 12582920 | tf_op jit(solution)/shard_map/ppermute | solution.py:483
  14.4 3.4 %own_qkv.1 = (bf16[3,512,512]{2,1,0:T(8,128)(2,1)S(1)}, f32[2,8,128]{2,1,0:T(8,128)S(1)}) custom-call(bf16[512,1024]{1,0:T(8,128)(2,1)S(1)} %get-tuple-element.38.normed_ref, bf16[3,1024,512]{2,1,0:T(8,128)(2,1)} %bitcast.8, s32[1,128]{1,0:T(1,128)} %bitcast.18, s32[1,128]{1,0:T(1,128)} %bitcast.19), custom_call_target="tpu_custom_call" | custom-call | flops 1610612 | bytes 3145 | tf_op jit(solution)/shard_map/own_qkv/pallas_call | solution.py:486
  17.8 2.6 %own_attention.1 = (f32[512,512]{1,0:T(8,128)S(1)}, f32[512,512]{1,0:T(8,128)S(1)}, f32[512,512]{1,0:T(8,128)S(1)}) custom-call(bf16[3,512,512]{2,1,0:T(8,128)(2,1)S(1)} %get-tuple-element.39.qkv_ref, f32[2,8,128]{2,1,0:T(8,128)S(1)} %get-tuple-element.43.flags_ref), custom_call_target="tpu_custom_call" | custom-call | flops 1342177 | bytes 4194 | tf_op jit(solution)/shard_map/own_attention/pallas_call | solution.py:502
  20.4 10.3 %collective-permute-done.1.rows_ref = bf16[256,1024]{1,0:T(8,128)(2,1)S(1)} collective-permute-done((bf16[256,1024]{1,0:T(8,128)(2,1)S(1)}, bf16[256,1024]{1,0:T(8,128)(2,1)S(1)}, u32[]{:S(2)}, u32[]{:S(2)}) %collective-permute-start.1) | collective-permute-done | bytes 524320 | tf_op jit(solution)/shard_map/ppermute | solution.py:484
  30.8 1.9 %collective-permute-start.2 = (bf16[256,1024]{1,0:T(8,128)(2,1)S(1)}, bf16[256,1024]{1,0:T(8,128)(2,1)S(1)}, u32[]{:S(2)}, u32[]{:S(2)}) collective-permute-start(bf16[256,1024]{1,0:T(8,128)(2,1)S(1)} %collective-permute-done.1.rows_ref), channel_id=1, source_target_pairs={{0,1},{1,0},{2,3},{3,2},{4,5},{5,4},{6,7},{7,6},{8,9},{9,8},{10,11... | collective-permute-start | bytes 1572872 | tf_op jit(solution)/shard_map/ppermute | solution.py:512
  32.7 2.3 %near_mine.1 = (f32[512,512]{1,0:T(8,128)S(1)}, f32[512,512]{1,0:T(8,128)S(1)}, f32[512,512]{1,0:T(8,128)S(1)}) custom-call(bf16[3,512,512]{2,1,0:T(8,128)(2,1)S(1)} %get-tuple-element.39.qkv_ref, bf16[256,1024]{1,0:T(8,128)(2,1)S(1)} %collective-permute-done.1.rows_ref, bf16[3,1024,512]{2,1,0:T(8,128)(2,1)S(1)} %bitcast.9, ...), custom_call_target="tpu_custom_call" | custom-call | flops 1610612 | bytes 8388 | tf_op jit(solution)/shard_map/near_mine/pallas_call | solution.py:515
  35.1 2.4 %near_theirs.1 = (f32[512,512]{1,0:T(8,128)S(1)}, f32[512,512]{1,0:T(8,128)S(1)}, f32[512,512]{1,0:T(8,128)S(1)}) custom-call(bf16[3,512,512]{2,1,0:T(8,128)(2,1)S(1)} %get-tuple-element.39.qkv_ref, bf16[256,1024]{1,0:T(8,128)(2,1)S(1)} %collective-permute-done.2.rows_ref, bf16[3,1024,512]{2,1,0:T(8,128)(2,1)S(1)} %bitcast.10, ...), custom_call_target="tpu_custom_call" | custom-call | flops 1610612 | bytes 8388 | tf_op jit(solution)/shard_map/near_theirs/pallas_call | solution.py:515
  37.4 2.5 %collective-permute-start.3 = (bf16[288,1024]{1,0:T(8,128)(2,1)S(1)}, bf16[288,1024]{1,0:T(8,128)(2,1)S(1)}, u32[]{:S(2)}, u32[]{:S(2)}) collective-permute-start(bf16[288,1024]{1,0:T(8,128)(2,1)S(1)} %collective-permute-done.rows_ref), channel_id=1, source_target_pairs={{0,1},{1,0},{2,3},{3,2},{4,5},{5,4},{6,7},{7,6},{8,9},{9,8},{10,11... | collective-permute-start | bytes 1769480 | tf_op jit(solution)/shard_map/ppermute | solution.py:531
  40.0 2.1 %far_mine.1 = (f32[512,512]{1,0:T(8,128)S(1)}, f32[512,512]{1,0:T(8,128)S(1)}, f32[512,512]{1,0:T(8,128)S(1)}) custom-call(bf16[3,512,512]{2,1,0:T(8,128)(2,1)S(1)} %get-tuple-element.39.qkv_ref, bf16[288,1024]{1,0:T(8,128)(2,1)S(1)} %collective-permute-done.rows_ref, bf16[3,1024,512]{2,1,0:T(8,128)(2,1)S(1)} %bitcast.11, ...), custom_call_target="tpu_custom_call" | custom-call | flops 1073741 | bytes 8388 | tf_op jit(solution)/shard_map/far_mine/pallas_call | solution.py:533
  42.1 0.0 copy-start.3
  42.1 0.0 copy-start.4
  42.1 3.2 %far_theirs.1 = (bf16[512,512]{1,0:T(8,128)(2,1)S(1)}, bf16[272,1024]{1,0:T(8,128)(2,1)S(1)}) custom-call(bf16[3,512,512]{2,1,0:T(8,128)(2,1)S(1)} %get-tuple-element.39.qkv_ref, bf16[288,1024]{1,0:T(8,128)(2,1)S(1)} %collective-permute-done.3.rows_ref, bf16[3,1024,512]{2,1,0:T(8,128)(2,1)S(1)} %bitcast.12, f32[2,8,128]{2,1,0:T(8,128)S(1)} %get-tuple-element.43.flags_ref, ...), custom_call_target="tpu_custom_call" | custom-call | flops 25179246592 | bytes 140509184 | tf_op jit(solution)/shard_map/far_theirs/pallas_call | solution.py:543
  45.3 1.9 %collective-permute-start.4 = (bf16[272,1024]{1,0:T(8,128)(2,1)S(1)}, bf16[272,1024]{1,0:T(8,128)(2,1)S(1)}, u32[]{:S(2)}, u32[]{:S(2)}) collective-permute-start(bf16[272,1024]{1,0:T(8,128)(2,1)S(1)} %get-tuple-element.65), channel_id=1, source_target_pairs={{0,1},{1,0},{2,3},{3,2},{4,5},{5,4},{6,7},{7,6},{8,9},{9,8},{10,11... | collective-permute-start | bytes 1671176 | tf_op jit(solution)/shard_map/ppermute | solution.py:553
  47.3 0.5 out_projection.1.base_ref
  47.8 1.4 %collective-permute-done.4.got_ref = bf16[272,1024]{1,0:T(8,128)(2,1)S(1)} collective-permute-done((bf16[272,1024]{1,0:T(8,128)(2,1)S(1)}, bf16[272,1024]{1,0:T(8,128)(2,1)S(1)}, u32[]{:S(2)}, u32[]{:S(2)}) %collective-permute-start.4) | collective-permute-done | bytes 557088 | tf_op jit(solution)/shard_map/ppermute | solution.py:553
  49.1 1.9 %gated_units.1 = (bf16[272,1024]{1,0:T(8,128)(2,1)S(1)}, bf16[16,1024]{1,0:T(8,128)(2,1)S(1)}, f32[256,1024]{1,0:T(8,128)S(1)}) custom-call(f32[272,1024]{1,0:T(8,128)S(1)} %out_projection.1.base_ref, bf16[272,1024]{1,0:T(8,128)(2,1)S(1)} %collective-permute-done.4.got_ref, f32[1,1024]{1,0:T(1,128)S(1)} %bitcast.13, bf16[1024,2048]{1,0:T(8,128)(2,1)S(1)} %copy-done.4), custom_call_target="tpu_custom_call" | custom-call | flops 1140850688 | bytes 5242880 | tf_op jit(solution)/shard_map/gated_units/pallas_call | solution.py:563
  51.0 6.0 %collective-permute-start.5 = (bf16[16,1024]{1,0:T(8,128)(2,1)S(1)}, bf16[16,1024]{1,0:T(8,128)(2,1)S(1)}, u32[]{:S(2)}, u32[]{:S(2)}) collective-permute-start(bf16[16,1024]{1,0:T(8,128)(2,1)S(1)} %get-tuple-element.67), channel_id=1, source_target_pairs={{1,2},{3,4},{5,6},{7,8},{9,10},{11,12},{13,14},{15,16},{17,18},{19... | collective-permute-start | bytes 98312 | tf_op jit(solution)/shard_map/ppermute | solution.py:578
  57.1 2.3 %depthwise.1.sum_ref = f32[256,1024]{1,0:T(8,128)S(1)} custom-call(bf16[272,1024]{1,0:T(8,128)(2,1)S(1)} %get-tuple-element.66.gated_ref, bf16[31,1024]{1,0:T(8,128)(2,1)S(1)} %copy-done.7, f32[2,8,128]{2,1,0:T(8,128)S(1)} %get-tuple-element.43.flags_ref), custom_call_target="tpu_custom_call" | custom-call | flops 268435456 | bytes 1048576 | tf_op jit(solution)/shard_map/depthwise/pallas_call | solution.py:579
  59.4 2.3 %collective-permute-done.5.halo_ref = bf16[16,1024]{1,0:T(8,128)(2,1)S(1)} collective-permute-done((bf16[16,1024]{1,0:T(8,128)(2,1)S(1)}, bf16[16,1024]{1,0:T(8,128)(2,1)S(1)}, u32[]{:S(2)}, u32[]{:S(2)}) %collective-permute-start.5) | collective-permute-done | bytes 32800 | tf_op jit(solution)/shard_map/ppermute | solution.py:578
  61.7 7.2 %tail.1 = bf16[256,1024]{1,0:T(8,128)(2,1)} custom-call(f32[256,1024]{1,0:T(8,128)S(1)} %depthwise.1.sum_ref, bf16[16,1024]{1,0:T(8,128)(2,1)S(1)} %collective-permute-done.5.halo_ref, bf16[31,1024]{1,0:T(8,128)(2,1)S(1)} %copy-done.7, f32[2,8,128]{2,1,0:T(8,128)S(1)} %get-tuple-element.43.flags_ref, f32[256,1024]{1,0:T(8,128)S(1)} %get-tuple-element.68.first_ref, ...), custom_call_target="tpu_custom_call" | custom-call | flops 4831838208 | bytes 18874368 | tf_op jit(solution)/shard_map/tail/pallas_call | solution.py:592
  (27 shorter events, 0.1 us)
Async XLA Ops:
  0.0 32.7 %copy-start = (bf16[1024,3,512]{2,0,1:T(8,128)(2,1)S(1)}, bf16[1024,3,512]{2,0,1:T(8,128)(2,1)}, u32[]{:S(2)}) copy-start(bf16[1024,3,512]{2,0,1:T(8,128)(2,1)} %param.17) | copy-start | bytes 9437188
  2.0 28.8 %collective-permute-start.1 = (bf16[256,1024]{1,0:T(8,128)(2,1)S(1)}, bf16[256,1024]{1,0:T(8,128)(2,1)S(1)}, u32[]{:S(2)}, u32[]{:S(2)}) collective-permute-start(bf16[256,1024]{1,0:T(8,128)(2,1)S(1)} %get-tuple-element.42), channel_id=1, source_target_pairs={{0,2},{2,4},{4,6},{6,8},{8,10},{10,12},{12,14},{14,16},{16,18},{18... | collective-permute-start | bytes 1572872 | tf_op jit(solution)/shard_map/ppermute | solution.py:484
  5.4 32.0 %collective-permute-start = (bf16[288,1024]{1,0:T(8,128)(2,1)S(1)}, bf16[288,1024]{1,0:T(8,128)(2,1)S(1)}, u32[]{:S(2)}, u32[]{:S(2)}) collective-permute-start(bf16[288,1024]{1,0:T(8,128)(2,1)S(1)} %get-tuple-element.40), channel_id=1, source_target_pairs={{0,4},{2,6},{4,8},{6,10},{8,12},{10,14},{12,16},{14,18},{16,20},{1... | collective-permute-start | bytes 1769480 | tf_op jit(solution)/shard_map/ppermute | solution.py:485
  10.0 51.6 %collective-permute-start.6 = (bf16[1024,2048]{1,0:T(8,128)(2,1)}, bf16[1024,2048]{1,0:T(8,128)(2,1)S(1)}, u32[]{:S(2)}, u32[]{:S(2)}) collective-permute-start(bf16[1024,2048]{1,0:T(8,128)(2,1)} %up_own_ref.1), channel_id=1, source_target_pairs={{0,1},{1,0},{2,3},{3,2},{4,5},{5,4},{6,7},{7,6},{8,9},{9,8},{10,11... | collective-permute-start | bytes 12582920 | tf_op jit(solution)/shard_map/ppermute | solution.py:482
  12.0 49.7 %collective-permute-start.7 = (bf16[2048,1024]{1,0:T(8,128)(2,1)}, bf16[2048,1024]{1,0:T(8,128)(2,1)S(1)}, u32[]{:S(2)}, u32[]{:S(2)}) collective-permute-start(bf16[2048,1024]{1,0:T(8,128)(2,1)} %down_own_ref.1), channel_id=1, source_target_pairs={{0,1},{1,0},{2,3},{3,2},{4,5},{5,4},{6,7},{7,6},{8,9},{9,8},{10,11... | collective-permute-start | bytes 12582920 | tf_op jit(solution)/shard_map/ppermute | solution.py:483
  30.8 4.3 %collective-permute-start.2 = (bf16[256,1024]{1,0:T(8,128)(2,1)S(1)}, bf16[256,1024]{1,0:T(8,128)(2,1)S(1)}, u32[]{:S(2)}, u32[]{:S(2)}) collective-permute-start(bf16[256,1024]{1,0:T(8,128)(2,1)S(1)} %collective-permute-done.1.rows_ref), channel_id=1, source_target_pairs={{0,1},{1,0},{2,3},{3,2},{4,5},{5,4},{6,7},{7,6},{8,9},{9,8},{10,11... | collective-permute-start | bytes 1572872 | tf_op jit(solution)/shard_map/ppermute | solution.py:512
  37.4 4.7 %copy-start.6 = (bf16[512,1024]{1,0:T(8,128)(2,1)S(1)}, bf16[512,1024]{1,0:T(8,128)(2,1)}, u32[]{:S(2)}) copy-start(bf16[512,1024]{1,0:T(8,128)(2,1)} %w_out_ref.3) | copy-start | bytes 3145732
  37.4 4.6 %collective-permute-start.3 = (bf16[288,1024]{1,0:T(8,128)(2,1)S(1)}, bf16[288,1024]{1,0:T(8,128)(2,1)S(1)}, u32[]{:S(2)}, u32[]{:S(2)}) collective-permute-start(bf16[288,1024]{1,0:T(8,128)(2,1)S(1)} %collective-permute-done.rows_ref), channel_id=1, source_target_pairs={{0,1},{1,0},{2,3},{3,2},{4,5},{5,4},{6,7},{7,6},{8,9},{9,8},{10,11... | collective-permute-start | bytes 1769480 | tf_op jit(solution)/shard_map/ppermute | solution.py:531
  42.1 5.1 %copy-start.3 = (bf16[512,1024]{1,0:T(8,128)(2,1)S(1)}, bf16[512,1024]{1,0:T(8,128)(2,1)}, u32[]{:S(2)}) copy-start(bf16[512,1024]{1,0:T(8,128)(2,1)} %frames_ref.3) | copy-start | bytes 3145732
  42.1 7.0 %copy-start.4 = (bf16[1024,2048]{1,0:T(8,128)(2,1)S(1)}, bf16[1024,2048]{1,0:T(8,128)(2,1)}, u32[]{:S(2)}) copy-start(bf16[1024,2048]{1,0:T(8,128)(2,1)} %w_ref.1) | copy-start | bytes 12582916
  42.1 7.0 %copy-start.8 = (f32[1024]{0:T(1024)S(1)}, f32[1024]{0:T(1024)}, u32[]{:S(2)}) copy-start(f32[1024]{0:T(1024)} %param.19) | copy-start | bytes 12292
  45.3 3.9 %collective-permute-start.4 = (bf16[272,1024]{1,0:T(8,128)(2,1)S(1)}, bf16[272,1024]{1,0:T(8,128)(2,1)S(1)}, u32[]{:S(2)}, u32[]{:S(2)}) collective-permute-start(bf16[272,1024]{1,0:T(8,128)(2,1)S(1)} %get-tuple-element.65), channel_id=1, source_target_pairs={{0,1},{1,0},{2,3},{3,2},{4,5},{5,4},{6,7},{7,6},{8,9},{9,8},{10,11... | collective-permute-start | bytes 1671176 | tf_op jit(solution)/shard_map/ppermute | solution.py:553
  47.2 9.8 %copy-start.7 = (bf16[31,1024]{1,0:T(8,128)(2,1)S(1)}, bf16[31,1024]{1,0:T(8,128)(2,1)}, u32[]{:S(2)}) copy-start(bf16[31,1024]{1,0:T(8,128)(2,1)} %taps_ref.3) | copy-start | bytes 190468
  47.2 14.4 %copy-start.2 = (bf16[2048,1024]{1,0:T(8,128)(2,1)S(1)}, bf16[2048,1024]{1,0:T(8,128)(2,1)}, u32[]{:S(2)}) copy-start(bf16[2048,1024]{1,0:T(8,128)(2,1)} %down_own_ref.1) | copy-start | bytes 12582916
  47.7 14.0 %copy-start.1 = (bf16[1024,2048]{1,0:T(8,128)(2,1)S(1)}, bf16[1024,2048]{1,0:T(8,128)(2,1)}, u32[]{:S(2)}) copy-start(bf16[1024,2048]{1,0:T(8,128)(2,1)} %up_own_ref.1) | copy-start | bytes 12582916
  47.7 14.0 %copy-start.5 = (bf16[1024,1024]{1,0:T(8,128)(2,1)S(1)}, bf16[1024,1024]{1,0:T(8,128)(2,1)}, u32[]{:S(2)}) copy-start(bf16[1024,1024]{1,0:T(8,128)(2,1)} %w_point_ref.1) | copy-start | bytes 6291460
  47.7 14.0 %copy-start.9 = (f32[1024]{0:T(1024)S(1)}, f32[1024]{0:T(1024)}, u32[]{:S(2)}) copy-start(f32[1024]{0:T(1024)} %param.22) | copy-start | bytes 12292
  47.8 14.0 %copy-start.10 = (f32[1024]{0:T(1024)S(1)}, f32[1024]{0:T(1024)}, u32[]{:S(2)}) copy-start(f32[1024]{0:T(1024)} %param.24) | copy-start | bytes 12292
  47.8 14.0 %copy-start.11 = (f32[1024]{0:T(1024)S(1)}, f32[1024]{0:T(1024)}, u32[]{:S(2)}) copy-start(f32[1024]{0:T(1024)} %param.27) | copy-start | bytes 12292
  51.0 10.7 %collective-permute-start.5 = (bf16[16,1024]{1,0:T(8,128)(2,1)S(1)}, bf16[16,1024]{1,0:T(8,128)(2,1)S(1)}, u32[]{:S(2)}, u32[]{:S(2)}) collective-permute-start(bf16[16,1024]{1,0:T(8,128)(2,1)S(1)} %get-tuple-element.67), channel_id=1, source_target_pairs={{1,2},{3,4},{5,6},{7,8},{9,10},{11,12},{13,14},{15,16},{17,18},{19... | collective-permute-start | bytes 98312 | tf_op jit(solution)/shard_map/ppermute | solution.py:578
